TPU v7x, 512 devices: a whole 4x8x8 slice. The times are simulated.
512 devices in a mesh: seq: 16 (over y, core), leaf: 32 (over x, z).
Axes of the slice: x: 4, y: 8, z: 8, core: 2. Of those that a mesh axis runs over, the one named last changes fastest.
Arguments:
- queries: bfloat16 [256, 4, 4096], P('leaf'), may hold values from -32 to 32
- prompt_kv: bfloat16 [2, 20480, 512], P(None, 'seq'), may hold values from -8 to 8
- node_kv: bfloat16 [2, 512, 256, 512], P(None, 'leaf', 'seq'), may hold values from -8 to 8
- node_lengths: int32 [512], P('leaf'), may hold values from 128 to 256, as said below
- ancestors: int32 [256, 10], P('leaf'), may hold values from -1 to 511, as said below
Outputs:
- attended: bfloat16 [256, 4, 4096], P('leaf', None, 'seq')
Inputs may be any that keep to these rules, and one draw needn't show every extreme that they name: `ancestors`: each entry is -1 or a node id, owner * 16 + slot, whose owner is an index of leaf. The last entry of every row is the leaf's own node, owned by the index of leaf that holds the leaf. A node whose owner is not the index of leaf holding the leaf sits in slot 15 of its owner, and each owner holds one such node at most. `node_lengths`: multiples of 128.
All inputs are finite; a program needn't handle non-finite values.
Results may differ from a plain program's by a relative error of at most 0.0028.
Values may be sent and summed in bfloat16 or wider, within the bound.
No kernel may reach another device: no remote copies, remote signals or barrier semaphores. Data moves between devices by JAX's collectives and lax.ppermute only.
A program may use at most 64 MiB of HBM per device.

v0:
```python
import math

import jax
import jax.numpy as jnp
from jax import lax
from jax.sharding import PartitionSpec as P

HEADS = 16
KV_HEADS = 2
HEAD_DIM = 256


def joined(x, axis, combine):
    everything = jax.tree.map(lambda part: lax.all_gather(part, axis), x)
    initial = jax.tree.map(lambda part: part[0], everything)

    def hop(k, so_far):
        return combine(so_far, jax.tree.map(lambda part: part[k], everything))

    return lax.fori_loop(1, lax.axis_size(axis), hop, initial)


def combine_parts(first_part, second_part):
    first_max, first_total, first_sum = first_part
    second_max, second_total, second_sum = second_part
    top_max = jnp.maximum(first_max, second_max)
    first_weight = jnp.exp(first_max - top_max)
    second_weight = jnp.exp(second_max - top_max)
    return (
        top_max,
        first_total * first_weight + second_total * second_weight,
        first_sum * first_weight[..., None] + second_sum * second_weight[..., None],
    )


def shards(queries, prompt_kv, node_kv, node_lengths, ancestors):
    leaf_count, step_count, feat_width = queries.shape
    group_size = HEADS // KV_HEADS
    node_slots = node_kv.shape[1]
    token_count = node_kv.shape[2]
    level_count = ancestors.shape[1]
    score_scale = 1.0 / math.sqrt(HEAD_DIM)
    query_rows = queries.reshape(leaf_count, step_count, KV_HEADS, group_size, HEAD_DIM)
    prompt_keys = prompt_kv[0].reshape(-1, KV_HEADS, HEAD_DIM)
    prompt_values = prompt_kv[1].reshape(-1, KV_HEADS, HEAD_DIM)
    prompt_scores = (
        jnp.einsum("lskgd,pkd->lskgp", query_rows, prompt_keys, preferred_element_type=jnp.float32)
        * score_scale
    )
    shared_kv, shared_lengths = (
        lax.all_gather(node_kv[:, node_slots - 1 :], "leaf", axis=1, tiled=True),
        lax.all_gather(
            node_lengths[node_slots - 1 :].astype(jnp.bfloat16), "leaf", axis=0, tiled=True
        ),
    )
    kv_table = jnp.concatenate([node_kv, shared_kv], axis=1)
    length_table = jnp.concatenate([node_lengths, shared_lengths.astype(jnp.int32)])
    device_id = lax.axis_index("leaf")
    safe_ids = jnp.maximum(ancestors, 0)
    owner_dev = safe_ids // node_slots
    row_index = jnp.where(owner_dev == device_id, safe_ids % node_slots, node_slots + owner_dev)
    picked = kv_table[:, row_index]
    entries = jnp.arange(length_table.shape[0], dtype=jnp.int32)
    lengths = jnp.sum(jnp.where(row_index[..., None] == entries, length_table, 0), axis=-1)
    position = lax.axis_index("seq") * token_count + jnp.arange(token_count, dtype=jnp.int32)
    present = (ancestors >= 0)[:, :, None] & (position[None, None, :] < lengths[:, :, None])
    step_ids = jnp.arange(step_count, dtype=jnp.int32)
    own_limit = lengths[:, -1][:, None] - step_count + step_ids[None, :]
    last_level = jnp.arange(level_count, dtype=jnp.int32) == level_count - 1
    causal = jnp.logical_not(last_level)[None, None, :, None] | (
        position[None, None, None, :] <= own_limit[:, :, None, None]
    )
    allowed = present[:, None] & causal
    node_keys = picked[0].reshape(leaf_count, level_count, token_count, KV_HEADS, HEAD_DIM)
    node_values = picked[1].reshape(leaf_count, level_count, token_count, KV_HEADS, HEAD_DIM)
    node_scores = (
        jnp.einsum("lskgd,ljtkd->lskgjt", query_rows, node_keys, preferred_element_type=jnp.float32)
        * score_scale
    )
    node_scores = jnp.where(allowed[:, :, None, None], node_scores, -jnp.inf)
    block_max = jnp.maximum(jnp.max(prompt_scores, axis=-1), jnp.max(node_scores, axis=(-2, -1)))
    prompt_weights = jnp.exp(prompt_scores - block_max[..., None])
    node_weights = jnp.exp(node_scores - block_max[..., None, None])
    block_total = jnp.sum(prompt_weights, axis=-1) + jnp.sum(node_weights, axis=(-2, -1))
    block_sum = jnp.einsum(
        "lskgp,pkd->lskgd",
        prompt_weights.astype(jnp.bfloat16),
        prompt_values,
        preferred_element_type=jnp.float32,
    )
    block_sum = block_sum + jnp.einsum(
        "lskgjt,ljtkd->lskgd",
        node_weights.astype(jnp.bfloat16),
        node_values,
        preferred_element_type=jnp.float32,
    )
    columns = feat_width // lax.axis_size("seq")
    col_start = lax.axis_index("seq") * columns
    merged = joined((block_max, block_total, block_sum), "seq", combine_parts)
    denominator = merged[1]
    numerator = merged[2].reshape(leaf_count, step_count, feat_width)
    numerator = lax.dynamic_slice_in_dim(numerator, col_start, columns, 2)
    spread = jnp.broadcast_to(denominator[..., None], denominator.shape + (HEAD_DIM,)).reshape(
        leaf_count, step_count, feat_width
    )
    spread = lax.dynamic_slice_in_dim(spread, col_start, columns, 2)
    return (numerator / spread).astype(jnp.bfloat16)


def solution(mesh):
    placed = (
        P("leaf", None, None),
        P(None, "seq", None),
        P(None, "leaf", "seq", None),
        P("leaf"),
        P("leaf", None),
    )
    return jax.shard_map(
        shards, mesh=mesh, in_specs=placed, out_specs=P("leaf", None, "seq"), check_vma=False
    )
```

profile of v0, /device:TPU:1, one launch (start us, length us, event | category | flops | bytes accessed | tf_op | source)
XLA Modules:
  0.0 209.7 jit_solution(9420879240600532048)
XLA Ops:
  6.5 1.4 slice.34
  8.0 0.7 convert.3
  8.7 0.6 slice.32
  9.2 1.3 dynamic-slice
  10.5 1.4 dynamic-update-slice
  11.9 67.9 %all-reduce = bf16[32]{0:T(256)(128)(2,1)S(1)} all-reduce(bf16[32]{0:T(256)(128)(2,1)S(1)} %dynamic-update-slice), channel_id=1, replica_groups=mesh['seq'=16,'leaf'=32] {'leaf'}, use_global_device_ids=true, to_apply=%add | all-reduce | flops 32 | bytes 128
  79.9 0.7 pad_add_fusion
  80.6 0.7 compare_select_fusion
  81.5 1.9 fusion.38
  83.4 0.3 select_reduce_fusion
  84.0 1.5 copy.122
  85.5 0.6 copy.121
  86.5 2.0 fusion.40
  88.5 5.6 %all-gather.6.cloned.1.call-done = bf16[2,32,16,512]{3,2,1,0:T(8,128)(2,1)} async-done(((bf16[2,1,16,512]{3,2,1,0:T(8,128)(2,1)}), bf16[2,32,16,512]{3,2,1,0:T(8,128)(2,1)}) %all-gather.6.cloned.1.call-update) | async-done | bytes 1048592 | tf_op jit(solution)/shard_map/all_gather | solution.py:51
  94.1 1.4 pad_maximum_fusion
  95.5 2.4 %gather_fusion = bf16[80,2,16,512]{3,2,1,0:T(8,128)(2,1)} fusion(bf16[2,48,16,512]{3,2,1,0:T(8,128)(2,1)S(1)} %pad_maximum_fusion, s32[1024]{0:T(1024)S(1)} %pad_clamp_fusion), kind=kCustom, calls=%fused_computation | custom fusion | bytes 5243200 | tf_op jit(solution)/shard_map/gather | solution.py:62
  97.9 2.0 copy.165
  99.9 0.3 fusion.39
  100.1 1.2 reshape_squeeze.13
  101.4 4.7 %fusion.10 = (f32[8,4,2,8]{3,1,2,0:T(4,128)S(1)}, f32[8,2,10,16,4,8]{3,5,4,2,1,0:T(8,128)}) fusion(pred[8,4,10,16]{3,1,2,0:T(4,128)(4,1)S(1)} %or_and_fusion, bf16[8,10,16,2,256,1]{4,3,2,1,0,5:T(2,128)(2,1)} %bitcast.84, bf16[8,4,2,8,256]{4,3,2,1,0:T(8,128)(2,1)S(1)} %reshape.94), kind=kOutput, calls=%fused_computation.24 | convolution fusion | flops 42188288 | bytes 1907712 | tf_op jit(solution)/shard_map/lskgd,ljtkd->lskgjt/dot_general | solution.py:77
  106.2 1.2 reshape_squeeze.15
  107.4 2.8 %fusion.8 = (bf16[8,4,2,8,10,16]{5,3,1,4,2,0:T(8,128)(2,1)S(1)}, f32[8,4,2,8]{3,1,2,0:T(4,128)S(1)}) fusion(f32[8,2,10,16,4,8]{3,5,4,2,1,0:T(8,128)} %get-tuple-element.248, f32[8,4,2,8]{3,1,2,0:T(4,128)S(1)} %copy.86, pred[8,4,10,16]{3,1,2,0:T(4,128)(4,1)S(1)} %or_and_fusion), kind=kLoop, calls=%fused_computation.22 | loop fusion | flops 409088 | bytes 500736 | tf_op jit(solution)/shard_map/convert_element_type | solution.py:93
  110.2 0.6 fusion.25
  110.8 1.1 copy-done
  111.9 0.4 copy-done.1
  112.3 1.4 fusion.22
  113.7 0.5 fusion.7
  114.3 29.6 %all-gather.1 = f32[128,4,2,8]{3,1,2,0:T(4,128)S(1)} all-gather(f32[8,4,2,8]{3,1,2,0:T(4,128)S(1)} %copy.91), channel_id=3, replica_groups=mesh['seq'=16,'leaf'=32] {'seq'}, dimensions={0}, use_global_device_ids=true | all-gather | bytes 34816 | tf_op jit(solution)/shard_map/all_gather | solution.py:14
  143.9 19.9 %all-gather = f32[128,4,2,8]{3,1,2,0:T(4,128)S(1)} all-gather(f32[8,4,2,8]{3,1,2,0:T(4,128)S(1)} %copy.86), channel_id=2, replica_groups=mesh['seq'=16,'leaf'=32] {'seq'}, dimensions={0}, use_global_device_ids=true | all-gather | bytes 34816 | tf_op jit(solution)/shard_map/all_gather | solution.py:14
  163.8 15.2 %all-gather.8.cloned.1.call-done = f32[128,4,2,8,256]{4,3,1,0,2:T(8,128)} async-done(((f32[8,4,2,8,256]{4,3,1,0,2:T(8,128)}), f32[128,4,2,8,256]{4,3,1,0,2:T(8,128)}) %all-gather.8.cloned.1.call-update) | async-done | bytes 8388624 | tf_op jit(solution)/shard_map/all_gather | solution.py:14
  179.1 1.1 slice.51
  180.2 21.3 %while.19 = (s32[]{:T(128)}, f32[8,4,2,8]{3,2,1,0:T(2,128)S(1)}, f32[8,4,2,8]{3,2,1,0:T(2,128)S(1)}, f32[8,4,2,8,256]{4,3,2,1,0:T(8,128)S(1)}, f32[16,8,4,2,8]{4...) while((s32[]{:T(128)}, f32[8,4,2,8]{3,2,1,0:T(2,128)S(1)}, ...), condition=%wide.region_6.7_spmd, body=%wide.region_5.6_spmd.sunk | while | flops 396293 | bytes 1601679 | solution.py:20
  180.4 1.3 fusion.47
  181.8 1.3 fusion.47
  183.2 1.3 fusion.47
  184.6 1.3 fusion.47
  186.0 1.3 fusion.47
  187.5 1.3 fusion.47
  188.9 1.3 fusion.47
  190.3 1.3 fusion.47
  191.7 1.3 fusion.47
  193.2 1.3 fusion.47
  194.6 1.3 fusion.47
  196.0 1.3 fusion.47
  197.4 1.3 fusion.47
  198.8 1.3 fusion.47
  200.3 1.3 fusion.47
  202.2 0.6 fusion.32
  (72 shorter events, 3.2 us)
Async XLA Ops:
  6.5 87.6 %all-gather.6.cloned.1.call-start = ((), (), s32[]{:S(2)}) async-start(), calls=%async_computation | async-start | bytes 1081344 | tf_op jit(solution)/shard_map/all_gather | solution.py:51
  7.9 171.2 %all-gather.8.cloned.1.call-start = ((), (), s32[]{:S(2)}) async-start(), calls=%async_computation.1 | async-start | bytes 8912896 | tf_op jit(solution)/shard_map/all_gather | solution.py:14
  81.5 2.4 %copy-start.4 = (bf16[8,4,4096]{2,1,0:T(4,128)(2,1)S(1)}, bf16[8,4,4096]{2,1,0:T(4,128)(2,1)}, u32[]{:S(2)}) copy-start(bf16[8,4,4096]{2,1,0:T(4,128)(2,1)} %param.7) | copy-start | bytes 786436
  85.5 0.7 copy-start.5
  86.5 7.6 %copy-start.3 = (bf16[2,16,16,512]{3,2,1,0:T(8,128)(2,1)S(1)}, bf16[2,16,16,512]{3,2,1,0:T(8,128)(2,1)}, u32[]{:S(2)}) copy-start(bf16[2,16,16,512]{3,2,1,0:T(8,128)(2,1)} %param.9) | copy-start | bytes 1572868
  107.4 2.8 %copy-start.2 = (bf16[8,10,16,2,256]{4,3,2,1,0:T(2,128)(2,1)S(1)}, bf16[8,10,16,2,256]{4,3,2,1,0:T(2,128)(2,1)}, u32[]{:S(2)}) copy-start(bf16[8,10,16,2,256]{4,3,2,1,0:T(2,128)(2,1)} %reshape_squeeze.15) | copy-start | bytes 3932164
  110.2 1.7 copy-start
  110.2 2.1 copy-start.1
Sparse Core Ops, SparseCore 0:
  10.5 83.5 all-gather.5
  113.9 65.1 all-gather.7
where the time goes:
time: 211 us; the launch traced here: 210 us
  blocking collectives  117 us (55%)
  other arithmetic  28.8 us (14%)
  waiting for transfers between devices  20.8 us (10%)
  local copies, waits for them, and re-layouts  19.7 us (9%)
  between operations  13.6 us (6%)
  matrix products  8.81 us (4%)
    unnamed x1, blocking collectives  67.9 us
    all_gather x2, blocking collectives, joined(): everything = jax.tree.map(lambda part: lax.all_gather(part, axis), x)  49.5 us
    add x15, other arithmetic, combine_parts(): first_sum * first_weight[..., None] + second_sum * second_weight[..., None]  19.3 us
    all_gather x1, waiting for transfers between devices, joined(): everything = jax.tree.map(lambda part: lax.all_gather(part, axis), x)  15.2 us
    unnamed x17, local copies, waits for them, and re-layouts  6.24 us
    all_gather x1, waiting for transfers between devices, shards(): lax.all_gather(node_kv[:, node_slots - 1:], 'leaf', axis=1, tiled=True)  5.58 us
    dot_general x1, matrix products, shards(): jnp.einsum('lskgd,ljtkd->lskgjt', query_rows, node_keys, preferred_elemen...  4.74 us
    gather x2, local copies, waits for them, and re-layouts, shards(): picked = kv_table[:, row_index]  4.39 us
  transfers between devices with their start and end apart: 2, of which 2 were waited for; matrix products, arithmetic and copies ran while one was open for 6% of the time, Pallas kernels for 0%

commit v1 on v0

v1 whole, which is shorter than its diff:
```python
import functools

import jax
import jax.numpy as jnp
from jax import lax
from jax.experimental import pallas as pl
from jax.experimental.pallas import tpu as pltpu
from jax.sharding import PartitionSpec as P

HEADS = 16
KV_HEADS = 2
HEAD_DIM = 256
GROUP = HEADS // KV_HEADS
CHUNK = 256
LANES = 128
INVALID_KEY = 256.0


def fold(x, combine):
    parts = [x[:, i : i + LANES] for i in range(0, x.shape[1], LANES)]
    return functools.reduce(combine, parts)


def node_counts(anc, ids, levels):
    counts = jnp.zeros((anc.shape[0], ids.shape[1]), jnp.float32)
    for level in levels:
        counts = counts + jnp.where(anc[:, level : level + 1] == ids, 1.0, 0.0)
    return counts


def tall(mask, reps):
    return jnp.concatenate([mask] * reps, axis=0)


def attend_kernel(
    steps, place_ref, lengths_ref, anc_ref, q_ref, prompt_ref, node_ref, shared_ref, out_ref, s_ref
):
    leaf_count, level_count = anc_ref.shape
    node_slots = lengths_ref.shape[0]
    owners = shared_ref.shape[0]
    node_cols = node_ref.shape[1]
    tokens = node_cols // node_slots
    prompt_cols = prompt_ref.shape[1]
    shared_cols = owners * tokens
    rows = steps * leaf_count
    first_pos = place_ref[0] * tokens
    device = place_ref[1]
    anc = anc_ref[...]

    lane = lax.broadcasted_iota(jnp.int32, (1, node_cols), 1)
    slot = lane // tokens
    position = first_pos + lane % tokens
    length = jnp.zeros((1, node_cols), jnp.int32)
    for n in range(node_slots):
        length = jnp.where(slot == n, lengths_ref[n], length)
    ids = device * node_slots + slot
    upper = node_counts(anc, ids, range(level_count - 1))
    own = node_counts(anc, ids, [level_count - 1])
    local_mult = []
    for step in range(steps):
        causal = jnp.where(position <= length - steps + step, 1.0, 0.0)
        local_mult.append(jnp.where(position < length, upper + own * causal, 0.0))
    local_mult = jnp.concatenate(local_mult, axis=0)

    lane = lax.broadcasted_iota(jnp.int32, (1, shared_cols), 1)
    owner = lane // tokens
    shared_count = node_counts(anc, owner * node_slots + node_slots - 1, range(level_count - 1))
    shared_count = jnp.where(owner == device, 0.0, shared_count)

    for k in range(KV_HEADS):
        cols = slice(k * HEAD_DIM, (k + 1) * HEAD_DIM)
        query = jnp.concatenate(
            [q_ref[:, (k * GROUP + h) * HEAD_DIM : (k * GROUP + h + 1) * HEAD_DIM] for h in range(GROUP)], axis=0
        )
        query = query * jnp.bfloat16(1.0 / 16.0)

        def scores(keys):
            return lax.dot_general(query, keys, (((1,), (1,)), ((), ())), preferred_element_type=jnp.float32)

        top = None
        for start in range(0, prompt_cols, CHUNK):
            s = scores(prompt_ref[0, start : start + CHUNK, cols])
            s_ref[:, start : start + CHUNK] = s
            part = fold(s, jnp.maximum)
            top = part if top is None else jnp.maximum(top, part)
        s = scores(node_ref[0, :, cols])
        s = jnp.where(tall(local_mult, GROUP) > 0.0, s, -jnp.inf)
        s_ref[:, prompt_cols : prompt_cols + node_cols] = s
        top = jnp.maximum(top, fold(s, jnp.maximum))
        shared_keys = shared_ref[:, 0:tokens, cols].reshape(shared_cols, HEAD_DIM)
        flags = lax.dot_general(
            jnp.where(lax.broadcasted_iota(jnp.int32, (8, HEAD_DIM), 1) == 0, 1.0, 0.0).astype(jnp.bfloat16),
            shared_keys,
            (((1,), (1,)), ((), ())),
            preferred_element_type=jnp.float32,
        )
        shared_mult = jnp.where(flags[0:1] < INVALID_KEY / 2, shared_count, 0.0)
        shared_mult = tall(shared_mult, steps)
        s = scores(shared_keys)
        s = jnp.where(tall(shared_mult, GROUP) > 0.0, s, -jnp.inf)
        s_ref[:, prompt_cols + node_cols : prompt_cols + node_cols + shared_cols] = s
        top = jnp.maximum(top, fold(s, jnp.maximum))
        block_max = jnp.max(top, axis=1, keepdims=True)

        total = jnp.zeros((GROUP * rows, LANES), jnp.float32)
        acc = jnp.zeros((GROUP * rows, HEAD_DIM), jnp.float32)
        for start in range(0, prompt_cols, CHUNK):
            w = jnp.exp(s_ref[:, start : start + CHUNK] - block_max)
            total = total + fold(w, jnp.add)
            acc = acc + jnp.dot(
                w.astype(jnp.bfloat16), prompt_ref[1, start : start + CHUNK, cols], preferred_element_type=jnp.float32
            )
        w = jnp.exp(s_ref[:, prompt_cols : prompt_cols + node_cols] - block_max) * tall(local_mult, GROUP)
        total = total + fold(w, jnp.add)
        acc = acc + jnp.dot(w.astype(jnp.bfloat16), node_ref[1, :, cols], preferred_element_type=jnp.float32)
        w = jnp.exp(
            s_ref[:, prompt_cols + node_cols : prompt_cols + node_cols + shared_cols] - block_max
        ) * tall(shared_mult, GROUP)
        total = total + fold(w, jnp.add)
        shared_values = shared_ref[:, tokens : 2 * tokens, cols].reshape(shared_cols, HEAD_DIM)
        acc = acc + jnp.dot(w.astype(jnp.bfloat16), shared_values, preferred_element_type=jnp.float32)
        total = jnp.sum(total, axis=1, keepdims=True)

        half = rows // 2
        lane = lax.broadcasted_iota(jnp.int32, (GROUP * rows, LANES), 1)
        stats = jnp.where(lane == 0, block_max, jnp.where(lane == 1, total, 0.0))
        for h in range(GROUP):
            for part in range(2):
                first = h * rows + part * half
                out_ref[k * GROUP + h, :, part * HEAD_DIM : (part + 1) * HEAD_DIM] = acc[first : first + half]
            low, high = stats[h * rows : h * rows + half], stats[h * rows + half : (h + 1) * rows]
            out_ref[k * GROUP + h, :, 2 * HEAD_DIM :] = jnp.where(
                lane[:half] < LANES // 2, low, pltpu.roll(high, LANES // 2, 1)
            )


def merge_kernel(parts_ref, out_ref):
    blocks, half, _ = parts_ref.shape
    leaf_count, steps, _ = out_ref.shape
    for part in range(2):
        first = part * LANES // 2
        stats = [parts_ref[b, :, 2 * HEAD_DIM :] for b in range(blocks)]
        tops = [st[:, first : first + 1] for st in stats]
        row_max = functools.reduce(jnp.maximum, tops)
        denominator = jnp.zeros((half, 1), jnp.float32)
        numerator = jnp.zeros((half, HEAD_DIM), jnp.float32)
        for b in range(blocks):
            scale = jnp.exp(tops[b] - row_max)
            denominator = denominator + scale * stats[b][:, first + 1 : first + 2]
            numerator = numerator + scale * parts_ref[b, :, part * HEAD_DIM : (part + 1) * HEAD_DIM]
        merged = (numerator / denominator).astype(jnp.bfloat16)
        for i in range(half // leaf_count):
            out_ref[:, part * half // leaf_count + i, :] = merged[i * leaf_count : (i + 1) * leaf_count]


def shards(queries, prompt_kv, node_kv, node_lengths, ancestors):
    leaf_count, steps, feat_width = queries.shape
    node_slots, tokens = node_kv.shape[1:3]
    width = KV_HEADS * HEAD_DIM
    rows = steps * leaf_count
    blocks = lax.axis_size("seq")
    owners = lax.axis_size("leaf")
    place = jnp.stack([lax.axis_index("seq"), lax.axis_index("leaf")]).astype(jnp.int32)

    present = lax.axis_index("seq") * tokens < node_lengths[node_slots - 1]
    last = node_kv[:, node_slots - 1]
    last = jnp.stack([jnp.where(present, last[0], jnp.bfloat16(INVALID_KEY)), last[1]])
    last = jnp.broadcast_to(last.reshape(1, 2 * tokens, width), (owners, 2 * tokens, width))
    shared = lax.all_to_all(last, "leaf", 0, 0, tiled=True)

    query_rows = queries.transpose(1, 0, 2).reshape(rows, feat_width)
    cols = prompt_kv.shape[1] + node_slots * tokens + owners * tokens
    vmem = pl.BlockSpec(memory_space=pltpu.VMEM)
    smem = pl.BlockSpec(memory_space=pltpu.SMEM)
    parts = pl.pallas_call(
        functools.partial(attend_kernel, steps),
        out_shape=jax.ShapeDtypeStruct((HEADS, rows // 2, 2 * HEAD_DIM + LANES), jnp.float32),
        in_specs=[smem, smem, vmem, vmem, vmem, vmem, vmem],
        out_specs=vmem,
        scratch_shapes=[pltpu.VMEM((GROUP * rows, cols), jnp.float32)],
        compiler_params=pltpu.CompilerParams(vmem_limit_bytes=32 * 1024 * 1024),
    )(
        place,
        node_lengths,
        ancestors,
        query_rows,
        prompt_kv,
        node_kv.reshape(2, node_slots * tokens, width),
        shared,
    )
    parts = lax.all_to_all(parts, "seq", 0, 0, tiled=True)
    return pl.pallas_call(
        merge_kernel,
        out_shape=jax.ShapeDtypeStruct((leaf_count, steps, HEAD_DIM), jnp.bfloat16),
        in_specs=[vmem],
        out_specs=vmem,
        compiler_params=pltpu.CompilerParams(vmem_limit_bytes=32 * 1024 * 1024),
    )(parts)


def solution(mesh):
    placed = (
        P("leaf", None, None),
        P(None, "seq", None),
        P(None, "leaf", "seq", None),
        P("leaf"),
        P("leaf", None),
    )
    return jax.shard_map(
        shards, mesh=mesh, in_specs=placed, out_specs=P("leaf", None, "seq"), check_vma=False
    )
```

time: 211 us -> 80.3 us (0.38)
  blocking collectives: 117 us -> 32.1 us
  other arithmetic: 28.8 us -> 0.83 us
  local copies, waits for them, and re-layouts: 19.7 us -> 4.3 us
  starting transfers between devices: 0.04 us -> 13.7 us
  between operations: 13.6 us -> 0.71 us
  matrix products: 8.81 us -> 0 us
  Pallas kernels: 0 us -> 3.89 us
  waiting for transfers between devices: 20.8 us -> 24.4 us
    unnamed x1 -> x0, blocking collectives: 67.9 us -> none
    all_gather x2 -> x0, blocking collectives: 49.5 us -> none  [joined(): everything = jax.tree.map(lambda part: lax.all_gather(part, axis), x)]
    all_to_all x0 -> x1, blocking collectives: none -> 32.1 us  [shards(): parts = lax.all_to_all(parts, 'seq', 0, 0, tiled=True)]
    all_to_all x0 -> x1, waiting for transfers between devices: none -> 24.4 us  [shards(): shared = lax.all_to_all(last, 'leaf', 0, 0, tiled=True)]
    all_gather x2 -> x0, waiting for transfers between devices: 20.8 us -> none  [the longest x1 15.2 us: joined(): everything = jax.tree.map(lambda part: lax.all_gather(part, axis), x)]
    add x33 -> x0, other arithmetic: 20.7 us -> none  [the longest x15 19.3 us: combine_parts(): first_sum * first_weight[..., None] + second_sum * second_weight[..., None]]
    all_to_all x0 -> x1, starting transfers between devices: none -> 13.7 us  [shards(): shared = lax.all_to_all(last, 'leaf', 0, 0, tiled=True)]
    dot_general x4 -> x0, matrix products: 8.81 us -> none  [the longest x1 4.74 us: shards(): jnp.einsum('lskgd,ljtkd->lskgjt', query_rows, node_keys, preferred_elemen...]
  transfers between devices with their start and end apart: 2 -> 1, of which waited for: 2 -> 1; matrix products, arithmetic and copies ran while one was open for 6% -> 0% of each run, Pallas kernels for 0% -> 0%
where the time goes in v1:
time: 80.3 us; the launch traced here: 79.9 us
  blocking collectives  32.1 us (40%)
  waiting for transfers between devices  24.4 us (30%)
  starting transfers between devices  13.7 us (17%)
  local copies, waits for them, and re-layouts  4.3 us (5%)
  Pallas kernels  3.89 us (5%)
  other arithmetic  0.83 us (1%)
    all_to_all x1, blocking collectives, shards(): parts = lax.all_to_all(parts, 'seq', 0, 0, tiled=True)  32.1 us
    all_to_all x1, waiting for transfers between devices, shards(): shared = lax.all_to_all(last, 'leaf', 0, 0, tiled=True)  24.4 us
    all_to_all x1, starting transfers between devices, shards(): shared = lax.all_to_all(last, 'leaf', 0, 0, tiled=True)  13.7 us
    pallas_call x1, Pallas kernels, shards(): pl.pallas_call(functools.partial(attend_kernel, steps), out_shape=jax.Sha...  2.94 us
    unnamed x10, local copies, waits for them, and re-layouts  1.75 us
  transfers between devices with their start and end apart: 1, of which 1 were waited for; matrix products, arithmetic and copies ran while one was open for 0% of the time, Pallas kernels for 0%

profile of v1, /device:TPU:1, one launch (start us, length us, event | category | flops | bytes accessed | tf_op | source)
XLA Modules:
  0.0 79.9 jit_solution(1466070500598278323)
XLA Ops:
  0.0 0.0 copy-start.3
  0.0 0.0 copy-start.1
  0.0 0.0 copy-start.4
  0.0 0.0 copy-start.2
  0.0 1.3 %slice.16 = s32[1]{0:T(128)} slice(s32[16]{0:T(128)} %lengths_ref.1), slice={[15:16]} | slice | bytes 8 | tf_op jit(solution)/shard_map/slice | solution.py:165
  2.0 0.7 select_bitcast_fusion
  2.7 1.1 %broadcast_in_dim.13 = bf16[32,32,512]{2,1,0:T(8,128)(2,1)} broadcast(bf16[32,512]{1,0:T(8,128)(2,1)S(1)} %bitcast.16), dimensions={1,2} | broadcast | bytes 1081344 | tf_op jit(solution)/shard_map/broadcast_in_dim | solution.py:168
  3.8 13.7 %all-to-all-start = ((bf16[32,32,512]{2,1,0:T(8,128)(2,1)}), bf16[32,32,512]{2,1,0:T(8,128)(2,1)S(1)}, u32[]{:S(2)}, u32[]{:S(2)}) async-start(bf16[32,32,512]{2,1,0:T(8,128)(2,1)} %broadcast_in_dim.13), calls=%async_computation | async-start | bytes 2097152 | tf_op jit(solution)/shard_map/all_to_all | solution.py:169
  17.5 0.0 copy-done.4
  17.6 0.2 copy.8
  17.7 0.1 pad_add_fusion.place_ref
  17.8 24.4 %all-to-all-done.shared_ref = bf16[32,32,512]{2,1,0:T(8,128)(2,1)S(1)} async-done(((bf16[32,32,512]{2,1,0:T(8,128)(2,1)}), bf16[32,32,512]{2,1,0:T(8,128)(2,1)S(1)}, u32[]{:S(2)}, u32[]{:S(2)}) %all-to-all-start) | async-done | bytes 1048608 | tf_op jit(solution)/shard_map/all_to_all | solution.py:169
  42.2 0.0 copy-done.3
  42.2 0.0 copy-done.1
  42.2 0.0 copy-done.2
  42.2 0.0 copy-start
  42.2 1.7 %copy-done = bf16[2,1280,512]{2,1,0:T(8,128)(2,1)S(1)} copy-done((bf16[2,1280,512]{2,1,0:T(8,128)(2,1)S(1)}, bf16[2,1280,512]{2,1,0:T(8,128)(2,1)}, u32[]{:S(2)}) %copy-start) | copy-done | bytes 2621464
  43.9 2.9 %shard_map.55 = f32[16,16,640]{2,1,0:T(8,128)S(1)} custom-call(s32[2]{0:T(128)S(1)} %pad_add_fusion.place_ref, s32[16]{0:T(128)S(1)} %copy-done.3, s32[8,10]{1,0:T(8,128)S(1)} %copy-done.2, bf16[32,4096]{1,0:T(8,128)(2,1)S(1)} %bitcast.13, bf16[2,1280,512]{2,1,0:T(8,128)(2,1)S(1)} %copy-done, bf16[2,256,512]{2,1,0:T(8,128)(2,1)S(1)} %bitcast.14, ...), custom_call_target="tpu_custom_call" | custom-call | tf_op jit(solution)/shard_map/pallas_call | solution.py:175
  46.9 32.1 %all_to_all.10.parts_ref = f32[16,16,640]{2,1,0:T(8,128)S(1)} all-to-all(f32[16,16,640]{2,1,0:T(8,128)S(1)} %shard_map.55), channel_id=1, replica_groups=mesh['seq'=16,'leaf'=32] {'seq'}, dimensions={0} | all-to-all | bytes 1310720 | tf_op jit(solution)/shard_map/all_to_all | solution.py:191
  79.0 0.9 %shard_map.56 = bf16[8,4,256]{2,1,0:T(4,128)(2,1)} custom-call(f32[16,16,640]{2,1,0:T(8,128)S(1)} %all_to_all.10.parts_ref), custom_call_target="tpu_custom_call" | custom-call | tf_op jit(solution)/shard_map/pallas_call | solution.py:192
  (1 shorter events, 0.0 us)
Async XLA Ops:
  0.0 42.2 %copy-start.3 = (s32[16]{0:T(128)S(1)}, s32[16]{0:T(128)}, u32[]{:S(2)}) copy-start(s32[16]{0:T(128)} %lengths_ref.1) | copy-start | bytes 196
  0.0 42.2 %copy-start.1 = (bf16[2,16,16,512]{3,2,1,0:T(8,128)(2,1)S(1)}, bf16[2,16,16,512]{3,2,1,0:T(8,128)(2,1)}, u32[]{:S(2)}) copy-start(bf16[2,16,16,512]{3,2,1,0:T(8,128)(2,1)} %param.7) | copy-start | bytes 1572868
  0.0 17.5 %copy-start.4 = (bf16[8,4,4096]{2,1,0:T(4,128)(2,1)S(1)}, bf16[8,4,4096]{2,1,0:T(4,128)(2,1)}, u32[]{:S(2)}) copy-start(bf16[8,4,4096]{2,1,0:T(4,128)(2,1)} %param.5) | copy-start | bytes 786436
  0.0 42.2 %copy-start.2 = (s32[8,10]{1,0:T(8,128)S(1)}, s32[8,10]{1,0:T(8,128)}, u32[]{:S(2)}) copy-start(s32[8,10]{1,0:T(8,128)} %anc_ref.1) | copy-start | bytes 964
  3.8 38.3 %all-to-all-start = ((bf16[32,32,512]{2,1,0:T(8,128)(2,1)}), bf16[32,32,512]{2,1,0:T(8,128)(2,1)S(1)}, u32[]{:S(2)}, u32[]{:S(2)}) async-start(bf16[32,32,512]{2,1,0:T(8,128)(2,1)} %broadcast_in_dim.13), calls=%async_computation | async-start | bytes 2097152 | tf_op jit(solution)/shard_map/all_to_all | solution.py:169
  42.2 1.7 %copy-start = (bf16[2,1280,512]{2,1,0:T(8,128)(2,1)S(1)}, bf16[2,1280,512]{2,1,0:T(8,128)(2,1)}, u32[]{:S(2)}) copy-start(bf16[2,1280,512]{2,1,0:T(8,128)(2,1)} %prompt_ref.1) | copy-start | bytes 7864324

commit v2 on v1

v2 whole, which is shorter than its diff:
```python
import functools

import jax
import jax.numpy as jnp
from jax import lax
from jax.experimental import pallas as pl
from jax.experimental.pallas import tpu as pltpu
from jax.sharding import PartitionSpec as P

HEADS = 16
KV_HEADS = 2
HEAD_DIM = 256
GROUP = HEADS // KV_HEADS
CHUNK = 256
LANES = 128
Z = 8
INVALID_KEY = 256.0
TOP = 32767.0
POINTS = (2.0**18, 2.0**26, 2.0**23)

VMEM = pl.BlockSpec(memory_space=pltpu.VMEM)
SMEM = pl.BlockSpec(memory_space=pltpu.SMEM)


def params(mib):
    return pltpu.CompilerParams(vmem_limit_bytes=mib * 1024 * 1024)


def fold(x, combine):
    parts = [x[:, i : i + LANES] for i in range(0, x.shape[1], LANES)]
    return functools.reduce(combine, parts)


def tall(x, reps):
    return jnp.concatenate([x] * reps, axis=0)


def node_counts(anc, ids, levels):
    counts = jnp.zeros((anc.shape[0], ids.shape[1]), jnp.float32)
    for level in levels:
        counts = counts + jnp.where(anc[:, level : level + 1] == ids, 1.0, 0.0)
    return counts


def group_query(q_ref, k):
    heads = range(k * GROUP, (k + 1) * GROUP)
    query = jnp.concatenate([q_ref[:, h * HEAD_DIM : (h + 1) * HEAD_DIM] for h in heads], axis=0)
    return query * jnp.bfloat16(1.0 / 16.0)


def dot_nt(a, b):
    return lax.dot_general(a, b, (((1,), (1,)), ((), ())), preferred_element_type=jnp.float32)


def post_kernel(lengths_ref, node_ref, out_ref):
    node_slots = lengths_ref.shape[0]
    tokens = node_ref.shape[2]
    present = lax.axis_index("seq") * tokens < lengths_ref[node_slots - 1]
    keys = jnp.where(present, node_ref[0, 0], jnp.bfloat16(INVALID_KEY))
    values = node_ref[1, 0]
    for copy in range(out_ref.shape[0]):
        out_ref[copy, 0:tokens] = keys
        out_ref[copy, tokens : 2 * tokens] = values


def early_kernel(steps, lengths_ref, anc_ref, q_ref, prompt_ref, node_ref, w_ref, max_ref, total_ref):
    leaf_count, level_count = anc_ref.shape
    node_slots = lengths_ref.shape[0]
    node_cols = node_ref.shape[1]
    tokens = node_cols // node_slots
    prompt_cols = prompt_ref.shape[1]
    anc = anc_ref[...]

    lane = lax.broadcasted_iota(jnp.int32, (1, node_cols), 1)
    slot = lane // tokens
    position = lax.axis_index("seq") * tokens + lane % tokens
    length = jnp.zeros((1, node_cols), jnp.int32)
    for n in range(node_slots):
        length = jnp.where(slot == n, lengths_ref[n], length)
    ids = lax.axis_index("leaf") * node_slots + slot
    upper = node_counts(anc, ids, range(level_count - 1))
    own = node_counts(anc, ids, [level_count - 1])
    mult = []
    for step in range(steps):
        causal = jnp.where(position <= length - steps + step, 1.0, 0.0)
        mult.append(jnp.where(position < length, upper + own * causal, 0.0))
    mult = tall(jnp.concatenate(mult, axis=0), GROUP)

    for k in range(KV_HEADS):
        cols = slice(k * HEAD_DIM, (k + 1) * HEAD_DIM)
        query = group_query(q_ref, k)
        top = None
        for start in range(0, prompt_cols, CHUNK):
            s = dot_nt(query, prompt_ref[0, start : start + CHUNK, cols])
            w_ref[k, :, start : start + CHUNK] = s
            part = fold(s, jnp.maximum)
            top = part if top is None else jnp.maximum(top, part)
        s = dot_nt(query, node_ref[0, :, cols])
        s = jnp.where(mult > 0.0, s, -jnp.inf)
        w_ref[k, :, prompt_cols:] = s
        top = jnp.max(jnp.maximum(top, fold(s, jnp.maximum)), axis=1, keepdims=True)
        total = jnp.zeros((s.shape[0], LANES), jnp.float32)
        for start in range(0, prompt_cols, CHUNK):
            w = jnp.exp(w_ref[k, :, start : start + CHUNK] - top)
            w_ref[k, :, start : start + CHUNK] = w
            total = total + fold(w, jnp.add)
        w = jnp.exp(w_ref[k, :, prompt_cols:] - top) * mult
        w_ref[k, :, prompt_cols:] = w
        total = total + fold(w, jnp.add)
        total_ref[k] = jnp.broadcast_to(jnp.sum(total, axis=1, keepdims=True), total.shape)
        max_ref[k] = jnp.broadcast_to(top, total.shape)


def late_kernel(
    steps, node_slots, anc_ref, q_ref, shared_ref, w_ref, max_ref, total_ref, prompt_ref, node_ref, out_ref
):
    leaf_count, level_count = anc_ref.shape
    owners = shared_ref.shape[0]
    tokens = shared_ref.shape[1] // 2
    prompt_cols = prompt_ref.shape[1]
    shared_cols = owners * tokens
    rows = steps * leaf_count
    half = rows // 2

    lane = lax.broadcasted_iota(jnp.int32, (1, shared_cols), 1)
    owner = lane // tokens
    count = node_counts(anc_ref[...], owner * node_slots + node_slots - 1, range(level_count - 1))
    count = jnp.where(owner == lax.axis_index("leaf"), 0.0, count)
    pick = jnp.where(lax.broadcasted_iota(jnp.int32, (8, HEAD_DIM), 1) == 0, 1.0, 0.0).astype(jnp.bfloat16)

    for k in range(KV_HEADS):
        cols = slice(k * HEAD_DIM, (k + 1) * HEAD_DIM)
        keys = shared_ref[:, 0:tokens, cols].reshape(shared_cols, HEAD_DIM)
        values = shared_ref[:, tokens : 2 * tokens, cols].reshape(shared_cols, HEAD_DIM)
        marks = dot_nt(pick, keys)[0:1]
        mult = tall(jnp.where(marks < INVALID_KEY / 2, count, 0.0), steps * GROUP)
        s = dot_nt(group_query(q_ref, k), keys)
        s = jnp.where(mult > 0.0, s, -jnp.inf)
        early_max = max_ref[k]
        block_max = jnp.maximum(jnp.max(fold(s, jnp.maximum), axis=1, keepdims=True), early_max)
        scale = jnp.exp(early_max - block_max)
        w = jnp.exp(s - block_max[:, 0:1]) * mult
        total = jnp.sum(fold(w, jnp.add), axis=1, keepdims=True) + total_ref[k] * scale
        acc = jnp.dot(w.astype(jnp.bfloat16), values, preferred_element_type=jnp.float32)
        wide = jnp.concatenate([scale, scale], axis=1)
        for start in range(0, prompt_cols, CHUNK):
            w = (w_ref[k, :, start : start + CHUNK] * wide).astype(jnp.bfloat16)
            acc = acc + jnp.dot(w, prompt_ref[0, start : start + CHUNK, cols], preferred_element_type=jnp.float32)
        w = (w_ref[k, :, prompt_cols:] * wide).astype(jnp.bfloat16)
        acc = acc + jnp.dot(w, node_ref[0, :, cols], preferred_element_type=jnp.float32)

        reach = jnp.maximum(jnp.max(fold(jnp.abs(acc), jnp.maximum), axis=1, keepdims=True), 1e-30)
        data = jnp.round(acc * (TOP / reach)).astype(jnp.int32).astype(jnp.int16)
        fixed = [
            jnp.round(value * point).astype(jnp.int32)
            for value, point in zip((block_max, jnp.log(total), jnp.log(reach)), POINTS)
        ]
        lane = lax.broadcasted_iota(jnp.int32, (GROUP * rows, LANES), 1)
        stats = jnp.zeros((GROUP * rows, LANES), jnp.int32)
        for i, value in enumerate(fixed):
            stats = jnp.where(lane == 2 * i, value >> 16, stats)
            stats = jnp.where(lane == 2 * i + 1, (value & 0xFFFF) - 0x8000, stats)
        lane = lane[:half]
        for h in range(GROUP):
            first = h * rows
            for part in range(2):
                lanes = slice(part * HEAD_DIM, (part + 1) * HEAD_DIM)
                out_ref[k * GROUP + h, :, lanes] = data[first + part * half : first + (part + 1) * half]
            low, high = stats[first : first + half], stats[first + half : first + rows]
            both = jnp.where(lane < LANES // 2, low, pltpu.roll(high, LANES // 2, 1))
            out_ref[k * GROUP + h, :, 2 * HEAD_DIM :] = both.astype(jnp.int16)


def merge_kernel(parts_ref, out_ref):
    blocks, half, _ = parts_ref.shape
    leaf_count = out_ref.shape[0]
    stats = [parts_ref[b, :, 2 * HEAD_DIM :].astype(jnp.int32) for b in range(blocks)]
    for part in range(2):
        first = part * LANES // 2

        def value(b, i):
            high = stats[b][:, first + 2 * i : first + 2 * i + 1]
            low = stats[b][:, first + 2 * i + 1 : first + 2 * i + 2] + 0x8000
            return ((high << 16) + low).astype(jnp.float32) * (1.0 / POINTS[i])

        tops = [value(b, 0) for b in range(blocks)]
        row_max = functools.reduce(jnp.maximum, tops)
        denominator = jnp.zeros((half, 1), jnp.float32)
        numerator = jnp.zeros((half, HEAD_DIM), jnp.float32)
        for b in range(blocks):
            shift = tops[b] - row_max
            denominator = denominator + jnp.exp(shift + value(b, 1))
            data = parts_ref[b, :, part * HEAD_DIM : (part + 1) * HEAD_DIM].astype(jnp.int32).astype(jnp.float32)
            numerator = numerator + jnp.exp(shift + value(b, 2)) * data
        merged = (numerator / (denominator * TOP)).astype(jnp.bfloat16)
        for i in range(half // leaf_count):
            out_ref[:, part * half // leaf_count + i, :] = merged[i * leaf_count : (i + 1) * leaf_count]


def gather_shared(own, owners):
    along_z = [list(range(x, x + Z)) for x in range(0, owners, Z)]
    along_x = [list(range(z, owners, Z)) for z in range(Z)]
    plane = lax.all_to_all(own, "leaf", 0, 0, tiled=True, axis_index_groups=along_z)
    plane = jnp.broadcast_to(plane[None], (owners // Z,) + plane.shape)
    shared = lax.all_to_all(plane, "leaf", 0, 0, tiled=True, axis_index_groups=along_x)
    return shared.reshape((owners,) + own.shape[1:])


def shards(queries, prompt_kv, node_kv, node_lengths, ancestors):
    leaf_count, steps, feat_width = queries.shape
    node_slots, tokens = node_kv.shape[1:3]
    prompt_cols = prompt_kv.shape[1]
    width = KV_HEADS * HEAD_DIM
    rows = steps * leaf_count
    owners = lax.axis_size("leaf")

    own = pl.pallas_call(
        post_kernel,
        out_shape=jax.ShapeDtypeStruct((Z, 2 * tokens, width), jnp.bfloat16),
        grid=(1,),
        in_specs=[SMEM, pl.BlockSpec((2, 1, tokens, width), lambda i: (0, node_slots - 1, 0, 0))],
        out_specs=VMEM,
        compiler_params=params(8),
    )(node_lengths, node_kv)
    shared = gather_shared(own, owners)

    query_rows = queries.transpose(1, 0, 2).reshape(rows, feat_width)
    nodes = node_kv.reshape(2, node_slots * tokens, width)
    cols = prompt_cols + node_slots * tokens
    keys_of = lambda n: pl.BlockSpec((1, n, width), lambda i: (0, 0, 0))
    values_of = lambda n: pl.BlockSpec((1, n, width), lambda i: (1, 0, 0))
    row_shape = jax.ShapeDtypeStruct((KV_HEADS, GROUP * rows, LANES), jnp.float32)
    early, early_max, early_total = pl.pallas_call(
        functools.partial(early_kernel, steps),
        out_shape=(jax.ShapeDtypeStruct((KV_HEADS, GROUP * rows, cols), jnp.float32), row_shape, row_shape),
        grid=(1,),
        in_specs=[SMEM, VMEM, VMEM, keys_of(prompt_cols), keys_of(node_slots * tokens)],
        out_specs=(VMEM, VMEM, VMEM),
        compiler_params=params(16),
        cost_estimate=pl.CostEstimate(flops=500_000_000, bytes_accessed=6_000_000, transcendentals=800_000),
    )(node_lengths, ancestors, query_rows, prompt_kv, nodes)

    parts = pl.pallas_call(
        functools.partial(late_kernel, steps, node_slots),
        out_shape=jax.ShapeDtypeStruct((HEADS, rows // 2, 2 * HEAD_DIM + LANES), jnp.int16),
        grid=(1,),
        in_specs=[VMEM, VMEM, VMEM, VMEM, VMEM, VMEM, values_of(prompt_cols), values_of(node_slots * tokens)],
        out_specs=VMEM,
        compiler_params=params(16),
    )(ancestors, query_rows, shared, early, early_max, early_total, prompt_kv, nodes)

    parts = lax.all_to_all(parts, "seq", 0, 0, tiled=True)
    return pl.pallas_call(
        merge_kernel,
        out_shape=jax.ShapeDtypeStruct((leaf_count, steps, HEAD_DIM), jnp.bfloat16),
        in_specs=[VMEM],
        out_specs=VMEM,
        compiler_params=params(8),
    )(parts)


def solution(mesh):
    placed = (
        P("leaf", None, None),
        P(None, "seq", None),
        P(None, "leaf", "seq", None),
        P("leaf"),
        P("leaf", None),
    )
    return jax.shard_map(
        shards, mesh=mesh, in_specs=placed, out_specs=P("leaf", None, "seq"), check_vma=False
    )
```

time: 80.3 us -> 72.9 us (0.908)
  waiting for transfers between devices: 24.4 us -> 6.6 us
  blocking collectives: 32.1 us -> 44.9 us
  starting transfers between devices: 13.7 us -> 4.24 us
  local copies, waits for them, and re-layouts: 4.3 us -> 10.8 us
  Pallas kernels: 3.89 us -> 5.88 us
  other arithmetic: 0.83 us -> 0 us
    all_to_all x0 -> x1, blocking collectives: none -> 21.2 us  [gather_shared(): lax.all_to_all(own, 'leaf', 0, 0, tiled=True, axis_index_groups=along_z)]
    all_to_all x1, waiting for transfers between devices: 24.4 us -> 6.6 us  [gather_shared(): lax.all_to_all(plane, 'leaf', 0, 0, tiled=True, axis_index_groups=along_x)]
    all_to_all x1, starting transfers between devices: 13.7 us -> 4.24 us  [gather_shared(): lax.all_to_all(plane, 'leaf', 0, 0, tiled=True, axis_index_groups=along_x)]
    all_to_all x1, blocking collectives: 32.1 us -> 23.7 us  [shards(): parts = lax.all_to_all(parts, 'seq', 0, 0, tiled=True)]
    unnamed x10 -> x24, local copies, waits for them, and re-layouts: 1.75 us -> 8.57 us
    pallas_call x1 -> x3, Pallas kernels: 2.94 us -> 4.92 us  [the longest x1 2.84 us: shards(): pl.pallas_call(functools.partial(late_kernel, steps, node_slots), out_sha...]
    slice x1 -> x0, local copies, waits for them, and re-layouts: 1.31 us -> none  [shards(): present = lax.axis_index('seq') * tokens < node_lengths[node_slots - 1]]
    transpose x1, local copies, waits for them, and re-layouts: 0.15 us -> 1.1 us  [shards(): query_rows = queries.transpose(1, 0, 2).reshape(rows, feat_width)]
  transfers between devices with their start and end apart: 1 -> 1, of which waited for: 1 -> 1; matrix products, arithmetic and copies ran while one was open for 0% -> 2% of each run, Pallas kernels for 0% -> 2%
where the time goes in v2:
time: 72.9 us; the launch traced here: 72.5 us
  blocking collectives  44.9 us (62%)
  local copies, waits for them, and re-layouts  10.8 us (15%)
  waiting for transfers between devices  6.6 us (9%)
  Pallas kernels  5.88 us (8%)
  starting transfers between devices  4.24 us (6%)
    all_to_all x1, blocking collectives, shards(): parts = lax.all_to_all(parts, 'seq', 0, 0, tiled=True)  23.7 us
    all_to_all x1, blocking collectives, gather_shared(): lax.all_to_all(own, 'leaf', 0, 0, tiled=True, axis_index_groups=along_z)  21.2 us
    unnamed x24, local copies, waits for them, and re-layouts  8.57 us
    all_to_all x1, waiting for transfers between devices, gather_shared(): lax.all_to_all(plane, 'leaf', 0, 0, tiled=True, axis_index_groups=along_x)  6.6 us
    all_to_all x1, starting transfers between devices, gather_shared(): lax.all_to_all(plane, 'leaf', 0, 0, tiled=True, axis_index_groups=along_x)  4.24 us
    pallas_call x1, Pallas kernels, shards(): pl.pallas_call(functools.partial(late_kernel, steps, node_slots), out_sha...  2.84 us
    pallas_call x1, Pallas kernels, shards(): pl.pallas_call(functools.partial(early_kernel, steps), out_shape=(jax.Sha...  1.52 us
  transfers between devices with their start and end apart: 1, of which 1 were waited for; matrix products, arithmetic and copies ran while one was open for 2% of the time, Pallas kernels for 2%

profile of v2, /device:TPU:1, one launch (start us, length us, event | category | flops | bytes accessed | tf_op | source)
XLA Modules:
  0.0 72.5 jit_solution(16506463623291703972)
XLA Ops:
  0.0 0.0 copy-start.1
  0.0 1.0 %copy-done.1 = bf16[2,16,16,512]{3,2,1,0:T(8,128)(2,1)S(1)} copy-done((bf16[2,16,16,512]{3,2,1,0:T(8,128)(2,1)S(1)}, bf16[2,16,16,512]{3,2,1,0:T(8,128)(2,1)}, u32[]{:S(2)}) %copy-start.1) | copy-done | bytes 524312
  1.0 0.0 copy-start.10
  1.0 0.7 copy-done.10
  1.7 0.0 copy-start
  1.7 0.0 copy-start.2
  1.7 0.0 copy-start.9
  1.7 0.0 copy-start.11
  1.7 0.6 shard_map.55
  2.3 21.2 %all_to_all.15 = bf16[8,32,512]{2,1,0:T(8,128)(2,1)S(1)} all-to-all(bf16[8,32,512]{2,1,0:T(8,128)(2,1)S(1)} %shard_map.55), channel_id=1, replica_groups={{0,1,2,3,4,5,6,7},{8,9,10,11,12,13,14,15},{16,17,18,19,20,21,22,23},{24..., dimensions={0} | all-to-all | bytes 524288 | tf_op jit(solution)/shard_map/all_to_all | solution.py:203
  23.4 1.1 %broadcast_in_dim.2 = bf16[4,8,32,512]{3,2,1,0:T(8,128)(2,1)} broadcast(bf16[8,32,512]{2,1,0:T(8,128)(2,1)S(1)} %all_to_all.15), dimensions={1,2,3} | broadcast | bytes 1310720 | tf_op jit(solution)/shard_map/broadcast_in_dim | solution.py:204
  24.5 4.2 %all-to-all-start.1 = ((bf16[4,8,32,512]{3,2,1,0:T(8,128)(2,1)}), bf16[4,8,32,512]{3,2,1,0:T(8,128)(2,1)}, u32[]{:S(2)}, u32[]{:S(2)}) async-start(bf16[4,8,32,512]{3,2,1,0:T(8,128)(2,1)} %broadcast_in_dim.2), calls=%async_computation.1 | async-start | bytes 2097152 | tf_op jit(solution)/shard_map/all_to_all | solution.py:205
  28.8 1.1 %copy.8 = bf16[4,8,4096]{2,1,0:T(8,128)(2,1)S(1)} copy(bf16[4,8,4096]{2,0,1:T(4,128)(2,1)} %bitcast.10) | data formatting | bytes 524288 | tf_op jit(solution)/shard_map/transpose | solution.py:227
  29.9 0.0 copy-done
  29.9 0.0 copy-done.2
  29.9 0.0 copy-done.9
  29.9 0.0 copy-done.11
  29.9 1.5 %shard_map.56 = (f32[2,256,1536]{2,1,0:T(8,128)S(1)}, f32[2,256,128]{2,1,0:T(8,128)S(1)}, f32[2,256,128]{2,1,0:T(8,128)S(1)}) custom-call(s32[16]{0:T(128)S(1)} %copy-done.11, s32[8,10]{1,0:T(8,128)S(1)} %copy-done.9, bf16[32,4096]{1,0:T(8,128)(2,1)S(1)} %bitcast.8, bf16[2,1280,512]{2,1,0:T(8,128)(2,1)S(1)} %copy-done, bf16[2,256,512]{2,1,0:T(8,128)(2,1)S(1)} %bitcast.6), custom_call_target="tpu_custom_call" | custom-call | flops 500000000 | bytes 6000000 | tf_op jit(solution)/shard_map/pallas_call | solution.py:233
  31.5 0.0 copy-start.3
  31.5 1.6 %copy-done.3 = f32[2,256,1536]{2,1,0:T(8,128)} copy-done((f32[2,256,1536]{2,1,0:T(8,128)}, f32[2,256,1536]{2,1,0:T(8,128)S(1)}, u32[]{:S(2)}) %copy-start.3) | copy-done | bytes 3145752
  33.1 0.0 copy-start.5
  33.1 0.7 copy-done.5
  33.8 0.0 copy-start.7
  33.8 0.7 copy-done.7
  34.5 6.6 %all-to-all-done.1 = bf16[4,8,32,512]{3,2,1,0:T(8,128)(2,1)} async-done(((bf16[4,8,32,512]{3,2,1,0:T(8,128)(2,1)}), bf16[4,8,32,512]{3,2,1,0:T(8,128)(2,1)}, u32[]{:S(2)}, u32[]{:S(2)}) %all-to-all-start.1) | async-done | bytes 1048608 | tf_op jit(solution)/shard_map/all_to_all | solution.py:205
  41.1 0.0 copy-start.4
  41.1 1.9 %copy-done.4 = f32[2,256,1536]{2,1,0:T(8,128)S(1)} copy-done((f32[2,256,1536]{2,1,0:T(8,128)S(1)}, f32[2,256,1536]{2,1,0:T(8,128)}, u32[]{:S(2)}) %copy-start.4) | copy-done | bytes 3145752
  43.0 0.0 copy-start.6
  43.0 0.9 %copy-done.6 = f32[2,256,128]{2,1,0:T(8,128)S(1)} copy-done((f32[2,256,128]{2,1,0:T(8,128)S(1)}, f32[2,256,128]{2,1,0:T(8,128)}, u32[]{:S(2)}) %copy-start.6) | copy-done | bytes 262168
  44.0 0.0 copy-start.8
  44.0 0.9 %copy-done.8 = f32[2,256,128]{2,1,0:T(8,128)S(1)} copy-done((f32[2,256,128]{2,1,0:T(8,128)S(1)}, f32[2,256,128]{2,1,0:T(8,128)}, u32[]{:S(2)}) %copy-start.8) | copy-done | bytes 262168
  44.9 2.8 %shard_map.57 = s16[16,16,640]{2,1,0:T(8,128)(2,1)S(1)} custom-call(s32[8,10]{1,0:T(8,128)S(1)} %copy-done.9, bf16[32,4096]{1,0:T(8,128)(2,1)S(1)} %bitcast.9, bf16[32,32,512]{2,1,0:T(8,128)(2,1)} %bitcast.2.shared_ref, f32[2,256,1536]{2,1,0:T(8,128)S(1)} %copy-done.4, f32[2,256,128]{2,1,0:T(8,128)S(1)} %copy-done.6, f32[2,256,128]{2,1,0:T(8,128)S(1)} %copy-done.8, ...), custom_call_target="tpu_custom_call" | custom-call | tf_op jit(solution)/shard_map/pallas_call | solution.py:243
  47.8 23.7 %all_to_all.16.parts_ref = s16[16,16,640]{2,1,0:T(8,128)(2,1)S(1)} all-to-all(s16[16,16,640]{2,1,0:T(8,128)(2,1)S(1)} %shard_map.57), channel_id=1, replica_groups=mesh['seq'=16,'leaf'=32] {'seq'}, dimensions={0} | all-to-all | bytes 655360 | tf_op jit(solution)/shard_map/all_to_all | solution.py:252
  71.5 1.0 %shard_map.58 = bf16[8,4,256]{2,1,0:T(4,128)(2,1)} custom-call(s16[16,16,640]{2,1,0:T(8,128)(2,1)S(1)} %all_to_all.16.parts_ref), custom_call_target="tpu_custom_call" | custom-call | tf_op jit(solution)/shard_map/pallas_call | solution.py:253
Async XLA Ops:
  0.0 1.0 %copy-start.1 = (bf16[2,16,16,512]{3,2,1,0:T(8,128)(2,1)S(1)}, bf16[2,16,16,512]{3,2,1,0:T(8,128)(2,1)}, u32[]{:S(2)}) copy-start(bf16[2,16,16,512]{3,2,1,0:T(8,128)(2,1)} %node_ref.1) | copy-start | bytes 1572868
  1.0 0.7 copy-start.10
  1.7 28.2 %copy-start = (bf16[2,1280,512]{2,1,0:T(8,128)(2,1)S(1)}, bf16[2,1280,512]{2,1,0:T(8,128)(2,1)}, u32[]{:S(2)}) copy-start(bf16[2,1280,512]{2,1,0:T(8,128)(2,1)} %prompt_ref.3) | copy-start | bytes 7864324
  1.7 28.2 %copy-start.2 = (bf16[2,16,16,512]{3,2,1,0:T(8,128)(2,1)S(1)}, bf16[2,16,16,512]{3,2,1,0:T(8,128)(2,1)}, u32[]{:S(2)}) copy-start(bf16[2,16,16,512]{3,2,1,0:T(8,128)(2,1)} %node_ref.1) | copy-start | bytes 1572868
  1.7 28.2 %copy-start.9 = (s32[8,10]{1,0:T(8,128)S(1)}, s32[8,10]{1,0:T(8,128)}, u32[]{:S(2)}) copy-start(s32[8,10]{1,0:T(8,128)} %anc_ref.3) | copy-start | bytes 964
  1.7 28.2 %copy-start.11 = (s32[16]{0:T(128)S(1)}, s32[16]{0:T(128)}, u32[]{:S(2)}) copy-start(s32[16]{0:T(128)} %lengths_ref.3) | copy-start | bytes 196
  24.5 16.6 %all-to-all-start.1 = ((bf16[4,8,32,512]{3,2,1,0:T(8,128)(2,1)}), bf16[4,8,32,512]{3,2,1,0:T(8,128)(2,1)}, u32[]{:S(2)}, u32[]{:S(2)}) async-start(bf16[4,8,32,512]{3,2,1,0:T(8,128)(2,1)} %broadcast_in_dim.2), calls=%async_computation.1 | async-start | bytes 2097152 | tf_op jit(solution)/shard_map/all_to_all | solution.py:205
  31.5 1.6 %copy-start.3 = (f32[2,256,1536]{2,1,0:T(8,128)}, f32[2,256,1536]{2,1,0:T(8,128)S(1)}, u32[]{:S(2)}) copy-start(f32[2,256,1536]{2,1,0:T(8,128)S(1)} %get-tuple-element.8.w_ref) | copy-start | bytes 9437188
  33.1 0.7 %copy-start.5 = (f32[2,256,128]{2,1,0:T(8,128)}, f32[2,256,128]{2,1,0:T(8,128)S(1)}, u32[]{:S(2)}) copy-start(f32[2,256,128]{2,1,0:T(8,128)S(1)} %get-tuple-element.9.max_ref) | copy-start | bytes 786436
  33.8 0.7 copy-start.7
  41.1 1.9 %copy-start.4 = (f32[2,256,1536]{2,1,0:T(8,128)S(1)}, f32[2,256,1536]{2,1,0:T(8,128)}, u32[]{:S(2)}) copy-start(f32[2,256,1536]{2,1,0:T(8,128)} %copy-done.3) | copy-start | bytes 9437188
  43.0 0.9 %copy-start.6 = (f32[2,256,128]{2,1,0:T(8,128)S(1)}, f32[2,256,128]{2,1,0:T(8,128)}, u32[]{:S(2)}) copy-start(f32[2,256,128]{2,1,0:T(8,128)} %copy-done.5) | copy-start | bytes 786436
  44.0 0.9 %copy-start.8 = (f32[2,256,128]{2,1,0:T(8,128)S(1)}, f32[2,256,128]{2,1,0:T(8,128)}, u32[]{:S(2)}) copy-start(f32[2,256,128]{2,1,0:T(8,128)} %copy-done.7) | copy-start | bytes 786436

commit v3 on v2

--- a/solution.py
+++ b/solution.py
@@ -19,7 +19,11 @@
 POINTS = (2.0**18, 2.0**26, 2.0**23)
 
 VMEM = pl.BlockSpec(memory_space=pltpu.VMEM)
-SMEM = pl.BlockSpec(memory_space=pltpu.SMEM)
+HBM = pl.BlockSpec(memory_space=pltpu.HBM)
+
+
+def in_hbm(*arrays):
+    return [pltpu.with_memory_space_constraint(array, pltpu.HBM) for array in arrays]
 
 
 def params(mib):
@@ -52,24 +56,77 @@
     return lax.dot_general(a, b, (((1,), (1,)), ((), ())), preferred_element_type=jnp.float32)
 
 
-def post_kernel(lengths_ref, node_ref, out_ref):
-    node_slots = lengths_ref.shape[0]
-    tokens = node_ref.shape[2]
+def fetch(pairs, sems):
+    copies = [pltpu.make_async_copy(src, dst, sems.at[i]) for i, (src, dst) in enumerate(pairs)]
+    for copy in copies:
+        copy.start()
+    return copies
+
+
+def post_kernel(lengths_hbm, node_hbm, out_ref, node_ref, lengths_ref, sems):
+    node_slots = lengths_hbm.shape[0]
+    tokens = node_ref.shape[1]
+    for copy in fetch([(node_hbm.at[:, node_slots - 1], node_ref), (lengths_hbm, lengths_ref)], sems):
+        copy.wait()
     present = lax.axis_index("seq") * tokens < lengths_ref[node_slots - 1]
-    keys = jnp.where(present, node_ref[0, 0], jnp.bfloat16(INVALID_KEY))
-    values = node_ref[1, 0]
+    keys = jnp.where(present, node_ref[0], jnp.bfloat16(INVALID_KEY))
+    values = node_ref[1]
     for copy in range(out_ref.shape[0]):
         out_ref[copy, 0:tokens] = keys
         out_ref[copy, tokens : 2 * tokens] = values
 
 
-def early_kernel(steps, lengths_ref, anc_ref, q_ref, prompt_ref, node_ref, w_ref, max_ref, total_ref):
+def copies_kernel(plane_ref, out_ref):
+    for copy in range(out_ref.shape[0]):
+        out_ref[copy] = plane_ref[...]
+
+
+def early_kernel(
+    steps,
+    lengths_hbm,
+    anc_hbm,
+    prompt_hbm,
+    node_hbm,
+    q_ref,
+    w_ref,
+    max_ref,
+    total_ref,
+    query_ref,
+    count_ref,
+    prompt_values_ref,
+    node_values_ref,
+    lengths_ref,
+    anc_ref,
+    prompt_ref,
+    node_ref,
+    sems,
+):
+    copies = fetch(
+        [
+            (lengths_hbm, lengths_ref),
+            (anc_hbm, anc_ref),
+            (node_hbm.at[0], node_ref),
+            (prompt_hbm.at[0], prompt_ref),
+            (node_hbm.at[1], node_values_ref),
+            (prompt_hbm.at[1], prompt_values_ref),
+        ],
+        sems,
+    )
     leaf_count, level_count = anc_ref.shape
-    node_slots = lengths_ref.shape[0]
-    node_cols = node_ref.shape[1]
-    tokens = node_cols // node_slots
-    prompt_cols = prompt_ref.shape[1]
+    node_slots, tokens, width = node_ref.shape
+    node_cols = node_slots * tokens
+    prompt_cols = prompt_ref.shape[0]
+    shared_cols = count_ref.shape[1]
+    for k in range(KV_HEADS):
+        query_ref[k] = group_query(q_ref, k)
+    copies[0].wait()
+    copies[1].wait()
     anc = anc_ref[...]
+
+    lane = lax.broadcasted_iota(jnp.int32, (1, shared_cols), 1)
+    owner = lane // tokens
+    count = node_counts(anc, owner * node_slots + node_slots - 1, range(level_count - 1))
+    count_ref[...] = jnp.where(owner == lax.axis_index("leaf"), 0.0, count)
 
     lane = lax.broadcasted_iota(jnp.int32, (1, node_cols), 1)
     slot = lane // tokens
@@ -85,17 +142,19 @@
         causal = jnp.where(position <= length - steps + step, 1.0, 0.0)
         mult.append(jnp.where(position < length, upper + own * causal, 0.0))
     mult = tall(jnp.concatenate(mult, axis=0), GROUP)
+    copies[2].wait()
+    copies[3].wait()
 
     for k in range(KV_HEADS):
         cols = slice(k * HEAD_DIM, (k + 1) * HEAD_DIM)
-        query = group_query(q_ref, k)
+        query = query_ref[k]
         top = None
         for start in range(0, prompt_cols, CHUNK):
-            s = dot_nt(query, prompt_ref[0, start : start + CHUNK, cols])
+            s = dot_nt(query, prompt_ref[start : start + CHUNK, cols])
             w_ref[k, :, start : start + CHUNK] = s
             part = fold(s, jnp.maximum)
             top = part if top is None else jnp.maximum(top, part)
-        s = dot_nt(query, node_ref[0, :, cols])
+        s = dot_nt(query, node_ref[:, :, cols].reshape(node_cols, HEAD_DIM))
         s = jnp.where(mult > 0.0, s, -jnp.inf)
         w_ref[k, :, prompt_cols:] = s
         top = jnp.max(jnp.maximum(top, fold(s, jnp.maximum)), axis=1, keepdims=True)
@@ -109,23 +168,20 @@
         total = total + fold(w, jnp.add)
         total_ref[k] = jnp.broadcast_to(jnp.sum(total, axis=1, keepdims=True), total.shape)
         max_ref[k] = jnp.broadcast_to(top, total.shape)
-
-
-def late_kernel(
-    steps, node_slots, anc_ref, q_ref, shared_ref, w_ref, max_ref, total_ref, prompt_ref, node_ref, out_ref
-):
-    leaf_count, level_count = anc_ref.shape
+    copies[4].wait()
+    copies[5].wait()
+
+
+def late_kernel(query_ref, shared_ref, w_ref, max_ref, total_ref, count_ref, prompt_ref, node_ref, out_ref):
     owners = shared_ref.shape[0]
     tokens = shared_ref.shape[1] // 2
-    prompt_cols = prompt_ref.shape[1]
+    prompt_cols = prompt_ref.shape[0]
+    node_cols = node_ref.shape[0] * node_ref.shape[1]
     shared_cols = owners * tokens
-    rows = steps * leaf_count
+    rows = query_ref.shape[1] // GROUP
     half = rows // 2
-
-    lane = lax.broadcasted_iota(jnp.int32, (1, shared_cols), 1)
-    owner = lane // tokens
-    count = node_counts(anc_ref[...], owner * node_slots + node_slots - 1, range(level_count - 1))
-    count = jnp.where(owner == lax.axis_index("leaf"), 0.0, count)
+    count = count_ref[...]
+    reps = GROUP * rows // count.shape[0]
     pick = jnp.where(lax.broadcasted_iota(jnp.int32, (8, HEAD_DIM), 1) == 0, 1.0, 0.0).astype(jnp.bfloat16)
 
     for k in range(KV_HEADS):
@@ -133,8 +189,8 @@
         keys = shared_ref[:, 0:tokens, cols].reshape(shared_cols, HEAD_DIM)
         values = shared_ref[:, tokens : 2 * tokens, cols].reshape(shared_cols, HEAD_DIM)
         marks = dot_nt(pick, keys)[0:1]
-        mult = tall(jnp.where(marks < INVALID_KEY / 2, count, 0.0), steps * GROUP)
-        s = dot_nt(group_query(q_ref, k), keys)
+        mult = tall(jnp.where(marks < INVALID_KEY / 2, count, 0.0), reps)
+        s = dot_nt(query_ref[k], keys)
         s = jnp.where(mult > 0.0, s, -jnp.inf)
         early_max = max_ref[k]
         block_max = jnp.maximum(jnp.max(fold(s, jnp.maximum), axis=1, keepdims=True), early_max)
@@ -145,9 +201,10 @@
         wide = jnp.concatenate([scale, scale], axis=1)
         for start in range(0, prompt_cols, CHUNK):
             w = (w_ref[k, :, start : start + CHUNK] * wide).astype(jnp.bfloat16)
-            acc = acc + jnp.dot(w, prompt_ref[0, start : start + CHUNK, cols], preferred_element_type=jnp.float32)
+            acc = acc + jnp.dot(w, prompt_ref[start : start + CHUNK, cols], preferred_element_type=jnp.float32)
         w = (w_ref[k, :, prompt_cols:] * wide).astype(jnp.bfloat16)
-        acc = acc + jnp.dot(w, node_ref[0, :, cols], preferred_element_type=jnp.float32)
+        node_values = node_ref[:, :, cols].reshape(node_cols, HEAD_DIM)
+        acc = acc + jnp.dot(w, node_values, preferred_element_type=jnp.float32)
 
         reach = jnp.maximum(jnp.max(fold(jnp.abs(acc), jnp.maximum), axis=1, keepdims=True), 1e-30)
         data = jnp.round(acc * (TOP / reach)).astype(jnp.int32).astype(jnp.int16)
@@ -201,7 +258,13 @@
     along_z = [list(range(x, x + Z)) for x in range(0, owners, Z)]
     along_x = [list(range(z, owners, Z)) for z in range(Z)]
     plane = lax.all_to_all(own, "leaf", 0, 0, tiled=True, axis_index_groups=along_z)
-    plane = jnp.broadcast_to(plane[None], (owners // Z,) + plane.shape)
+    plane = pl.pallas_call(
+        copies_kernel,
+        out_shape=jax.ShapeDtypeStruct((owners // Z,) + plane.shape, plane.dtype),
+        in_specs=[VMEM],
+        out_specs=VMEM,
+        compiler_params=params(8),
+    )(plane)
     shared = lax.all_to_all(plane, "leaf", 0, 0, tiled=True, axis_index_groups=along_x)
     return shared.reshape((owners,) + own.shape[1:])
 
@@ -217,37 +280,51 @@
     own = pl.pallas_call(
         post_kernel,
         out_shape=jax.ShapeDtypeStruct((Z, 2 * tokens, width), jnp.bfloat16),
-        grid=(1,),
-        in_specs=[SMEM, pl.BlockSpec((2, 1, tokens, width), lambda i: (0, node_slots - 1, 0, 0))],
+        in_specs=[HBM, HBM],
         out_specs=VMEM,
+        scratch_shapes=[
+            pltpu.VMEM((2, tokens, width), jnp.bfloat16),
+            pltpu.SMEM((node_slots,), jnp.int32),
+            pltpu.SemaphoreType.DMA((2,)),
+        ],
         compiler_params=params(8),
-    )(node_lengths, node_kv)
+    )(*in_hbm(node_lengths, node_kv))
     shared = gather_shared(own, owners)
 
     query_rows = queries.transpose(1, 0, 2).reshape(rows, feat_width)
-    nodes = node_kv.reshape(2, node_slots * tokens, width)
     cols = prompt_cols + node_slots * tokens
-    keys_of = lambda n: pl.BlockSpec((1, n, width), lambda i: (0, 0, 0))
-    values_of = lambda n: pl.BlockSpec((1, n, width), lambda i: (1, 0, 0))
     row_shape = jax.ShapeDtypeStruct((KV_HEADS, GROUP * rows, LANES), jnp.float32)
-    early, early_max, early_total = pl.pallas_call(
+    weights, early_max, early_total, query, count, prompt_values, node_values = pl.pallas_call(
         functools.partial(early_kernel, steps),
-        out_shape=(jax.ShapeDtypeStruct((KV_HEADS, GROUP * rows, cols), jnp.float32), row_shape, row_shape),
-        grid=(1,),
-        in_specs=[SMEM, VMEM, VMEM, keys_of(prompt_cols), keys_of(node_slots * tokens)],
-        out_specs=(VMEM, VMEM, VMEM),
+        out_shape=(
+            jax.ShapeDtypeStruct((KV_HEADS, GROUP * rows, cols), jnp.float32),
+            row_shape,
+            row_shape,
+            jax.ShapeDtypeStruct((KV_HEADS, GROUP * rows, HEAD_DIM), jnp.bfloat16),
+            jax.ShapeDtypeStruct((leaf_count, owners * tokens), jnp.float32),
+            jax.ShapeDtypeStruct((prompt_cols, width), jnp.bfloat16),
+            jax.ShapeDtypeStruct((node_slots, tokens, width), jnp.bfloat16),
+        ),
+        in_specs=[HBM, HBM, HBM, HBM, VMEM],
+        out_specs=(VMEM,) * 7,
+        scratch_shapes=[
+            pltpu.SMEM((node_slots,), jnp.int32),
+            pltpu.VMEM(ancestors.shape, jnp.int32),
+            pltpu.VMEM((prompt_cols, width), jnp.bfloat16),
+            pltpu.VMEM((node_slots, tokens, width), jnp.bfloat16),
+            pltpu.SemaphoreType.DMA((6,)),
+        ],
         compiler_params=params(16),
         cost_estimate=pl.CostEstimate(flops=500_000_000, bytes_accessed=6_000_000, transcendentals=800_000),
-    )(node_lengths, ancestors, query_rows, prompt_kv, nodes)
+    )(*in_hbm(node_lengths, ancestors, prompt_kv, node_kv), query_rows)
 
     parts = pl.pallas_call(
-        functools.partial(late_kernel, steps, node_slots),
+        late_kernel,
         out_shape=jax.ShapeDtypeStruct((HEADS, rows // 2, 2 * HEAD_DIM + LANES), jnp.int16),
-        grid=(1,),
-        in_specs=[VMEM, VMEM, VMEM, VMEM, VMEM, VMEM, values_of(prompt_cols), values_of(node_slots * tokens)],
+        in_specs=[VMEM] * 8,
         out_specs=VMEM,
         compiler_params=params(16),
-    )(ancestors, query_rows, shared, early, early_max, early_total, prompt_kv, nodes)
+    )(query, shared, weights, early_max, early_total, count, prompt_values, node_values)
 
     parts = lax.all_to_all(parts, "seq", 0, 0, tiled=True)
     return pl.pallas_call(

time: 72.9 us -> 67.7 us (0.929)
  local copies, waits for them, and re-layouts: 10.8 us -> 3.69 us
  waiting for transfers between devices: 6.6 us -> 7.8 us
  Pallas kernels: 5.88 us -> 6.87 us
    unnamed x24 -> x6, local copies, waits for them, and re-layouts: 8.57 us -> 3.54 us
    all_to_all x1, waiting for transfers between devices: 6.6 us -> 7.8 us  [gather_shared(): lax.all_to_all(plane, 'leaf', 0, 0, tiled=True, axis_index_groups=along_x)]
    broadcast_in_dim x1 -> x0, local copies, waits for them, and re-layouts: 1.1 us -> none  [gather_shared(): plane = jnp.broadcast_to(plane[None], (owners // Z,) + plane.shape)]
    transpose x1, local copies, waits for them, and re-layouts: 1.1 us -> 0.15 us  [shards(): query_rows = queries.transpose(1, 0, 2).reshape(rows, feat_width)]
    pallas_call x1, Pallas kernels: 1.52 us -> 2.47 us  [shards(): pl.pallas_call(functools.partial(early_kernel, steps), out_shape=(jax.Sha...]
    pallas_call x1 -> x2, Pallas kernels: 2.84 us -> 2.6 us  [the longest x1 1.55 us: shards(): pl.pallas_call(late_kernel, out_shape=jax.ShapeDtypeStruct((HEADS, rows /...]
  transfers between devices with their start and end apart: 1 -> 1, of which waited for: 1 -> 1; matrix products, arithmetic and copies ran while one was open for 2% -> 0% of each run, Pallas kernels for 2% -> 4%
where the time goes in v3:
time: 67.7 us; the launch traced here: 67.4 us
  blocking collectives  45 us (66%)
  waiting for transfers between devices  7.8 us (12%)
  Pallas kernels  6.87 us (10%)
  starting transfers between devices  4.01 us (6%)
  local copies, waits for them, and re-layouts  3.69 us (5%)
    all_to_all x1, blocking collectives, shards(): parts = lax.all_to_all(parts, 'seq', 0, 0, tiled=True)  23.9 us
    all_to_all x1, blocking collectives, gather_shared(): lax.all_to_all(own, 'leaf', 0, 0, tiled=True, axis_index_groups=along_z)  21 us
    all_to_all x1, waiting for transfers between devices, gather_shared(): lax.all_to_all(plane, 'leaf', 0, 0, tiled=True, axis_index_groups=along_x)  7.8 us
    all_to_all x1, starting transfers between devices, gather_shared(): lax.all_to_all(plane, 'leaf', 0, 0, tiled=True, axis_index_groups=along_x)  4.01 us
    unnamed x6, local copies, waits for them, and re-layouts  3.54 us
    pallas_call x1, Pallas kernels, shards(): pl.pallas_call(functools.partial(early_kernel, steps), out_shape=(jax.Sha...  2.47 us
    pallas_call x1, Pallas kernels, shards(): pl.pallas_call(late_kernel, out_shape=jax.ShapeDtypeStruct((HEADS, rows /...  1.55 us
  transfers between devices with their start and end apart: 1, of which 1 were waited for; matrix products, arithmetic and copies ran while one was open for 0% of the time, Pallas kernels for 4%

profile of v3, /device:TPU:1, one launch (start us, length us, event | category | flops | bytes accessed | tf_op | source)
XLA Modules:
  0.0 67.4 jit_solution(18322448282410922115)
XLA Ops:
  0.0 0.0 copy-start.2
  0.0 0.8 %shard_map.56 = bf16[8,32,512]{2,1,0:T(8,128)(2,1)S(1)} custom-call(s32[16]{0:T(128)} %lengths_hbm.3, bf16[2,16,16,512]{3,2,1,0:T(8,128)(2,1)} %node_hbm.3), custom_call_target="tpu_custom_call" | custom-call | tf_op jit(solution)/shard_map/pallas_call | solution.py:280
  0.9 21.0 %all_to_all.15.plane_ref = bf16[8,32,512]{2,1,0:T(8,128)(2,1)S(1)} all-to-all(bf16[8,32,512]{2,1,0:T(8,128)(2,1)S(1)} %shard_map.56), channel_id=1, replica_groups={{0,1,2,3,4,5,6,7},{8,9,10,11,12,13,14,15},{16,17,18,19,20,21,22,23},{24..., dimensions={0} | all-to-all | bytes 524288 | tf_op jit(solution)/shard_map/all_to_all | solution.py:260
  21.9 1.0 %shard_map.57 = bf16[4,8,32,512]{3,2,1,0:T(8,128)(2,1)} custom-call(bf16[8,32,512]{2,1,0:T(8,128)(2,1)S(1)} %all_to_all.15.plane_ref), custom_call_target="tpu_custom_call" | custom-call | tf_op jit(solution)/shard_map/pallas_call | solution.py:261
  22.9 4.0 %all-to-all-start.1 = ((bf16[4,8,32,512]{3,2,1,0:T(8,128)(2,1)}), bf16[4,8,32,512]{3,2,1,0:T(8,128)(2,1)S(1)}, u32[]{:S(2)}, u32[]{:S(2)}) async-start(bf16[4,8,32,512]{3,2,1,0:T(8,128)(2,1)} %shard_map.57), calls=%async_computation.1 | async-start | bytes 2097152 | tf_op jit(solution)/shard_map/all_to_all | solution.py:268
  27.0 0.0 copy-done.2
  27.0 0.1 copy.8
  27.1 2.5 %shard_map.55 = (f32[2,256,1536]{2,1,0:T(8,128)S(1)}, f32[2,256,128]{2,1,0:T(8,128)S(1)}, f32[2,256,128]{2,1,0:T(8,128)S(1)}, bf16[2,256,256]{2,1,0:T(8,128)(2,1...) custom-call(s32[16]{0:T(128)} %lengths_hbm.3, s32[8,10]{1,0:T(8,128)} %anc_hbm.1, ...), custom_call_target="tpu_custom_call" | custom-call | flops 500000000 | bytes 6000000 | tf_op jit(solution)/shard_map/pallas_call | solution.py:297
  29.6 0.0 copy-start
  29.6 1.6 %copy-done = f32[2,256,1536]{2,1,0:T(8,128)} copy-done((f32[2,256,1536]{2,1,0:T(8,128)}, f32[2,256,1536]{2,1,0:T(8,128)S(1)}, u32[]{:S(2)}) %copy-start) | copy-done | bytes 3145752
  31.2 7.8 %all-to-all-done.1 = bf16[4,8,32,512]{3,2,1,0:T(8,128)(2,1)S(1)} async-done(((bf16[4,8,32,512]{3,2,1,0:T(8,128)(2,1)}), bf16[4,8,32,512]{3,2,1,0:T(8,128)(2,1)S(1)}, u32[]{:S(2)}, u32[]{:S(2)}) %all-to-all-start.1) | async-done | bytes 1048608 | tf_op jit(solution)/shard_map/all_to_all | solution.py:268
  39.0 0.0 copy-start.1
  39.0 1.9 %copy-done.1 = f32[2,256,1536]{2,1,0:T(8,128)S(1)} copy-done((f32[2,256,1536]{2,1,0:T(8,128)S(1)}, f32[2,256,1536]{2,1,0:T(8,128)}, u32[]{:S(2)}) %copy-start.1) | copy-done | bytes 3145752
  40.9 1.6 %shard_map.58 = s16[16,16,640]{2,1,0:T(8,128)(2,1)S(1)} custom-call(bf16[2,256,256]{2,1,0:T(8,128)(2,1)S(1)} %get-tuple-element.12.query_ref, bf16[32,32,512]{2,1,0:T(8,128)(2,1)S(1)} %bitcast.5, f32[2,256,1536]{2,1,0:T(8,128)S(1)} %copy-done.1, f32[2,256,128]{2,1,0:T(8,128)S(1)} %get-tuple-element.14.max_ref, ...), custom_call_target="tpu_custom_call" | custom-call | tf_op jit(solution)/shard_map/pallas_call | solution.py:321
  42.5 23.9 %all_to_all.16.parts_ref = s16[16,16,640]{2,1,0:T(8,128)(2,1)S(1)} all-to-all(s16[16,16,640]{2,1,0:T(8,128)(2,1)S(1)} %shard_map.58), channel_id=1, replica_groups=mesh['seq'=16,'leaf'=32] {'seq'}, dimensions={0} | all-to-all | bytes 655360 | tf_op jit(solution)/shard_map/all_to_all | solution.py:329
  66.4 1.0 %shard_map.59 = bf16[8,4,256]{2,1,0:T(4,128)(2,1)} custom-call(s16[16,16,640]{2,1,0:T(8,128)(2,1)S(1)} %all_to_all.16.parts_ref), custom_call_target="tpu_custom_call" | custom-call | tf_op jit(solution)/shard_map/pallas_call | solution.py:330
Async XLA Ops:
  0.0 27.0 %copy-start.2 = (bf16[8,4,4096]{2,1,0:T(4,128)(2,1)S(1)}, bf16[8,4,4096]{2,1,0:T(4,128)(2,1)}, u32[]{:S(2)}) copy-start(bf16[8,4,4096]{2,1,0:T(4,128)(2,1)} %param.5) | copy-start | bytes 786436
  22.9 16.1 %all-to-all-start.1 = ((bf16[4,8,32,512]{3,2,1,0:T(8,128)(2,1)}), bf16[4,8,32,512]{3,2,1,0:T(8,128)(2,1)S(1)}, u32[]{:S(2)}, u32[]{:S(2)}) async-start(bf16[4,8,32,512]{3,2,1,0:T(8,128)(2,1)} %shard_map.57), calls=%async_computation.1 | async-start | bytes 2097152 | tf_op jit(solution)/shard_map/all_to_all | solution.py:268
  29.6 1.7 %copy-start = (f32[2,256,1536]{2,1,0:T(8,128)}, f32[2,256,1536]{2,1,0:T(8,128)S(1)}, u32[]{:S(2)}) copy-start(f32[2,256,1536]{2,1,0:T(8,128)S(1)} %get-tuple-element.13.w_ref) | copy-start | bytes 9437188
  39.0 1.9 %copy-start.1 = (f32[2,256,1536]{2,1,0:T(8,128)S(1)}, f32[2,256,1536]{2,1,0:T(8,128)}, u32[]{:S(2)}) copy-start(f32[2,256,1536]{2,1,0:T(8,128)} %copy-done) | copy-start | bytes 9437188

commit v4 on v3

--- a/solution.py
+++ b/solution.py
@@ -76,9 +76,9 @@
         out_ref[copy, tokens : 2 * tokens] = values
 
 
-def copies_kernel(plane_ref, out_ref):
-    for copy in range(out_ref.shape[0]):
-        out_ref[copy] = plane_ref[...]
+def copies_kernel(plane_ref, out_hbm, sems):
+    for copy in fetch([(plane_ref, out_hbm.at[i]) for i in range(out_hbm.shape[0])], sems):
+        copy.wait()
 
 
 def early_kernel(
@@ -88,7 +88,7 @@
     prompt_hbm,
     node_hbm,
     q_ref,
-    w_ref,
+    w_hbm,
     max_ref,
     total_ref,
     query_ref,
@@ -99,7 +99,9 @@
     anc_ref,
     prompt_ref,
     node_ref,
+    w_ref,
     sems,
+    w_sems,
 ):
     copies = fetch(
         [
@@ -151,28 +153,34 @@
         top = None
         for start in range(0, prompt_cols, CHUNK):
             s = dot_nt(query, prompt_ref[start : start + CHUNK, cols])
-            w_ref[k, :, start : start + CHUNK] = s
+            w_ref[k, start // CHUNK] = s
             part = fold(s, jnp.maximum)
             top = part if top is None else jnp.maximum(top, part)
         s = dot_nt(query, node_ref[:, :, cols].reshape(node_cols, HEAD_DIM))
         s = jnp.where(mult > 0.0, s, -jnp.inf)
-        w_ref[k, :, prompt_cols:] = s
+        w_ref[k, prompt_cols // CHUNK] = s
         top = jnp.max(jnp.maximum(top, fold(s, jnp.maximum)), axis=1, keepdims=True)
         total = jnp.zeros((s.shape[0], LANES), jnp.float32)
         for start in range(0, prompt_cols, CHUNK):
-            w = jnp.exp(w_ref[k, :, start : start + CHUNK] - top)
-            w_ref[k, :, start : start + CHUNK] = w
+            w = jnp.exp(w_ref[k, start // CHUNK] - top)
+            w_ref[k, start // CHUNK] = w
             total = total + fold(w, jnp.add)
-        w = jnp.exp(w_ref[k, :, prompt_cols:] - top) * mult
-        w_ref[k, :, prompt_cols:] = w
+        w = jnp.exp(w_ref[k, prompt_cols // CHUNK] - top) * mult
+        w_ref[k, prompt_cols // CHUNK] = w
+        copies += fetch([(w_ref.at[k], w_hbm.at[k])], w_sems.at[pl.ds(k, 1)])
         total = total + fold(w, jnp.add)
         total_ref[k] = jnp.broadcast_to(jnp.sum(total, axis=1, keepdims=True), total.shape)
         max_ref[k] = jnp.broadcast_to(top, total.shape)
-    copies[4].wait()
-    copies[5].wait()
-
-
-def late_kernel(query_ref, shared_ref, w_ref, max_ref, total_ref, count_ref, prompt_ref, node_ref, out_ref):
+    for copy in copies[4:]:
+        copy.wait()
+
+
+def late_kernel(
+    query_ref, shared_ref, w_hbm, max_ref, total_ref, count_ref, prompt_ref, node_ref, out_ref, w_ref, sems
+):
+    chunks = w_ref.shape[1]
+    places = [(k, c) for k in range(KV_HEADS) for c in range(chunks)]
+    copies = fetch([(w_hbm.at[k, c], w_ref.at[k, c]) for k, c in places], sems)
     owners = shared_ref.shape[0]
     tokens = shared_ref.shape[1] // 2
     prompt_cols = prompt_ref.shape[0]
@@ -200,9 +208,11 @@
         acc = jnp.dot(w.astype(jnp.bfloat16), values, preferred_element_type=jnp.float32)
         wide = jnp.concatenate([scale, scale], axis=1)
         for start in range(0, prompt_cols, CHUNK):
-            w = (w_ref[k, :, start : start + CHUNK] * wide).astype(jnp.bfloat16)
+            copies[k * chunks + start // CHUNK].wait()
+            w = (w_ref[k, start // CHUNK] * wide).astype(jnp.bfloat16)
             acc = acc + jnp.dot(w, prompt_ref[start : start + CHUNK, cols], preferred_element_type=jnp.float32)
-        w = (w_ref[k, :, prompt_cols:] * wide).astype(jnp.bfloat16)
+        copies[k * chunks + chunks - 1].wait()
+        w = (w_ref[k, chunks - 1] * wide).astype(jnp.bfloat16)
         node_values = node_ref[:, :, cols].reshape(node_cols, HEAD_DIM)
         acc = acc + jnp.dot(w, node_values, preferred_element_type=jnp.float32)
 
@@ -260,9 +270,10 @@
     plane = lax.all_to_all(own, "leaf", 0, 0, tiled=True, axis_index_groups=along_z)
     plane = pl.pallas_call(
         copies_kernel,
-        out_shape=jax.ShapeDtypeStruct((owners // Z,) + plane.shape, plane.dtype),
+        out_shape=pltpu.HBM((owners // Z,) + plane.shape, plane.dtype),
         in_specs=[VMEM],
-        out_specs=VMEM,
+        out_specs=HBM,
+        scratch_shapes=[pltpu.SemaphoreType.DMA((owners // Z,))],
         compiler_params=params(8),
     )(plane)
     shared = lax.all_to_all(plane, "leaf", 0, 0, tiled=True, axis_index_groups=along_x)
@@ -292,12 +303,13 @@
     shared = gather_shared(own, owners)
 
     query_rows = queries.transpose(1, 0, 2).reshape(rows, feat_width)
-    cols = prompt_cols + node_slots * tokens
+    assert prompt_cols % CHUNK == 0 and node_slots * tokens == CHUNK
+    weights_shape = (KV_HEADS, prompt_cols // CHUNK + 1, GROUP * rows, CHUNK)
     row_shape = jax.ShapeDtypeStruct((KV_HEADS, GROUP * rows, LANES), jnp.float32)
     weights, early_max, early_total, query, count, prompt_values, node_values = pl.pallas_call(
         functools.partial(early_kernel, steps),
         out_shape=(
-            jax.ShapeDtypeStruct((KV_HEADS, GROUP * rows, cols), jnp.float32),
+            pltpu.HBM(weights_shape, jnp.float32),
             row_shape,
             row_shape,
             jax.ShapeDtypeStruct((KV_HEADS, GROUP * rows, HEAD_DIM), jnp.bfloat16),
@@ -306,13 +318,15 @@
             jax.ShapeDtypeStruct((node_slots, tokens, width), jnp.bfloat16),
         ),
         in_specs=[HBM, HBM, HBM, HBM, VMEM],
-        out_specs=(VMEM,) * 7,
+        out_specs=(HBM,) + (VMEM,) * 6,
         scratch_shapes=[
             pltpu.SMEM((node_slots,), jnp.int32),
             pltpu.VMEM(ancestors.shape, jnp.int32),
             pltpu.VMEM((prompt_cols, width), jnp.bfloat16),
             pltpu.VMEM((node_slots, tokens, width), jnp.bfloat16),
+            pltpu.VMEM(weights_shape, jnp.float32),
             pltpu.SemaphoreType.DMA((6,)),
+            pltpu.SemaphoreType.DMA((KV_HEADS,)),
         ],
         compiler_params=params(16),
         cost_estimate=pl.CostEstimate(flops=500_000_000, bytes_accessed=6_000_000, transcendentals=800_000),
@@ -321,10 +335,14 @@
     parts = pl.pallas_call(
         late_kernel,
         out_shape=jax.ShapeDtypeStruct((HEADS, rows // 2, 2 * HEAD_DIM + LANES), jnp.int16),
-        in_specs=[VMEM] * 8,
+        in_specs=[VMEM, VMEM, HBM] + [VMEM] * 5,
         out_specs=VMEM,
+        scratch_shapes=[
+            pltpu.VMEM(weights_shape, jnp.float32),
+            pltpu.SemaphoreType.DMA((weights_shape[0] * weights_shape[1],)),
+        ],
         compiler_params=params(16),
-    )(query, shared, weights, early_max, early_total, count, prompt_values, node_values)
+    )(query, shared, *in_hbm(weights), early_max, early_total, count, prompt_values, node_values)
 
     parts = lax.all_to_all(parts, "seq", 0, 0, tiled=True)
     return pl.pallas_call(

time: 67.7 us -> 67.7 us (level)
  local copies, waits for them, and re-layouts: 3.69 us -> 0.15 us
  Pallas kernels: 6.87 us -> 10.1 us
    unnamed x6 -> x2, local copies, waits for them, and re-layouts: 3.54 us -> 0.01 us
    pallas_call x1, Pallas kernels: 1.55 us -> 3.46 us  [shards(): pl.pallas_call(late_kernel, out_shape=jax.ShapeDtypeStruct((HEADS, rows /...]
    pallas_call x2, Pallas kernels: 3.51 us -> 4.89 us  [the longest x1 3.86 us: shards(): pl.pallas_call(functools.partial(early_kernel, steps), out_shape=(pltpu.H...]
  transfers between devices with their start and end apart: 1 -> 1, of which waited for: 1 -> 1; matrix products, arithmetic and copies ran while one was open for 0% -> 0% of each run, Pallas kernels for 4% -> 6%
where the time goes in v4:
time: 67.7 us; the launch traced here: 67.4 us
  blocking collectives  45 us (66%)
  Pallas kernels  10.1 us (15%)
  waiting for transfers between devices  8.06 us (12%)
  starting transfers between devices  4.02 us (6%)
    all_to_all x1, blocking collectives, shards(): parts = lax.all_to_all(parts, 'seq', 0, 0, tiled=True)  23.9 us
    all_to_all x1, blocking collectives, gather_shared(): lax.all_to_all(own, 'leaf', 0, 0, tiled=True, axis_index_groups=along_z)  21 us
    all_to_all x1, waiting for transfers between devices, gather_shared(): lax.all_to_all(plane, 'leaf', 0, 0, tiled=True, axis_index_groups=along_x)  8.06 us
    all_to_all x1, starting transfers between devices, gather_shared(): lax.all_to_all(plane, 'leaf', 0, 0, tiled=True, axis_index_groups=along_x)  4.02 us
    pallas_call x1, Pallas kernels, shards(): pl.pallas_call(functools.partial(early_kernel, steps), out_shape=(pltpu.H...  3.86 us
    pallas_call x1, Pallas kernels, shards(): pl.pallas_call(late_kernel, out_shape=jax.ShapeDtypeStruct((HEADS, rows /...  3.46 us
  transfers between devices with their start and end apart: 1, of which 1 were waited for; matrix products, arithmetic and copies ran while one was open for 0% of the time, Pallas kernels for 6%

profile of v4, /device:TPU:1, one launch (start us, length us, event | category | flops | bytes accessed | tf_op | source)
XLA Modules:
  0.0 67.4 jit_solution(8357545998912851823)
XLA Ops:
  0.0 0.0 copy-start
  0.0 0.8 %shard_map.56 = bf16[8,32,512]{2,1,0:T(8,128)(2,1)S(1)} custom-call(s32[16]{0:T(128)} %lengths_hbm.3, bf16[2,16,16,512]{3,2,1,0:T(8,128)(2,1)} %node_hbm.3), custom_call_target="tpu_custom_call" | custom-call | tf_op jit(solution)/shard_map/pallas_call | solution.py:291
  0.9 21.0 %all_to_all.15.plane_ref = bf16[8,32,512]{2,1,0:T(8,128)(2,1)S(1)} all-to-all(bf16[8,32,512]{2,1,0:T(8,128)(2,1)S(1)} %shard_map.56), channel_id=1, replica_groups={{0,1,2,3,4,5,6,7},{8,9,10,11,12,13,14,15},{16,17,18,19,20,21,22,23},{24..., dimensions={0} | all-to-all | bytes 524288 | tf_op jit(solution)/shard_map/all_to_all | solution.py:270
  21.9 1.0 %shard_map.57 = bf16[4,8,32,512]{3,2,1,0:T(8,128)(2,1)} custom-call(bf16[8,32,512]{2,1,0:T(8,128)(2,1)S(1)} %all_to_all.15.plane_ref), custom_call_target="tpu_custom_call" | custom-call | tf_op jit(solution)/shard_map/pallas_call | solution.py:271
  22.9 4.0 %all-to-all-start.1 = ((bf16[4,8,32,512]{3,2,1,0:T(8,128)(2,1)}), bf16[4,8,32,512]{3,2,1,0:T(8,128)(2,1)S(1)}, u32[]{:S(2)}, u32[]{:S(2)}) async-start(bf16[4,8,32,512]{3,2,1,0:T(8,128)(2,1)} %shard_map.57), calls=%async_computation.1 | async-start | bytes 2097152 | tf_op jit(solution)/shard_map/all_to_all | solution.py:279
  26.9 0.0 copy-done
  26.9 0.1 copy.8
  27.1 3.9 %shard_map.55 = (f32[2,6,256,256]{3,2,1,0:T(8,128)}, f32[2,256,128]{2,1,0:T(8,128)S(1)}, f32[2,256,128]{2,1,0:T(8,128)S(1)}, bf16[2,256,256]{2,1,0:T(8,128)(2,1)...) custom-call(s32[16]{0:T(128)} %lengths_hbm.3, s32[8,10]{1,0:T(8,128)} %anc_hbm.1, ...), custom_call_target="tpu_custom_call" | custom-call | flops 500000000 | bytes 6000000 | tf_op jit(solution)/shard_map/pallas_call | solution.py:309
  31.0 8.1 %all-to-all-done.1 = bf16[4,8,32,512]{3,2,1,0:T(8,128)(2,1)S(1)} async-done(((bf16[4,8,32,512]{3,2,1,0:T(8,128)(2,1)}), bf16[4,8,32,512]{3,2,1,0:T(8,128)(2,1)S(1)}, u32[]{:S(2)}, u32[]{:S(2)}) %all-to-all-start.1) | async-done | bytes 1048608 | tf_op jit(solution)/shard_map/all_to_all | solution.py:279
  39.0 3.5 %shard_map.58 = s16[16,16,640]{2,1,0:T(8,128)(2,1)S(1)} custom-call(bf16[2,256,256]{2,1,0:T(8,128)(2,1)S(1)} %get-tuple-element.12.query_ref, bf16[32,32,512]{2,1,0:T(8,128)(2,1)S(1)} %bitcast.5, f32[2,6,256,256]{3,2,1,0:T(8,128)} %get-tuple-element.13.w_hbm, f32[2,256,128]{2,1,0:T(8,128)S(1)} %get-tuple-element.14.max_ref, ...), custom_call_target="tpu_custom_call" | custom-call | tf_op jit(solution)/shard_map/pallas_call | solution.py:335
  42.5 23.9 %all_to_all.16.parts_ref = s16[16,16,640]{2,1,0:T(8,128)(2,1)S(1)} all-to-all(s16[16,16,640]{2,1,0:T(8,128)(2,1)S(1)} %shard_map.58), channel_id=1, replica_groups=mesh['seq'=16,'leaf'=32] {'seq'}, dimensions={0} | all-to-all | bytes 655360 | tf_op jit(solution)/shard_map/all_to_all | solution.py:347
  66.4 1.0 %shard_map.59 = bf16[8,4,256]{2,1,0:T(4,128)(2,1)} custom-call(s16[16,16,640]{2,1,0:T(8,128)(2,1)S(1)} %all_to_all.16.parts_ref), custom_call_target="tpu_custom_call" | custom-call | tf_op jit(solution)/shard_map/pallas_call | solution.py:348
Async XLA Ops:
  0.0 26.9 %copy-start = (bf16[8,4,4096]{2,1,0:T(4,128)(2,1)S(1)}, bf16[8,4,4096]{2,1,0:T(4,128)(2,1)}, u32[]{:S(2)}) copy-start(bf16[8,4,4096]{2,1,0:T(4,128)(2,1)} %param.5) | copy-start | bytes 786436
  22.9 16.1 %all-to-all-start.1 = ((bf16[4,8,32,512]{3,2,1,0:T(8,128)(2,1)}), bf16[4,8,32,512]{3,2,1,0:T(8,128)(2,1)S(1)}, u32[]{:S(2)}, u32[]{:S(2)}) async-start(bf16[4,8,32,512]{3,2,1,0:T(8,128)(2,1)} %shard_map.57), calls=%async_computation.1 | async-start | bytes 2097152 | tf_op jit(solution)/shard_map/all_to_all | solution.py:279

commit v5 on v3

--- a/solution.py
+++ b/solution.py
@@ -76,7 +76,8 @@
         out_ref[copy, tokens : 2 * tokens] = values
 
 
-def copies_kernel(plane_ref, out_ref):
+def copies_kernel(plane_ref, early_ref, out_ref):
+    del early_ref
     for copy in range(out_ref.shape[0]):
         out_ref[copy] = plane_ref[...]
 
@@ -254,17 +255,17 @@
             out_ref[:, part * half // leaf_count + i, :] = merged[i * leaf_count : (i + 1) * leaf_count]
 
 
-def gather_shared(own, owners):
+def gather_shared(own, owners, early):
     along_z = [list(range(x, x + Z)) for x in range(0, owners, Z)]
     along_x = [list(range(z, owners, Z)) for z in range(Z)]
     plane = lax.all_to_all(own, "leaf", 0, 0, tiled=True, axis_index_groups=along_z)
     plane = pl.pallas_call(
         copies_kernel,
         out_shape=jax.ShapeDtypeStruct((owners // Z,) + plane.shape, plane.dtype),
-        in_specs=[VMEM],
+        in_specs=[VMEM, VMEM],
         out_specs=VMEM,
         compiler_params=params(8),
-    )(plane)
+    )(plane, early)
     shared = lax.all_to_all(plane, "leaf", 0, 0, tiled=True, axis_index_groups=along_x)
     return shared.reshape((owners,) + own.shape[1:])
 
@@ -289,8 +290,6 @@
         ],
         compiler_params=params(8),
     )(*in_hbm(node_lengths, node_kv))
-    shared = gather_shared(own, owners)
-
     query_rows = queries.transpose(1, 0, 2).reshape(rows, feat_width)
     cols = prompt_cols + node_slots * tokens
     row_shape = jax.ShapeDtypeStruct((KV_HEADS, GROUP * rows, LANES), jnp.float32)
@@ -318,6 +317,7 @@
         cost_estimate=pl.CostEstimate(flops=500_000_000, bytes_accessed=6_000_000, transcendentals=800_000),
     )(*in_hbm(node_lengths, ancestors, prompt_kv, node_kv), query_rows)
 
+    shared = gather_shared(own, owners, count)
     parts = pl.pallas_call(
         late_kernel,
         out_shape=jax.ShapeDtypeStruct((HEADS, rows // 2, 2 * HEAD_DIM + LANES), jnp.int16),

time: 67.7 us -> 65.8 us (0.972)
  starting transfers between devices: 4.01 us -> 10.9 us
  blocking collectives: 45 us -> 40 us
  waiting for transfers between devices: 7.8 us -> 2.88 us
  local copies, waits for them, and re-layouts: 3.69 us -> 5.02 us
    all_to_all x1, starting transfers between devices: 4.01 us -> 10.9 us  [gather_shared(): lax.all_to_all(own, 'leaf', 0, 0, tiled=True, axis_index_groups=along_z)]
    all_to_all x1, blocking collectives: 21 us -> 16 us  [gather_shared(): lax.all_to_all(plane, 'leaf', 0, 0, tiled=True, axis_index_groups=along_x)]
    all_to_all x1, waiting for transfers between devices: 7.8 us -> 2.88 us  [gather_shared(): lax.all_to_all(own, 'leaf', 0, 0, tiled=True, axis_index_groups=along_z)]
    pallas_call x1, Pallas kernels: 1.05 us -> 0.07 us  [gather_shared(): pl.pallas_call(copies_kernel, out_shape=jax.ShapeDtypeStruct((owners // Z...]
    transpose x1, local copies, waits for them, and re-layouts: 0.15 us -> 1.1 us  [shards(): query_rows = queries.transpose(1, 0, 2).reshape(rows, feat_width)]
    pallas_call x1, Pallas kernels: 0.85 us -> 1.54 us  [shards(): pl.pallas_call(post_kernel, out_shape=jax.ShapeDtypeStruct((Z, 2 * tokens...]
    unnamed x6 -> x20, local copies, waits for them, and re-layouts: 3.54 us -> 3.92 us
  transfers between devices with their start and end apart: 1 -> 1, of which waited for: 1 -> 1; matrix products, arithmetic and copies ran while one was open for 0% -> 2% of each run, Pallas kernels for 4% -> 4%
where the time goes in v5:
time: 65.8 us; the launch traced here: 65.4 us
  blocking collectives  40 us (61%)
  starting transfers between devices  10.9 us (17%)
  Pallas kernels  6.57 us (10%)
  local copies, waits for them, and re-layouts  5.02 us (8%)
  waiting for transfers between devices  2.88 us (4%)
    all_to_all x1, blocking collectives, shards(): parts = lax.all_to_all(parts, 'seq', 0, 0, tiled=True)  23.9 us
    all_to_all x1, blocking collectives, gather_shared(): lax.all_to_all(plane, 'leaf', 0, 0, tiled=True, axis_index_groups=along_x)  16 us
    all_to_all x1, starting transfers between devices, gather_shared(): lax.all_to_all(own, 'leaf', 0, 0, tiled=True, axis_index_groups=along_z)  10.9 us
    unnamed x20, local copies, waits for them, and re-layouts  3.92 us
    all_to_all x1, waiting for transfers between devices, gather_shared(): lax.all_to_all(own, 'leaf', 0, 0, tiled=True, axis_index_groups=along_z)  2.88 us
    pallas_call x1, Pallas kernels, shards(): pl.pallas_call(functools.partial(early_kernel, steps), out_shape=(jax.Sha...  2.47 us
    pallas_call x1, Pallas kernels, shards(): pl.pallas_call(post_kernel, out_shape=jax.ShapeDtypeStruct((Z, 2 * tokens...  1.54 us
    pallas_call x1, Pallas kernels, shards(): pl.pallas_call(late_kernel, out_shape=jax.ShapeDtypeStruct((HEADS, rows /...  1.54 us
  transfers between devices with their start and end apart: 1, of which 1 were waited for; matrix products, arithmetic and copies ran while one was open for 2% of the time, Pallas kernels for 4%

profile of v5, /device:TPU:1, one launch (start us, length us, event | category | flops | bytes accessed | tf_op | source)
XLA Modules:
  0.0 65.4 jit_solution(18070163217491859148)
XLA Ops:
  0.0 1.5 %shard_map.56 = bf16[8,32,512]{2,1,0:T(8,128)(2,1)} custom-call(s32[16]{0:T(128)} %lengths_hbm.3, bf16[2,16,16,512]{3,2,1,0:T(8,128)(2,1)} %node_hbm.3), custom_call_target="tpu_custom_call" | custom-call | tf_op jit(solution)/shard_map/pallas_call | solution.py:281
  1.6 10.9 %all-to-all-start = ((bf16[8,32,512]{2,1,0:T(8,128)(2,1)}), bf16[8,32,512]{2,1,0:T(8,128)(2,1)S(1)}, u32[]{:S(2)}, u32[]{:S(2)}) async-start(bf16[8,32,512]{2,1,0:T(8,128)(2,1)} %shard_map.56), calls=%async_computation | async-start | bytes 524288 | tf_op jit(solution)/shard_map/all_to_all | solution.py:261
  12.4 1.1 %copy.8 = bf16[4,8,4096]{2,1,0:T(8,128)(2,1)S(1)} copy(bf16[4,8,4096]{2,0,1:T(4,128)(2,1)} %bitcast.7) | data formatting | bytes 524288 | tf_op jit(solution)/shard_map/transpose | solution.py:293
  13.5 2.5 %shard_map.55 = (f32[2,256,1536]{2,1,0:T(8,128)S(1)}, f32[2,256,128]{2,1,0:T(8,128)S(1)}, f32[2,256,128]{2,1,0:T(8,128)S(1)}, bf16[2,256,256]{2,1,0:T(8,128)(2,1...) custom-call(s32[16]{0:T(128)} %lengths_hbm.3, s32[8,10]{1,0:T(8,128)} %anc_hbm.1, ...), custom_call_target="tpu_custom_call" | custom-call | flops 500000000 | bytes 6000000 | tf_op jit(solution)/shard_map/pallas_call | solution.py:296
  16.0 0.0 copy-start
  16.0 1.1 %copy-done = bf16[1280,512]{1,0:T(8,128)(2,1)} copy-done((bf16[1280,512]{1,0:T(8,128)(2,1)}, bf16[1280,512]{1,0:T(8,128)(2,1)S(1)}, u32[]{:S(2)}) %copy-start) | copy-done | bytes 1310744
  17.1 0.0 copy-start.2
  17.1 0.7 %copy-done.2 = f32[2,256,128]{2,1,0:T(8,128)} copy-done((f32[2,256,128]{2,1,0:T(8,128)}, f32[2,256,128]{2,1,0:T(8,128)S(1)}, u32[]{:S(2)}) %copy-start.2) | copy-done | bytes 262168
  17.8 0.0 copy-start.4
  17.8 0.7 %copy-done.4 = f32[2,256,128]{2,1,0:T(8,128)} copy-done((f32[2,256,128]{2,1,0:T(8,128)}, f32[2,256,128]{2,1,0:T(8,128)S(1)}, u32[]{:S(2)}) %copy-start.4) | copy-done | bytes 262168
  18.5 0.0 copy-start.6
  18.5 0.7 %copy-done.6 = bf16[2,256,256]{2,1,0:T(8,128)(2,1)} copy-done((bf16[2,256,256]{2,1,0:T(8,128)(2,1)}, bf16[2,256,256]{2,1,0:T(8,128)(2,1)S(1)}, u32[]{:S(2)}) %copy-start.6) | copy-done | bytes 262168
  19.2 0.0 copy-start.8
  19.2 0.7 %copy-done.8 = bf16[16,16,512]{2,1,0:T(8,128)(2,1)} copy-done((bf16[16,16,512]{2,1,0:T(8,128)(2,1)}, bf16[16,16,512]{2,1,0:T(8,128)(2,1)S(1)}, u32[]{:S(2)}) %copy-start.8) | copy-done | bytes 262168
  19.9 2.9 %all-to-all-done.plane_ref = bf16[8,32,512]{2,1,0:T(8,128)(2,1)S(1)} async-done(((bf16[8,32,512]{2,1,0:T(8,128)(2,1)}), bf16[8,32,512]{2,1,0:T(8,128)(2,1)S(1)}, u32[]{:S(2)}, u32[]{:S(2)}) %all-to-all-start) | async-done | bytes 262176 | tf_op jit(solution)/shard_map/all_to_all | solution.py:261
  22.8 0.0 copy-start.1
  22.8 0.0 copy-start.3
  22.8 0.0 copy-start.5
  22.8 0.0 copy-start.7
  22.8 0.0 copy-start.9
  22.8 0.1 shard_map.57
  22.9 16.0 %all_to_all.15 = bf16[4,8,32,512]{3,2,1,0:T(8,128)(2,1)S(1)} all-to-all(bf16[4,8,32,512]{3,2,1,0:T(8,128)(2,1)S(1)} %shard_map.57), channel_id=1, replica_groups={{0,8,16,24},{1,9,17,25},{2,10,18,26},{3,11,19,27},{4,12,20,28},{5,13,21..., dimensions={0} | all-to-all | bytes 2097152 | tf_op jit(solution)/shard_map/all_to_all | solution.py:269
  38.9 0.0 copy-done.1
  38.9 0.0 copy-done.3
  38.9 0.0 copy-done.5
  38.9 0.0 copy-done.7
  39.0 0.0 copy-done.9
  39.0 1.5 %shard_map.58 = s16[16,16,640]{2,1,0:T(8,128)(2,1)S(1)} custom-call(bf16[2,256,256]{2,1,0:T(8,128)(2,1)S(1)} %copy-done.7, bf16[32,32,512]{2,1,0:T(8,128)(2,1)S(1)} %bitcast.5, f32[2,256,1536]{2,1,0:T(8,128)S(1)} %get-tuple-element.14.w_ref, f32[2,256,128]{2,1,0:T(8,128)S(1)} %copy-done.3, f32[2,256,128]{2,1,0:T(8,128)S(1)} %copy-done.5, ...), custom_call_target="tpu_custom_call" | custom-call | tf_op jit(solution)/shard_map/pallas_call | solution.py:321
  40.5 23.9 %all_to_all.16.parts_ref = s16[16,16,640]{2,1,0:T(8,128)(2,1)S(1)} all-to-all(s16[16,16,640]{2,1,0:T(8,128)(2,1)S(1)} %shard_map.58), channel_id=1, replica_groups=mesh['seq'=16,'leaf'=32] {'seq'}, dimensions={0} | all-to-all | bytes 655360 | tf_op jit(solution)/shard_map/all_to_all | solution.py:329
  64.5 1.0 %shard_map.59 = bf16[8,4,256]{2,1,0:T(4,128)(2,1)} custom-call(s16[16,16,640]{2,1,0:T(8,128)(2,1)S(1)} %all_to_all.16.parts_ref), custom_call_target="tpu_custom_call" | custom-call | tf_op jit(solution)/shard_map/pallas_call | solution.py:330
Async XLA Ops:
  1.6 21.2 %all-to-all-start = ((bf16[8,32,512]{2,1,0:T(8,128)(2,1)}), bf16[8,32,512]{2,1,0:T(8,128)(2,1)S(1)}, u32[]{:S(2)}, u32[]{:S(2)}) async-start(bf16[8,32,512]{2,1,0:T(8,128)(2,1)} %shard_map.56), calls=%async_computation | async-start | bytes 524288 | tf_op jit(solution)/shard_map/all_to_all | solution.py:261
  16.0 1.1 %copy-start = (bf16[1280,512]{1,0:T(8,128)(2,1)}, bf16[1280,512]{1,0:T(8,128)(2,1)S(1)}, u32[]{:S(2)}) copy-start(bf16[1280,512]{1,0:T(8,128)(2,1)S(1)} %get-tuple-element.17.prompt_ref) | copy-start | bytes 3932164
  17.1 0.7 %copy-start.2 = (f32[2,256,128]{2,1,0:T(8,128)}, f32[2,256,128]{2,1,0:T(8,128)S(1)}, u32[]{:S(2)}) copy-start(f32[2,256,128]{2,1,0:T(8,128)S(1)} %get-tuple-element.15.max_ref) | copy-start | bytes 786436
  17.8 0.7 %copy-start.4 = (f32[2,256,128]{2,1,0:T(8,128)}, f32[2,256,128]{2,1,0:T(8,128)S(1)}, u32[]{:S(2)}) copy-start(f32[2,256,128]{2,1,0:T(8,128)S(1)} %get-tuple-element.16.total_ref) | copy-start | bytes 786436
  18.5 0.7 %copy-start.6 = (bf16[2,256,256]{2,1,0:T(8,128)(2,1)}, bf16[2,256,256]{2,1,0:T(8,128)(2,1)S(1)}, u32[]{:S(2)}) copy-start(bf16[2,256,256]{2,1,0:T(8,128)(2,1)S(1)} %get-tuple-element.12.query_ref) | copy-start | bytes 786436
  19.2 0.7 %copy-start.8 = (bf16[16,16,512]{2,1,0:T(8,128)(2,1)}, bf16[16,16,512]{2,1,0:T(8,128)(2,1)S(1)}, u32[]{:S(2)}) copy-start(bf16[16,16,512]{2,1,0:T(8,128)(2,1)S(1)} %get-tuple-element.18.node_ref) | copy-start | bytes 786436
  22.8 16.1 %copy-start.1 = (bf16[1280,512]{1,0:T(8,128)(2,1)S(1)}, bf16[1280,512]{1,0:T(8,128)(2,1)}, u32[]{:S(2)}) copy-start(bf16[1280,512]{1,0:T(8,128)(2,1)} %copy-done) | copy-start | bytes 3932164
  22.8 16.1 %copy-start.3 = (f32[2,256,128]{2,1,0:T(8,128)S(1)}, f32[2,256,128]{2,1,0:T(8,128)}, u32[]{:S(2)}) copy-start(f32[2,256,128]{2,1,0:T(8,128)} %copy-done.2) | copy-start | bytes 786436
  22.8 16.1 %copy-start.5 = (f32[2,256,128]{2,1,0:T(8,128)S(1)}, f32[2,256,128]{2,1,0:T(8,128)}, u32[]{:S(2)}) copy-start(f32[2,256,128]{2,1,0:T(8,128)} %copy-done.4) | copy-start | bytes 786436
  22.8 16.1 %copy-start.7 = (bf16[2,256,256]{2,1,0:T(8,128)(2,1)S(1)}, bf16[2,256,256]{2,1,0:T(8,128)(2,1)}, u32[]{:S(2)}) copy-start(bf16[2,256,256]{2,1,0:T(8,128)(2,1)} %copy-done.6) | copy-start | bytes 786436
  22.8 16.1 %copy-start.9 = (bf16[16,16,512]{2,1,0:T(8,128)(2,1)S(1)}, bf16[16,16,512]{2,1,0:T(8,128)(2,1)}, u32[]{:S(2)}) copy-start(bf16[16,16,512]{2,1,0:T(8,128)(2,1)} %copy-done.8) | copy-start | bytes 786436

commit v6 on v5

--- a/solution.py
+++ b/solution.py
@@ -89,7 +89,7 @@
     prompt_hbm,
     node_hbm,
     q_ref,
-    w_ref,
+    w_hbm,
     max_ref,
     total_ref,
     query_ref,
@@ -100,7 +100,9 @@
     anc_ref,
     prompt_ref,
     node_ref,
+    w_ref,
     sems,
+    w_sems,
 ):
     copies = fetch(
         [
@@ -152,25 +154,29 @@
         top = None
         for start in range(0, prompt_cols, CHUNK):
             s = dot_nt(query, prompt_ref[start : start + CHUNK, cols])
-            w_ref[k, :, start : start + CHUNK] = s
+            w_ref[k, start // CHUNK] = s
             part = fold(s, jnp.maximum)
             top = part if top is None else jnp.maximum(top, part)
         s = dot_nt(query, node_ref[:, :, cols].reshape(node_cols, HEAD_DIM))
         s = jnp.where(mult > 0.0, s, -jnp.inf)
-        w_ref[k, :, prompt_cols:] = s
+        w_ref[k, prompt_cols // CHUNK] = s
         top = jnp.max(jnp.maximum(top, fold(s, jnp.maximum)), axis=1, keepdims=True)
         total = jnp.zeros((s.shape[0], LANES), jnp.float32)
         for start in range(0, prompt_cols, CHUNK):
-            w = jnp.exp(w_ref[k, :, start : start + CHUNK] - top)
-            w_ref[k, :, start : start + CHUNK] = w
+            c = start // CHUNK
+            w = jnp.exp(w_ref[k, c] - top)
+            w_ref[k, c] = w
+            copies += fetch([(w_ref.at[k, c], w_hbm.at[k, c])], w_sems.at[k, pl.ds(c, 1)])
             total = total + fold(w, jnp.add)
-        w = jnp.exp(w_ref[k, :, prompt_cols:] - top) * mult
-        w_ref[k, :, prompt_cols:] = w
+        c = prompt_cols // CHUNK
+        w = jnp.exp(w_ref[k, c] - top) * mult
+        w_ref[k, c] = w
+        copies += fetch([(w_ref.at[k, c], w_hbm.at[k, c])], w_sems.at[k, pl.ds(c, 1)])
         total = total + fold(w, jnp.add)
         total_ref[k] = jnp.broadcast_to(jnp.sum(total, axis=1, keepdims=True), total.shape)
         max_ref[k] = jnp.broadcast_to(top, total.shape)
-    copies[4].wait()
-    copies[5].wait()
+    for copy in copies[4:]:
+        copy.wait()
 
 
 def late_kernel(query_ref, shared_ref, w_ref, max_ref, total_ref, count_ref, prompt_ref, node_ref, out_ref):
@@ -201,9 +207,9 @@
         acc = jnp.dot(w.astype(jnp.bfloat16), values, preferred_element_type=jnp.float32)
         wide = jnp.concatenate([scale, scale], axis=1)
         for start in range(0, prompt_cols, CHUNK):
-            w = (w_ref[k, :, start : start + CHUNK] * wide).astype(jnp.bfloat16)
+            w = (w_ref[k, start // CHUNK] * wide).astype(jnp.bfloat16)
             acc = acc + jnp.dot(w, prompt_ref[start : start + CHUNK, cols], preferred_element_type=jnp.float32)
-        w = (w_ref[k, :, prompt_cols:] * wide).astype(jnp.bfloat16)
+        w = (w_ref[k, prompt_cols // CHUNK] * wide).astype(jnp.bfloat16)
         node_values = node_ref[:, :, cols].reshape(node_cols, HEAD_DIM)
         acc = acc + jnp.dot(w, node_values, preferred_element_type=jnp.float32)
 
@@ -291,12 +297,13 @@
         compiler_params=params(8),
     )(*in_hbm(node_lengths, node_kv))
     query_rows = queries.transpose(1, 0, 2).reshape(rows, feat_width)
-    cols = prompt_cols + node_slots * tokens
+    assert prompt_cols % CHUNK == 0 and node_slots * tokens == CHUNK
+    weights_shape = (KV_HEADS, prompt_cols // CHUNK + 1, GROUP * rows, CHUNK)
     row_shape = jax.ShapeDtypeStruct((KV_HEADS, GROUP * rows, LANES), jnp.float32)
     weights, early_max, early_total, query, count, prompt_values, node_values = pl.pallas_call(
         functools.partial(early_kernel, steps),
         out_shape=(
-            jax.ShapeDtypeStruct((KV_HEADS, GROUP * rows, cols), jnp.float32),
+            pltpu.HBM(weights_shape, jnp.float32),
             row_shape,
             row_shape,
             jax.ShapeDtypeStruct((KV_HEADS, GROUP * rows, HEAD_DIM), jnp.bfloat16),
@@ -305,13 +312,15 @@
             jax.ShapeDtypeStruct((node_slots, tokens, width), jnp.bfloat16),
         ),
         in_specs=[HBM, HBM, HBM, HBM, VMEM],
-        out_specs=(VMEM,) * 7,
+        out_specs=(HBM,) + (VMEM,) * 6,
         scratch_shapes=[
             pltpu.SMEM((node_slots,), jnp.int32),
             pltpu.VMEM(ancestors.shape, jnp.int32),
             pltpu.VMEM((prompt_cols, width), jnp.bfloat16),
             pltpu.VMEM((node_slots, tokens, width), jnp.bfloat16),
+            pltpu.VMEM(weights_shape, jnp.float32),
             pltpu.SemaphoreType.DMA((6,)),
+            pltpu.SemaphoreType.DMA(weights_shape[:2]),
         ],
         compiler_params=params(16),
         cost_estimate=pl.CostEstimate(flops=500_000_000, bytes_accessed=6_000_000, transcendentals=800_000),

time: 65.8 us -> 69.9 us (1.062)
  local copies, waits for them, and re-layouts: 5.02 us -> 9.16 us
  Pallas kernels: 6.57 us -> 8.01 us
  waiting for transfers between devices: 2.88 us -> 1.45 us
    unnamed x20 -> x22, local copies, waits for them, and re-layouts: 3.92 us -> 8.06 us
    pallas_call x1, Pallas kernels: 2.47 us -> 3.9 us  [shards(): pl.pallas_call(functools.partial(early_kernel, steps), out_shape=(pltpu.H...]
    all_to_all x1, waiting for transfers between devices: 2.88 us -> 1.45 us  [gather_shared(): lax.all_to_all(own, 'leaf', 0, 0, tiled=True, axis_index_groups=along_z)]
  transfers between devices with their start and end apart: 1 -> 1, of which waited for: 1 -> 1; matrix products, arithmetic and copies ran while one was open for 2% -> 2% of each run, Pallas kernels for 4% -> 6%
where the time goes in v6:
time: 69.9 us; the launch traced here: 69.4 us
  blocking collectives  39.8 us (57%)
  starting transfers between devices  10.9 us (16%)
  local copies, waits for them, and re-layouts  9.16 us (13%)
  Pallas kernels  8.01 us (11%)
  waiting for transfers between devices  1.45 us (2%)
    all_to_all x1, blocking collectives, shards(): parts = lax.all_to_all(parts, 'seq', 0, 0, tiled=True)  23.9 us
    all_to_all x1, blocking collectives, gather_shared(): lax.all_to_all(plane, 'leaf', 0, 0, tiled=True, axis_index_groups=along_x)  15.9 us
    all_to_all x1, starting transfers between devices, gather_shared(): lax.all_to_all(own, 'leaf', 0, 0, tiled=True, axis_index_groups=along_z)  10.9 us
    unnamed x22, local copies, waits for them, and re-layouts  8.06 us
    pallas_call x1, Pallas kernels, shards(): pl.pallas_call(functools.partial(early_kernel, steps), out_shape=(pltpu.H...  3.9 us
    pallas_call x1, Pallas kernels, shards(): pl.pallas_call(post_kernel, out_shape=jax.ShapeDtypeStruct((Z, 2 * tokens...  1.54 us
    pallas_call x1, Pallas kernels, shards(): pl.pallas_call(late_kernel, out_shape=jax.ShapeDtypeStruct((HEADS, rows /...  1.54 us
    all_to_all x1, waiting for transfers between devices, gather_shared(): lax.all_to_all(own, 'leaf', 0, 0, tiled=True, axis_index_groups=along_z)  1.45 us
  transfers between devices with their start and end apart: 1, of which 1 were waited for; matrix products, arithmetic and copies ran while one was open for 2% of the time, Pallas kernels for 6%

profile of v6, /device:TPU:1, one launch (start us, length us, event | category | flops | bytes accessed | tf_op | source)
XLA Modules:
  0.0 69.4 jit_solution(987281392267738686)
XLA Ops:
  0.0 1.5 %shard_map.56 = bf16[8,32,512]{2,1,0:T(8,128)(2,1)} custom-call(s32[16]{0:T(128)} %lengths_hbm.3, bf16[2,16,16,512]{3,2,1,0:T(8,128)(2,1)} %node_hbm.3), custom_call_target="tpu_custom_call" | custom-call | tf_op jit(solution)/shard_map/pallas_call | solution.py:287
  1.6 10.9 %all-to-all-start = ((bf16[8,32,512]{2,1,0:T(8,128)(2,1)}), bf16[8,32,512]{2,1,0:T(8,128)(2,1)S(1)}, u32[]{:S(2)}, u32[]{:S(2)}) async-start(bf16[8,32,512]{2,1,0:T(8,128)(2,1)} %shard_map.56), calls=%async_computation | async-start | bytes 524288 | tf_op jit(solution)/shard_map/all_to_all | solution.py:267
  12.4 1.1 %copy.8 = bf16[4,8,4096]{2,1,0:T(8,128)(2,1)S(1)} copy(bf16[4,8,4096]{2,0,1:T(4,128)(2,1)} %bitcast.7) | data formatting | bytes 524288 | tf_op jit(solution)/shard_map/transpose | solution.py:299
  13.5 3.9 %shard_map.55 = (f32[2,6,256,256]{3,2,1,0:T(8,128)}, f32[2,256,128]{2,1,0:T(8,128)S(1)}, f32[2,256,128]{2,1,0:T(8,128)S(1)}, bf16[2,256,256]{2,1,0:T(8,128)(2,1)...) custom-call(s32[16]{0:T(128)} %lengths_hbm.3, s32[8,10]{1,0:T(8,128)} %anc_hbm.1, ...), custom_call_target="tpu_custom_call" | custom-call | flops 500000000 | bytes 6000000 | tf_op jit(solution)/shard_map/pallas_call | solution.py:303
  17.4 0.0 copy-start.1
  17.5 1.1 %copy-done.1 = bf16[1280,512]{1,0:T(8,128)(2,1)} copy-done((bf16[1280,512]{1,0:T(8,128)(2,1)}, bf16[1280,512]{1,0:T(8,128)(2,1)S(1)}, u32[]{:S(2)}) %copy-start.1) | copy-done | bytes 1310744
  18.5 0.0 copy-start.3
  18.5 0.7 %copy-done.3 = f32[2,256,128]{2,1,0:T(8,128)} copy-done((f32[2,256,128]{2,1,0:T(8,128)}, f32[2,256,128]{2,1,0:T(8,128)S(1)}, u32[]{:S(2)}) %copy-start.3) | copy-done | bytes 262168
  19.2 0.0 copy-start.5
  19.2 0.7 %copy-done.5 = f32[2,256,128]{2,1,0:T(8,128)} copy-done((f32[2,256,128]{2,1,0:T(8,128)}, f32[2,256,128]{2,1,0:T(8,128)S(1)}, u32[]{:S(2)}) %copy-start.5) | copy-done | bytes 262168
  19.9 0.0 copy-start.7
  19.9 0.7 %copy-done.7 = bf16[2,256,256]{2,1,0:T(8,128)(2,1)} copy-done((bf16[2,256,256]{2,1,0:T(8,128)(2,1)}, bf16[2,256,256]{2,1,0:T(8,128)(2,1)S(1)}, u32[]{:S(2)}) %copy-start.7) | copy-done | bytes 262168
  20.6 0.0 copy-start.9
  20.6 0.7 %copy-done.9 = bf16[16,16,512]{2,1,0:T(8,128)(2,1)} copy-done((bf16[16,16,512]{2,1,0:T(8,128)(2,1)}, bf16[16,16,512]{2,1,0:T(8,128)(2,1)S(1)}, u32[]{:S(2)}) %copy-start.9) | copy-done | bytes 262168
  21.3 0.0 copy-start
  21.3 1.5 %all-to-all-done.plane_ref = bf16[8,32,512]{2,1,0:T(8,128)(2,1)S(1)} async-done(((bf16[8,32,512]{2,1,0:T(8,128)(2,1)}), bf16[8,32,512]{2,1,0:T(8,128)(2,1)S(1)}, u32[]{:S(2)}, u32[]{:S(2)}) %all-to-all-start) | async-done | bytes 262176 | tf_op jit(solution)/shard_map/all_to_all | solution.py:267
  22.8 0.0 copy-start.4
  22.8 0.1 shard_map.57
  22.9 15.9 %all_to_all.15 = bf16[4,8,32,512]{3,2,1,0:T(8,128)(2,1)S(1)} all-to-all(bf16[4,8,32,512]{3,2,1,0:T(8,128)(2,1)S(1)} %shard_map.57), channel_id=1, replica_groups={{0,8,16,24},{1,9,17,25},{2,10,18,26},{3,11,19,27},{4,12,20,28},{5,13,21..., dimensions={0} | all-to-all | bytes 2097152 | tf_op jit(solution)/shard_map/all_to_all | solution.py:275
  38.8 0.0 copy-done
  38.8 0.0 copy-done.4
  38.8 0.0 copy-start.2
  38.8 1.3 %copy-done.2 = bf16[1280,512]{1,0:T(8,128)(2,1)S(1)} copy-done((bf16[1280,512]{1,0:T(8,128)(2,1)S(1)}, bf16[1280,512]{1,0:T(8,128)(2,1)}, u32[]{:S(2)}) %copy-start.2) | copy-done | bytes 1310744
  40.1 0.0 copy-start.6
  40.1 0.9 %copy-done.6 = f32[2,256,128]{2,1,0:T(8,128)S(1)} copy-done((f32[2,256,128]{2,1,0:T(8,128)S(1)}, f32[2,256,128]{2,1,0:T(8,128)}, u32[]{:S(2)}) %copy-start.6) | copy-done | bytes 262168
  41.1 0.0 copy-start.8
  41.1 0.9 %copy-done.8 = bf16[2,256,256]{2,1,0:T(8,128)(2,1)S(1)} copy-done((bf16[2,256,256]{2,1,0:T(8,128)(2,1)S(1)}, bf16[2,256,256]{2,1,0:T(8,128)(2,1)}, u32[]{:S(2)}) %copy-start.8) | copy-done | bytes 262168
  42.0 0.0 copy-start.10
  42.0 0.9 %copy-done.10 = bf16[16,16,512]{2,1,0:T(8,128)(2,1)S(1)} copy-done((bf16[16,16,512]{2,1,0:T(8,128)(2,1)S(1)}, bf16[16,16,512]{2,1,0:T(8,128)(2,1)}, u32[]{:S(2)}) %copy-start.10) | copy-done | bytes 262168
  43.0 1.5 %shard_map.58 = s16[16,16,640]{2,1,0:T(8,128)(2,1)S(1)} custom-call(bf16[2,256,256]{2,1,0:T(8,128)(2,1)S(1)} %copy-done.8, bf16[32,32,512]{2,1,0:T(8,128)(2,1)S(1)} %bitcast.5, f32[2,6,256,256]{3,2,1,0:T(8,128)S(1)} %copy-done, f32[2,256,128]{2,1,0:T(8,128)S(1)} %copy-done.4, f32[2,256,128]{2,1,0:T(8,128)S(1)} %copy-done.6, ...), custom_call_target="tpu_custom_call" | custom-call | tf_op jit(solution)/shard_map/pallas_call | solution.py:330
  44.5 23.9 %all_to_all.16.parts_ref = s16[16,16,640]{2,1,0:T(8,128)(2,1)S(1)} all-to-all(s16[16,16,640]{2,1,0:T(8,128)(2,1)S(1)} %shard_map.58), channel_id=1, replica_groups=mesh['seq'=16,'leaf'=32] {'seq'}, dimensions={0} | all-to-all | bytes 655360 | tf_op jit(solution)/shard_map/all_to_all | solution.py:338
  68.4 1.0 %shard_map.59 = bf16[8,4,256]{2,1,0:T(4,128)(2,1)} custom-call(s16[16,16,640]{2,1,0:T(8,128)(2,1)S(1)} %all_to_all.16.parts_ref), custom_call_target="tpu_custom_call" | custom-call | tf_op jit(solution)/shard_map/pallas_call | solution.py:339
Async XLA Ops:
  1.6 21.2 %all-to-all-start = ((bf16[8,32,512]{2,1,0:T(8,128)(2,1)}), bf16[8,32,512]{2,1,0:T(8,128)(2,1)S(1)}, u32[]{:S(2)}, u32[]{:S(2)}) async-start(bf16[8,32,512]{2,1,0:T(8,128)(2,1)} %shard_map.56), calls=%async_computation | async-start | bytes 524288 | tf_op jit(solution)/shard_map/all_to_all | solution.py:267
  17.4 1.1 %copy-start.1 = (bf16[1280,512]{1,0:T(8,128)(2,1)}, bf16[1280,512]{1,0:T(8,128)(2,1)S(1)}, u32[]{:S(2)}) copy-start(bf16[1280,512]{1,0:T(8,128)(2,1)S(1)} %get-tuple-element.17.prompt_ref) | copy-start | bytes 3932164
  18.5 0.7 %copy-start.3 = (f32[2,256,128]{2,1,0:T(8,128)}, f32[2,256,128]{2,1,0:T(8,128)S(1)}, u32[]{:S(2)}) copy-start(f32[2,256,128]{2,1,0:T(8,128)S(1)} %get-tuple-element.15.max_ref) | copy-start | bytes 786436
  19.2 0.7 %copy-start.5 = (f32[2,256,128]{2,1,0:T(8,128)}, f32[2,256,128]{2,1,0:T(8,128)S(1)}, u32[]{:S(2)}) copy-start(f32[2,256,128]{2,1,0:T(8,128)S(1)} %get-tuple-element.16.total_ref) | copy-start | bytes 786436
  19.9 0.7 %copy-start.7 = (bf16[2,256,256]{2,1,0:T(8,128)(2,1)}, bf16[2,256,256]{2,1,0:T(8,128)(2,1)S(1)}, u32[]{:S(2)}) copy-start(bf16[2,256,256]{2,1,0:T(8,128)(2,1)S(1)} %get-tuple-element.12.query_ref) | copy-start | bytes 786436
  20.6 0.7 %copy-start.9 = (bf16[16,16,512]{2,1,0:T(8,128)(2,1)}, bf16[16,16,512]{2,1,0:T(8,128)(2,1)S(1)}, u32[]{:S(2)}) copy-start(bf16[16,16,512]{2,1,0:T(8,128)(2,1)S(1)} %get-tuple-element.18.node_ref) | copy-start | bytes 786436
  21.3 17.4 %copy-start = (f32[2,6,256,256]{3,2,1,0:T(8,128)S(1)}, f32[2,6,256,256]{3,2,1,0:T(8,128)}, u32[]{:S(2)}) copy-start(f32[2,6,256,256]{3,2,1,0:T(8,128)} %get-tuple-element.14.w_ref) | copy-start | bytes 9437188
  22.8 16.0 %copy-start.4 = (f32[2,256,128]{2,1,0:T(8,128)S(1)}, f32[2,256,128]{2,1,0:T(8,128)}, u32[]{:S(2)}) copy-start(f32[2,256,128]{2,1,0:T(8,128)} %copy-done.3) | copy-start | bytes 786436
  38.8 1.3 %copy-start.2 = (bf16[1280,512]{1,0:T(8,128)(2,1)S(1)}, bf16[1280,512]{1,0:T(8,128)(2,1)}, u32[]{:S(2)}) copy-start(bf16[1280,512]{1,0:T(8,128)(2,1)} %copy-done.1) | copy-start | bytes 3932164
  40.1 0.9 %copy-start.6 = (f32[2,256,128]{2,1,0:T(8,128)S(1)}, f32[2,256,128]{2,1,0:T(8,128)}, u32[]{:S(2)}) copy-start(f32[2,256,128]{2,1,0:T(8,128)} %copy-done.5) | copy-start | bytes 786436
  41.1 0.9 %copy-start.8 = (bf16[2,256,256]{2,1,0:T(8,128)(2,1)S(1)}, bf16[2,256,256]{2,1,0:T(8,128)(2,1)}, u32[]{:S(2)}) copy-start(bf16[2,256,256]{2,1,0:T(8,128)(2,1)} %copy-done.7) | copy-start | bytes 786436
  42.0 0.9 %copy-start.10 = (bf16[16,16,512]{2,1,0:T(8,128)(2,1)S(1)}, bf16[16,16,512]{2,1,0:T(8,128)(2,1)}, u32[]{:S(2)}) copy-start(bf16[16,16,512]{2,1,0:T(8,128)(2,1)} %copy-done.9) | copy-start | bytes 786436

commit v7 on v5

--- a/solution.py
+++ b/solution.py
@@ -173,7 +173,7 @@
     copies[5].wait()
 
 
-def late_kernel(query_ref, shared_ref, w_ref, max_ref, total_ref, count_ref, prompt_ref, node_ref, out_ref):
+def late_kernel(query_ref, shared_ref, w_ref, max_ref, total_ref, count_ref, prompt_ref, node_ref, own_ref, out_ref):
     owners = shared_ref.shape[0]
     tokens = shared_ref.shape[1] // 2
     prompt_cols = prompt_ref.shape[0]
@@ -207,26 +207,69 @@
         node_values = node_ref[:, :, cols].reshape(node_cols, HEAD_DIM)
         acc = acc + jnp.dot(w, node_values, preferred_element_type=jnp.float32)
 
-        reach = jnp.maximum(jnp.max(fold(jnp.abs(acc), jnp.maximum), axis=1, keepdims=True), 1e-30)
-        data = jnp.round(acc * (TOP / reach)).astype(jnp.int32).astype(jnp.int16)
-        fixed = [
-            jnp.round(value * point).astype(jnp.int32)
-            for value, point in zip((block_max, jnp.log(total), jnp.log(reach)), POINTS)
-        ]
-        lane = lax.broadcasted_iota(jnp.int32, (GROUP * rows, LANES), 1)
-        stats = jnp.zeros((GROUP * rows, LANES), jnp.int32)
-        for i, value in enumerate(fixed):
-            stats = jnp.where(lane == 2 * i, value >> 16, stats)
-            stats = jnp.where(lane == 2 * i + 1, (value & 0xFFFF) - 0x8000, stats)
-        lane = lane[:half]
-        for h in range(GROUP):
-            first = h * rows
-            for part in range(2):
-                lanes = slice(part * HEAD_DIM, (part + 1) * HEAD_DIM)
-                out_ref[k * GROUP + h, :, lanes] = data[first + part * half : first + (part + 1) * half]
-            low, high = stats[first : first + half], stats[first + half : first + rows]
-            both = jnp.where(lane < LANES // 2, low, pltpu.roll(high, LANES // 2, 1))
-            out_ref[k * GROUP + h, :, 2 * HEAD_DIM :] = both.astype(jnp.int16)
+        core = lax.rem(lax.axis_index("seq"), 2)
+        total = jnp.broadcast_to(total, block_max.shape)
+        for pair in range(GROUP // 2):
+            kept, sent = [], []
+            for x in (acc, block_max, total):
+                even = x[2 * pair * rows : (2 * pair + 1) * rows]
+                odd = x[(2 * pair + 1) * rows : (2 * pair + 2) * rows]
+                kept.append(jnp.where(core == 0, even, odd))
+                sent.append(jnp.where(core == 0, odd, even))
+            slot = k * (GROUP // 2) + pair
+            lane = lax.broadcasted_iota(jnp.int32, (half, LANES), 1)
+            stats = [jnp.where(lane % (LANES // 2) == 0, kept[1][i : i + half], kept[2][i : i + half]) for i in (0, half)]
+            own_ref[slot, :, 2 * HEAD_DIM :] = jnp.where(lane < LANES // 2, stats[0], stats[1])
+            own_ref[slot, :, 0:HEAD_DIM] = kept[0][:half]
+            own_ref[slot, :, HEAD_DIM : 2 * HEAD_DIM] = kept[0][half:]
+            data, fixed = to_wire(*sent)
+            out_ref[slot, :, 0:HEAD_DIM] = data[:half]
+            out_ref[slot, :, HEAD_DIM : 2 * HEAD_DIM] = data[half:]
+            out_ref[slot, :, 2 * HEAD_DIM :] = jnp.where(lane < LANES // 2, fixed[:half], fixed[half:]).astype(jnp.int16)
+
+
+def to_wire(acc, block_max, total):
+    reach = jnp.maximum(jnp.max(fold(jnp.abs(acc), jnp.maximum), axis=1, keepdims=True), 1e-30)
+    data = jnp.round(acc * (TOP / reach)).astype(jnp.int32).astype(jnp.int16)
+    lane = lax.broadcasted_iota(jnp.int32, block_max.shape, 1) % (LANES // 2)
+    log_total = jnp.log(total) * POINTS[1]
+    log_reach = jnp.log(reach) * POINTS[2]
+    value = jnp.where(lane < 2, block_max * POINTS[0], jnp.where(lane < 4, log_total, log_reach))
+    value = jnp.round(value).astype(jnp.int32)
+    return data, jnp.where(lane % 2 == 0, value >> 16, (value & 0xFFFF) - 0x8000)
+
+
+def from_wire(stats, first, i):
+    high = stats[:, first + 2 * i : first + 2 * i + 1]
+    low = stats[:, first + 2 * i + 1 : first + 2 * i + 2] + 0x8000
+    return ((high << 16) + low).astype(jnp.float32) * (1.0 / POINTS[i])
+
+
+def pair_kernel(own_ref, other_ref, out_ref):
+    slots, half, lanes = own_ref.shape
+    rows = slots * half
+    own_stats = own_ref[:, :, 2 * HEAD_DIM :].reshape(rows, LANES)
+    other_stats = other_ref[:, :, 2 * HEAD_DIM :].reshape(rows, LANES).astype(jnp.int32)
+    fixed = []
+    for part in range(2):
+        first = part * LANES // 2
+        span = slice(part * HEAD_DIM, (part + 1) * HEAD_DIM)
+        own_max, own_total = own_stats[:, first : first + 1], own_stats[:, first + 1 : first + 2]
+        other_max = from_wire(other_stats, first, 0)
+        top = jnp.maximum(own_max, other_max)
+        own_scale = jnp.exp(own_max - top)
+        shift = other_max - top
+        total = own_total * own_scale + jnp.exp(shift + from_wire(other_stats, first, 1))
+        other = other_ref[:, :, span].reshape(rows, HEAD_DIM).astype(jnp.int32).astype(jnp.float32)
+        acc = own_ref[:, :, span].reshape(rows, HEAD_DIM) * own_scale
+        acc = acc + other * (jnp.exp(shift + from_wire(other_stats, first, 2)) * (1.0 / TOP))
+        shape = (rows, LANES)
+        data, stats = to_wire(acc, jnp.broadcast_to(top, shape), jnp.broadcast_to(total, shape))
+        out_ref[:, :, span] = data.reshape(slots, half, HEAD_DIM)
+        fixed.append(stats)
+    lane = lax.broadcasted_iota(jnp.int32, (rows, LANES), 1)
+    stats = jnp.where(lane < LANES // 2, fixed[0], fixed[1]).astype(jnp.int16)
+    out_ref[:, :, 2 * HEAD_DIM :] = stats.reshape(slots, half, LANES)
 
 
 def merge_kernel(parts_ref, out_ref):
@@ -235,21 +278,15 @@
     stats = [parts_ref[b, :, 2 * HEAD_DIM :].astype(jnp.int32) for b in range(blocks)]
     for part in range(2):
         first = part * LANES // 2
-
-        def value(b, i):
-            high = stats[b][:, first + 2 * i : first + 2 * i + 1]
-            low = stats[b][:, first + 2 * i + 1 : first + 2 * i + 2] + 0x8000
-            return ((high << 16) + low).astype(jnp.float32) * (1.0 / POINTS[i])
-
-        tops = [value(b, 0) for b in range(blocks)]
+        tops = [from_wire(stats[b], first, 0) for b in range(blocks)]
         row_max = functools.reduce(jnp.maximum, tops)
         denominator = jnp.zeros((half, 1), jnp.float32)
         numerator = jnp.zeros((half, HEAD_DIM), jnp.float32)
         for b in range(blocks):
             shift = tops[b] - row_max
-            denominator = denominator + jnp.exp(shift + value(b, 1))
+            denominator = denominator + jnp.exp(shift + from_wire(stats[b], first, 1))
             data = parts_ref[b, :, part * HEAD_DIM : (part + 1) * HEAD_DIM].astype(jnp.int32).astype(jnp.float32)
-            numerator = numerator + jnp.exp(shift + value(b, 2)) * data
+            numerator = numerator + jnp.exp(shift + from_wire(stats[b], first, 2)) * data
         merged = (numerator / (denominator * TOP)).astype(jnp.bfloat16)
         for i in range(half // leaf_count):
             out_ref[:, part * half // leaf_count + i, :] = merged[i * leaf_count : (i + 1) * leaf_count]
@@ -318,15 +355,26 @@
     )(*in_hbm(node_lengths, ancestors, prompt_kv, node_kv), query_rows)
 
     shared = gather_shared(own, owners, count)
-    parts = pl.pallas_call(
+    seqs = lax.axis_size("seq")
+    wire = jax.ShapeDtypeStruct((HEADS // 2, rows // 2, 2 * HEAD_DIM + LANES), jnp.int16)
+    kept, sent = pl.pallas_call(
         late_kernel,
-        out_shape=jax.ShapeDtypeStruct((HEADS, rows // 2, 2 * HEAD_DIM + LANES), jnp.int16),
+        out_shape=(jax.ShapeDtypeStruct(wire.shape, jnp.float32), wire),
         in_specs=[VMEM] * 8,
-        out_specs=VMEM,
+        out_specs=(VMEM, VMEM),
         compiler_params=params(16),
     )(query, shared, weights, early_max, early_total, count, prompt_values, node_values)
 
-    parts = lax.all_to_all(parts, "seq", 0, 0, tiled=True)
+    got = lax.ppermute(sent, "seq", [(i, i ^ 1) for i in range(seqs)])
+    parts = pl.pallas_call(
+        pair_kernel,
+        out_shape=wire,
+        in_specs=[VMEM, VMEM],
+        out_specs=VMEM,
+        compiler_params=params(8),
+    )(kept, got)
+    chips = [list(range(c, seqs, 2)) for c in range(2)]
+    parts = lax.all_to_all(parts, "seq", 0, 0, tiled=True, axis_index_groups=chips)
     return pl.pallas_call(
         merge_kernel,
         out_shape=jax.ShapeDtypeStruct((leaf_count, steps, HEAD_DIM), jnp.bfloat16),

time: 65.8 us -> 64.4 us (0.979)
  blocking collectives: 40 us -> 31.3 us
  starting transfers between devices: 10.9 us -> 16.7 us
  waiting for transfers between devices: 2.88 us -> 3.87 us
    all_to_all x1, blocking collectives: 23.9 us -> 15.2 us  [shards(): lax.all_to_all(parts, 'seq', 0, 0, tiled=True, axis_index_groups=chips)]
    ppermute x0 -> x1, starting transfers between devices: none -> 5.87 us  [shards(): got = lax.ppermute(sent, 'seq', [(i, i ^ 1) for i in range(seqs)])]
    ppermute x0 -> x1, waiting for transfers between devices: none -> 1.01 us  [shards(): got = lax.ppermute(sent, 'seq', [(i, i ^ 1) for i in range(seqs)])]
    pallas_call x1 -> x2, Pallas kernels: 1.54 us -> 1.93 us  [the longest x1 1.42 us: shards(): pl.pallas_call(late_kernel, out_shape=(jax.ShapeDtypeStruct(wire.shape, j...]
  transfers between devices with their start and end apart: 1 -> 2, of which waited for: 1 -> 2; matrix products, arithmetic and copies ran while one was open for 2% -> 2% of each run, Pallas kernels for 4% -> 4%
where the time goes in v7:
time: 64.4 us; the launch traced here: 63.9 us
  blocking collectives  31.3 us (49%)
  starting transfers between devices  16.7 us (26%)
  Pallas kernels  6.92 us (11%)
  local copies, waits for them, and re-layouts  5.03 us (8%)
  waiting for transfers between devices  3.87 us (6%)
    all_to_all x1, blocking collectives, gather_shared(): lax.all_to_all(plane, 'leaf', 0, 0, tiled=True, axis_index_groups=along_x)  16 us
    all_to_all x1, blocking collectives, shards(): lax.all_to_all(parts, 'seq', 0, 0, tiled=True, axis_index_groups=chips)  15.2 us
    all_to_all x1, starting transfers between devices, gather_shared(): lax.all_to_all(own, 'leaf', 0, 0, tiled=True, axis_index_groups=along_z)  10.9 us
    ppermute x1, starting transfers between devices, shards(): got = lax.ppermute(sent, 'seq', [(i, i ^ 1) for i in range(seqs)])  5.87 us
    unnamed x20, local copies, waits for them, and re-layouts  3.93 us
    all_to_all x1, waiting for transfers between devices, gather_shared(): lax.all_to_all(own, 'leaf', 0, 0, tiled=True, axis_index_groups=along_z)  2.87 us
    pallas_call x1, Pallas kernels, shards(): pl.pallas_call(functools.partial(early_kernel, steps), out_shape=(jax.Sha...  2.47 us
    pallas_call x1, Pallas kernels, shards(): pl.pallas_call(post_kernel, out_shape=jax.ShapeDtypeStruct((Z, 2 * tokens...  1.55 us
  transfers between devices with their start and end apart: 2, of which 2 were waited for; matrix products, arithmetic and copies ran while one was open for 2% of the time, Pallas kernels for 4%

profile of v7, /device:TPU:1, one launch (start us, length us, event | category | flops | bytes accessed | tf_op | source)
XLA Modules:
  0.0 63.9 jit_solution(18074495962956527559)
XLA Ops:
  0.0 1.5 %shard_map.56 = bf16[8,32,512]{2,1,0:T(8,128)(2,1)} custom-call(s32[16]{0:T(128)} %lengths_hbm.3, bf16[2,16,16,512]{3,2,1,0:T(8,128)(2,1)} %node_hbm.3), custom_call_target="tpu_custom_call" | custom-call | tf_op jit(solution)/shard_map/pallas_call | solution.py:318
  1.6 10.9 %all-to-all-start = ((bf16[8,32,512]{2,1,0:T(8,128)(2,1)}), bf16[8,32,512]{2,1,0:T(8,128)(2,1)S(1)}, u32[]{:S(2)}, u32[]{:S(2)}) async-start(bf16[8,32,512]{2,1,0:T(8,128)(2,1)} %shard_map.56), calls=%async_computation | async-start | bytes 524288 | tf_op jit(solution)/shard_map/all_to_all | solution.py:298
  12.4 1.1 %copy.8 = bf16[4,8,4096]{2,1,0:T(8,128)(2,1)S(1)} copy(bf16[4,8,4096]{2,0,1:T(4,128)(2,1)} %bitcast.7) | data formatting | bytes 524288 | tf_op jit(solution)/shard_map/transpose | solution.py:330
  13.5 2.5 %shard_map.55 = (f32[2,256,1536]{2,1,0:T(8,128)S(1)}, f32[2,256,128]{2,1,0:T(8,128)S(1)}, f32[2,256,128]{2,1,0:T(8,128)S(1)}, bf16[2,256,256]{2,1,0:T(8,128)(2,1...) custom-call(s32[16]{0:T(128)} %lengths_hbm.3, s32[8,10]{1,0:T(8,128)} %anc_hbm.1, ...), custom_call_target="tpu_custom_call" | custom-call | flops 500000000 | bytes 6000000 | tf_op jit(solution)/shard_map/pallas_call | solution.py:333
  16.0 0.0 copy-start
  16.0 1.1 %copy-done = bf16[1280,512]{1,0:T(8,128)(2,1)} copy-done((bf16[1280,512]{1,0:T(8,128)(2,1)}, bf16[1280,512]{1,0:T(8,128)(2,1)S(1)}, u32[]{:S(2)}) %copy-start) | copy-done | bytes 1310744
  17.1 0.0 copy-start.2
  17.1 0.7 %copy-done.2 = f32[2,256,128]{2,1,0:T(8,128)} copy-done((f32[2,256,128]{2,1,0:T(8,128)}, f32[2,256,128]{2,1,0:T(8,128)S(1)}, u32[]{:S(2)}) %copy-start.2) | copy-done | bytes 262168
  17.8 0.0 copy-start.4
  17.8 0.7 %copy-done.4 = f32[2,256,128]{2,1,0:T(8,128)} copy-done((f32[2,256,128]{2,1,0:T(8,128)}, f32[2,256,128]{2,1,0:T(8,128)S(1)}, u32[]{:S(2)}) %copy-start.4) | copy-done | bytes 262168
  18.5 0.0 copy-start.6
  18.5 0.7 %copy-done.6 = bf16[2,256,256]{2,1,0:T(8,128)(2,1)} copy-done((bf16[2,256,256]{2,1,0:T(8,128)(2,1)}, bf16[2,256,256]{2,1,0:T(8,128)(2,1)S(1)}, u32[]{:S(2)}) %copy-start.6) | copy-done | bytes 262168
  19.2 0.0 copy-start.8
  19.2 0.7 %copy-done.8 = bf16[16,16,512]{2,1,0:T(8,128)(2,1)} copy-done((bf16[16,16,512]{2,1,0:T(8,128)(2,1)}, bf16[16,16,512]{2,1,0:T(8,128)(2,1)S(1)}, u32[]{:S(2)}) %copy-start.8) | copy-done | bytes 262168
  19.9 2.9 %all-to-all-done.plane_ref = bf16[8,32,512]{2,1,0:T(8,128)(2,1)S(1)} async-done(((bf16[8,32,512]{2,1,0:T(8,128)(2,1)}), bf16[8,32,512]{2,1,0:T(8,128)(2,1)S(1)}, u32[]{:S(2)}, u32[]{:S(2)}) %all-to-all-start) | async-done | bytes 262176 | tf_op jit(solution)/shard_map/all_to_all | solution.py:298
  22.8 0.0 copy-start.1
  22.8 0.0 copy-start.3
  22.8 0.0 copy-start.5
  22.8 0.0 copy-start.7
  22.8 0.0 copy-start.9
  22.8 0.1 shard_map.57
  22.9 16.0 %all_to_all.15 = bf16[4,8,32,512]{3,2,1,0:T(8,128)(2,1)S(1)} all-to-all(bf16[4,8,32,512]{3,2,1,0:T(8,128)(2,1)S(1)} %shard_map.57), channel_id=1, replica_groups={{0,8,16,24},{1,9,17,25},{2,10,18,26},{3,11,19,27},{4,12,20,28},{5,13,21..., dimensions={0} | all-to-all | bytes 2097152 | tf_op jit(solution)/shard_map/all_to_all | solution.py:306
  38.9 0.0 copy-done.1
  38.9 0.0 copy-done.3
  38.9 0.0 copy-done.5
  39.0 0.0 copy-done.7
  39.0 0.0 copy-done.9
  39.0 1.4 %shard_map.58 = (f32[8,16,640]{2,1,0:T(8,128)S(1)}, s16[8,16,640]{2,1,0:T(8,128)(2,1)S(1)}) custom-call(bf16[2,256,256]{2,1,0:T(8,128)(2,1)S(1)} %copy-done.7, bf16[32,32,512]{2,1,0:T(8,128)(2,1)S(1)} %bitcast.5, f32[2,256,1536]{2,1,0:T(8,128)S(1)} %get-tuple-element.16.w_ref, f32[2,256,128]{2,1,0:T(8,128)S(1)} %copy-done.3, f32[2,256,128]{2,1,0:T(8,128)S(1)} %copy-done.5, ...), custom_call_target="tpu_custom_call" | custom-call | tf_op jit(solution)/shard_map/pallas_call | solution.py:360
  40.4 5.9 %collective-permute-start = (s16[8,16,640]{2,1,0:T(8,128)(2,1)S(1)}, s16[8,16,640]{2,1,0:T(8,128)(2,1)S(1)}, u32[]{:S(2)}, u32[]{:S(2)}) collective-permute-start(s16[8,16,640]{2,1,0:T(8,128)(2,1)S(1)} %get-tuple-element.22), channel_id=1, source_target_pairs={{0,32},{32,0},{64,96},{96,64},{128,160},{160,128},{192,224},{224,1... | collective-permute-start | bytes 491528 | tf_op jit(solution)/shard_map/ppermute | solution.py:368
  46.3 1.0 %collective-permute-done.other_ref = s16[8,16,640]{2,1,0:T(8,128)(2,1)S(1)} collective-permute-done((s16[8,16,640]{2,1,0:T(8,128)(2,1)S(1)}, s16[8,16,640]{2,1,0:T(8,128)(2,1)S(1)}, u32[]{:S(2)}, u32[]{:S(2)}) %collective-permute-start) | collective-permute-done | bytes 163872 | tf_op jit(solution)/shard_map/ppermute | solution.py:368
  47.3 0.5 shard_map.59
  47.8 15.2 %all_to_all.16.parts_ref = s16[8,16,640]{2,1,0:T(8,128)(2,1)S(1)} all-to-all(s16[8,16,640]{2,1,0:T(8,128)(2,1)S(1)} %shard_map.59), channel_id=1, replica_groups={{0,64,128,192,256,320,384,448},{32,96,160,224,288,352,416,480},{1,65,12..., dimensions={0} | all-to-all | bytes 327680 | tf_op jit(solution)/shard_map/all_to_all | solution.py:377
  63.0 0.9 %shard_map.60 = bf16[8,4,256]{2,1,0:T(4,128)(2,1)} custom-call(s16[8,16,640]{2,1,0:T(8,128)(2,1)S(1)} %all_to_all.16.parts_ref), custom_call_target="tpu_custom_call" | custom-call | tf_op jit(solution)/shard_map/pallas_call | solution.py:378
Async XLA Ops:
  1.6 21.2 %all-to-all-start = ((bf16[8,32,512]{2,1,0:T(8,128)(2,1)}), bf16[8,32,512]{2,1,0:T(8,128)(2,1)S(1)}, u32[]{:S(2)}, u32[]{:S(2)}) async-start(bf16[8,32,512]{2,1,0:T(8,128)(2,1)} %shard_map.56), calls=%async_computation | async-start | bytes 524288 | tf_op jit(solution)/shard_map/all_to_all | solution.py:298
  16.0 1.1 %copy-start = (bf16[1280,512]{1,0:T(8,128)(2,1)}, bf16[1280,512]{1,0:T(8,128)(2,1)S(1)}, u32[]{:S(2)}) copy-start(bf16[1280,512]{1,0:T(8,128)(2,1)S(1)} %get-tuple-element.19.prompt_ref) | copy-start | bytes 3932164
  17.1 0.7 %copy-start.2 = (f32[2,256,128]{2,1,0:T(8,128)}, f32[2,256,128]{2,1,0:T(8,128)S(1)}, u32[]{:S(2)}) copy-start(f32[2,256,128]{2,1,0:T(8,128)S(1)} %get-tuple-element.17.max_ref) | copy-start | bytes 786436
  17.8 0.7 %copy-start.4 = (f32[2,256,128]{2,1,0:T(8,128)}, f32[2,256,128]{2,1,0:T(8,128)S(1)}, u32[]{:S(2)}) copy-start(f32[2,256,128]{2,1,0:T(8,128)S(1)} %get-tuple-element.18.total_ref) | copy-start | bytes 786436
  18.5 0.7 %copy-start.6 = (bf16[2,256,256]{2,1,0:T(8,128)(2,1)}, bf16[2,256,256]{2,1,0:T(8,128)(2,1)S(1)}, u32[]{:S(2)}) copy-start(bf16[2,256,256]{2,1,0:T(8,128)(2,1)S(1)} %get-tuple-element.14.query_ref) | copy-start | bytes 786436
  19.2 0.7 %copy-start.8 = (bf16[16,16,512]{2,1,0:T(8,128)(2,1)}, bf16[16,16,512]{2,1,0:T(8,128)(2,1)S(1)}, u32[]{:S(2)}) copy-start(bf16[16,16,512]{2,1,0:T(8,128)(2,1)S(1)} %get-tuple-element.20.node_ref) | copy-start | bytes 786436
  22.8 16.1 %copy-start.1 = (bf16[1280,512]{1,0:T(8,128)(2,1)S(1)}, bf16[1280,512]{1,0:T(8,128)(2,1)}, u32[]{:S(2)}) copy-start(bf16[1280,512]{1,0:T(8,128)(2,1)} %copy-done) | copy-start | bytes 3932164
  22.8 16.1 %copy-start.3 = (f32[2,256,128]{2,1,0:T(8,128)S(1)}, f32[2,256,128]{2,1,0:T(8,128)}, u32[]{:S(2)}) copy-start(f32[2,256,128]{2,1,0:T(8,128)} %copy-done.2) | copy-start | bytes 786436
  22.8 16.1 %copy-start.5 = (f32[2,256,128]{2,1,0:T(8,128)S(1)}, f32[2,256,128]{2,1,0:T(8,128)}, u32[]{:S(2)}) copy-start(f32[2,256,128]{2,1,0:T(8,128)} %copy-done.4) | copy-start | bytes 786436
  22.8 16.1 %copy-start.7 = (bf16[2,256,256]{2,1,0:T(8,128)(2,1)S(1)}, bf16[2,256,256]{2,1,0:T(8,128)(2,1)}, u32[]{:S(2)}) copy-start(bf16[2,256,256]{2,1,0:T(8,128)(2,1)} %copy-done.6) | copy-start | bytes 786436
  22.8 16.1 %copy-start.9 = (bf16[16,16,512]{2,1,0:T(8,128)(2,1)S(1)}, bf16[16,16,512]{2,1,0:T(8,128)(2,1)}, u32[]{:S(2)}) copy-start(bf16[16,16,512]{2,1,0:T(8,128)(2,1)} %copy-done.8) | copy-start | bytes 786436
  40.4 6.9 %collective-permute-start = (s16[8,16,640]{2,1,0:T(8,128)(2,1)S(1)}, s16[8,16,640]{2,1,0:T(8,128)(2,1)S(1)}, u32[]{:S(2)}, u32[]{:S(2)}) collective-permute-start(s16[8,16,640]{2,1,0:T(8,128)(2,1)S(1)} %get-tuple-element.22), channel_id=1, source_target_pairs={{0,32},{32,0},{64,96},{96,64},{128,160},{160,128},{192,224},{224,1... | collective-permute-start | bytes 491528 | tf_op jit(solution)/shard_map/ppermute | solution.py:368

commit v8 on v7

--- a/solution.py
+++ b/solution.py
@@ -74,12 +74,6 @@
     for copy in range(out_ref.shape[0]):
         out_ref[copy, 0:tokens] = keys
         out_ref[copy, tokens : 2 * tokens] = values
-
-
-def copies_kernel(plane_ref, early_ref, out_ref):
-    del early_ref
-    for copy in range(out_ref.shape[0]):
-        out_ref[copy] = plane_ref[...]
 
 
 def early_kernel(
@@ -118,6 +112,7 @@
     node_cols = node_slots * tokens
     prompt_cols = prompt_ref.shape[0]
     shared_cols = count_ref.shape[1]
+    planes = shared_cols // (tokens * Z)
     for k in range(KV_HEADS):
         query_ref[k] = group_query(q_ref, k)
     copies[0].wait()
@@ -125,9 +120,11 @@
     anc = anc_ref[...]
 
     lane = lax.broadcasted_iota(jnp.int32, (1, shared_cols), 1)
-    owner = lane // tokens
+    device = lax.axis_index("leaf")
+    plane, along_z = lane // (tokens * Z), lane // tokens % Z
+    owner = lax.rem(device // Z - plane + planes, planes) * Z + along_z
     count = node_counts(anc, owner * node_slots + node_slots - 1, range(level_count - 1))
-    count_ref[...] = jnp.where(owner == lax.axis_index("leaf"), 0.0, count)
+    count_ref[...] = jnp.where(owner == device, 0.0, count)
 
     lane = lax.broadcasted_iota(jnp.int32, (1, node_cols), 1)
     slot = lane // tokens
@@ -173,22 +170,28 @@
     copies[5].wait()
 
 
-def late_kernel(query_ref, shared_ref, w_ref, max_ref, total_ref, count_ref, prompt_ref, node_ref, own_ref, out_ref):
-    owners = shared_ref.shape[0]
-    tokens = shared_ref.shape[1] // 2
+def late_kernel(planes, *refs):
+    shared_refs = refs[:planes]
+    query_ref, w_ref, max_ref, total_ref, count_ref, prompt_ref, node_ref, own_ref, out_ref = refs[planes:]
+    tokens = shared_refs[0].shape[1] // 2
     prompt_cols = prompt_ref.shape[0]
     node_cols = node_ref.shape[0] * node_ref.shape[1]
-    shared_cols = owners * tokens
     rows = query_ref.shape[1] // GROUP
     half = rows // 2
+
+    def shared_rows(first, cols):
+        return jnp.concatenate(
+            [ref[:, first : first + tokens, cols].reshape(Z * tokens, HEAD_DIM) for ref in shared_refs], axis=0
+        )
+
     count = count_ref[...]
     reps = GROUP * rows // count.shape[0]
     pick = jnp.where(lax.broadcasted_iota(jnp.int32, (8, HEAD_DIM), 1) == 0, 1.0, 0.0).astype(jnp.bfloat16)
 
     for k in range(KV_HEADS):
         cols = slice(k * HEAD_DIM, (k + 1) * HEAD_DIM)
-        keys = shared_ref[:, 0:tokens, cols].reshape(shared_cols, HEAD_DIM)
-        values = shared_ref[:, tokens : 2 * tokens, cols].reshape(shared_cols, HEAD_DIM)
+        keys = shared_rows(0, cols)
+        values = shared_rows(tokens, cols)
         marks = dot_nt(pick, keys)[0:1]
         mult = tall(jnp.where(marks < INVALID_KEY / 2, count, 0.0), reps)
         s = dot_nt(query_ref[k], keys)
@@ -292,19 +295,14 @@
             out_ref[:, part * half // leaf_count + i, :] = merged[i * leaf_count : (i + 1) * leaf_count]
 
 
-def gather_shared(own, owners, early):
+def gather_shared(own, owners):
     along_z = [list(range(x, x + Z)) for x in range(0, owners, Z)]
-    along_x = [list(range(z, owners, Z)) for z in range(Z)]
     plane = lax.all_to_all(own, "leaf", 0, 0, tiled=True, axis_index_groups=along_z)
-    plane = pl.pallas_call(
-        copies_kernel,
-        out_shape=jax.ShapeDtypeStruct((owners // Z,) + plane.shape, plane.dtype),
-        in_specs=[VMEM, VMEM],
-        out_specs=VMEM,
-        compiler_params=params(8),
-    )(plane, early)
-    shared = lax.all_to_all(plane, "leaf", 0, 0, tiled=True, axis_index_groups=along_x)
-    return shared.reshape((owners,) + own.shape[1:])
+    planes = owners // Z
+    got = {0: plane}
+    for k in sorted(range(1, planes), key=lambda k: (min(k, planes - k), k)):
+        got[k] = lax.ppermute(plane, "leaf", [(i, (i + k * Z) % owners) for i in range(owners)])
+    return [got[k] for k in range(planes)]
 
 
 def shards(queries, prompt_kv, node_kv, node_lengths, ancestors):
@@ -354,16 +352,16 @@
         cost_estimate=pl.CostEstimate(flops=500_000_000, bytes_accessed=6_000_000, transcendentals=800_000),
     )(*in_hbm(node_lengths, ancestors, prompt_kv, node_kv), query_rows)
 
-    shared = gather_shared(own, owners, count)
+    shared = gather_shared(own, owners)
     seqs = lax.axis_size("seq")
     wire = jax.ShapeDtypeStruct((HEADS // 2, rows // 2, 2 * HEAD_DIM + LANES), jnp.int16)
     kept, sent = pl.pallas_call(
-        late_kernel,
+        functools.partial(late_kernel, len(shared)),
         out_shape=(jax.ShapeDtypeStruct(wire.shape, jnp.float32), wire),
-        in_specs=[VMEM] * 8,
+        in_specs=[VMEM] * (len(shared) + 7),
         out_specs=(VMEM, VMEM),
         compiler_params=params(16),
-    )(query, shared, weights, early_max, early_total, count, prompt_values, node_values)
+    )(*shared, query, weights, early_max, early_total, count, prompt_values, node_values)
 
     got = lax.ppermute(sent, "seq", [(i, i ^ 1) for i in range(seqs)])
     parts = pl.pallas_call(

time: 64.4 us -> 65.4 us (1.016)
  blocking collectives: 31.3 us -> 36.3 us
  waiting for transfers between devices: 3.87 us -> 8.1 us
  local copies, waits for them, and re-layouts: 5.03 us -> 1.1 us
  starting transfers between devices: 16.7 us -> 13.3 us
  Pallas kernels: 6.92 us -> 6.13 us
    all_to_all x1 -> x0, starting transfers between devices: 10.9 us -> none  [gather_shared(): lax.all_to_all(own, 'leaf', 0, 0, tiled=True, axis_index_groups=along_z)]
    ppermute x0 -> x3, starting transfers between devices: none -> 9.32 us  [gather_shared(): lax.ppermute(plane, 'leaf', [(i, (i + k * Z) % owners) for i in range(own...]
    ppermute x0 -> x3, waiting for transfers between devices: none -> 7.09 us  [gather_shared(): lax.ppermute(plane, 'leaf', [(i, (i + k * Z) % owners) for i in range(own...]
    all_to_all x1, blocking collectives: 16 us -> 21 us  [gather_shared(): lax.all_to_all(own, 'leaf', 0, 0, tiled=True, axis_index_groups=along_z)]
    unnamed x20 -> x0, local copies, waits for them, and re-layouts: 3.93 us -> none
    all_to_all x1 -> x0, waiting for transfers between devices: 2.87 us -> none  [gather_shared(): lax.all_to_all(own, 'leaf', 0, 0, tiled=True, axis_index_groups=along_z)]
    ppermute x1, starting transfers between devices: 5.87 us -> 4.02 us  [shards(): got = lax.ppermute(sent, 'seq', [(i, i ^ 1) for i in range(seqs)])]
    pallas_call x1, Pallas kernels: 1.55 us -> 0.83 us  [shards(): pl.pallas_call(post_kernel, out_shape=jax.ShapeDtypeStruct((Z, 2 * tokens...]
  transfers between devices with their start and end apart: 2 -> 4, of which waited for: 2 -> 3; matrix products, arithmetic and copies ran while one was open for 2% -> 2% of each run, Pallas kernels for 4% -> 4%
where the time goes in v8:
time: 65.4 us; the launch traced here: 65 us
  blocking collectives  36.3 us (56%)
  starting transfers between devices  13.3 us (20%)
  waiting for transfers between devices  8.1 us (12%)
  Pallas kernels  6.13 us (9%)
  local copies, waits for them, and re-layouts  1.1 us (2%)
    all_to_all x1, blocking collectives, gather_shared(): lax.all_to_all(own, 'leaf', 0, 0, tiled=True, axis_index_groups=along_z)  21 us
    all_to_all x1, blocking collectives, shards(): lax.all_to_all(parts, 'seq', 0, 0, tiled=True, axis_index_groups=chips)  15.2 us
    ppermute x3, starting transfers between devices, gather_shared(): lax.ppermute(plane, 'leaf', [(i, (i + k * Z) % owners) for i in range(own...  9.32 us
    ppermute x3, waiting for transfers between devices, gather_shared(): lax.ppermute(plane, 'leaf', [(i, (i + k * Z) % owners) for i in range(own...  7.09 us
    ppermute x1, starting transfers between devices, shards(): got = lax.ppermute(sent, 'seq', [(i, i ^ 1) for i in range(seqs)])  4.02 us
    pallas_call x1, Pallas kernels, shards(): pl.pallas_call(functools.partial(early_kernel, steps), out_shape=(jax.Sha...  2.47 us
    pallas_call x1, Pallas kernels, shards(): pl.pallas_call(functools.partial(late_kernel, len(shared)), out_shape=(ja...  1.41 us
  transfers between devices with their start and end apart: 4, of which 3 were waited for; matrix products, arithmetic and copies ran while one was open for 2% of the time, Pallas kernels for 4%

profile of v8, /device:TPU:1, one launch (start us, length us, event | category | flops | bytes accessed | tf_op | source)
XLA Modules:
  0.0 65.0 jit_solution(9435619064319177774)
XLA Ops:
  0.0 0.8 %shard_map.55 = bf16[8,32,512]{2,1,0:T(8,128)(2,1)S(1)} custom-call(s32[16]{0:T(128)} %lengths_hbm.3, bf16[2,16,16,512]{3,2,1,0:T(8,128)(2,1)} %node_hbm.3), custom_call_target="tpu_custom_call" | custom-call | tf_op jit(solution)/shard_map/pallas_call | solution.py:316
  0.8 21.0 %all_to_all.10.refs_0_ = bf16[8,32,512]{2,1,0:T(8,128)(2,1)S(1)} all-to-all(bf16[8,32,512]{2,1,0:T(8,128)(2,1)S(1)} %shard_map.55), channel_id=1, replica_groups={{0,1,2,3,4,5,6,7},{8,9,10,11,12,13,14,15},{16,17,18,19,20,21,22,23},{24..., dimensions={0} | all-to-all | bytes 524288 | tf_op jit(solution)/shard_map/all_to_all | solution.py:300
  21.9 4.4 %collective-permute-start.2 = (bf16[8,32,512]{2,1,0:T(8,128)(2,1)S(1)}, bf16[8,32,512]{2,1,0:T(8,128)(2,1)S(1)}, u32[]{:S(2)}, u32[]{:S(2)}) collective-permute-start(bf16[8,32,512]{2,1,0:T(8,128)(2,1)S(1)} %all_to_all.10.refs_0_), channel_id=1, source_target_pairs={{0,24},{1,25},{2,26},{3,27},{4,28},{5,29},{6,30},{7,31},{8,0},{9,1... | collective-permute-start | bytes 786440 | tf_op jit(solution)/shard_map/ppermute | solution.py:304
  26.3 2.4 %collective-permute-start.1 = (bf16[8,32,512]{2,1,0:T(8,128)(2,1)S(1)}, bf16[8,32,512]{2,1,0:T(8,128)(2,1)S(1)}, u32[]{:S(2)}, u32[]{:S(2)}) collective-permute-start(bf16[8,32,512]{2,1,0:T(8,128)(2,1)S(1)} %all_to_all.10.refs_0_), channel_id=1, source_target_pairs={{0,16},{1,17},{2,18},{3,19},{4,20},{5,21},{6,22},{7,23},{8,24},{9,... | collective-permute-start | bytes 786440 | tf_op jit(solution)/shard_map/ppermute | solution.py:304
  28.7 2.5 %collective-permute-start = (bf16[8,32,512]{2,1,0:T(8,128)(2,1)S(1)}, bf16[8,32,512]{2,1,0:T(8,128)(2,1)S(1)}, u32[]{:S(2)}, u32[]{:S(2)}) collective-permute-start(bf16[8,32,512]{2,1,0:T(8,128)(2,1)S(1)} %all_to_all.10.refs_0_), channel_id=1, source_target_pairs={{0,8},{1,9},{2,10},{3,11},{4,12},{5,13},{6,14},{7,15},{8,16},{9,17... | collective-permute-start | bytes 786440 | tf_op jit(solution)/shard_map/ppermute | solution.py:304
  31.2 1.1 %copy.8 = bf16[4,8,4096]{2,1,0:T(8,128)(2,1)S(1)} copy(bf16[4,8,4096]{2,0,1:T(4,128)(2,1)} %bitcast.5) | data formatting | bytes 524288 | tf_op jit(solution)/shard_map/transpose | solution.py:328
  32.3 2.5 %shard_map.56 = (f32[2,256,1536]{2,1,0:T(8,128)S(1)}, f32[2,256,128]{2,1,0:T(8,128)S(1)}, f32[2,256,128]{2,1,0:T(8,128)S(1)}, bf16[2,256,256]{2,1,0:T(8,128)(2,1...) custom-call(s32[16]{0:T(128)} %lengths_hbm.3, s32[8,10]{1,0:T(8,128)} %anc_hbm.1, ...), custom_call_target="tpu_custom_call" | custom-call | flops 500000000 | bytes 6000000 | tf_op jit(solution)/shard_map/pallas_call | solution.py:331
  34.8 0.0 collective-permute-done.2.refs_3_
  34.8 0.1 collective-permute-done.1.refs_2_
  35.0 6.9 %collective-permute-done.refs_1_ = bf16[8,32,512]{2,1,0:T(8,128)(2,1)S(1)} collective-permute-done((bf16[8,32,512]{2,1,0:T(8,128)(2,1)S(1)}, bf16[8,32,512]{2,1,0:T(8,128)(2,1)S(1)}, u32[]{:S(2)}, u32[]{:S(2)}) %collective-permute-start) | collective-permute-done | bytes 262176 | tf_op jit(solution)/shard_map/ppermute | solution.py:304
  41.9 1.4 %shard_map.57 = (f32[8,16,640]{2,1,0:T(8,128)S(1)}, s16[8,16,640]{2,1,0:T(8,128)(2,1)S(1)}) custom-call(bf16[8,32,512]{2,1,0:T(8,128)(2,1)S(1)} %all_to_all.10.refs_0_, bf16[8,32,512]{2,1,0:T(8,128)(2,1)S(1)} %collective-permute-done.refs_1_, bf16[8,32,512]{2,1,0:T(8,128)(2,1)S(1)} %collective-permute-done.1.refs_2_, ...), custom_call_target="tpu_custom_call" | custom-call | tf_op jit(solution)/shard_map/pallas_call | solution.py:358
  43.3 4.0 %collective-permute-start.3 = (s16[8,16,640]{2,1,0:T(8,128)(2,1)S(1)}, s16[8,16,640]{2,1,0:T(8,128)(2,1)S(1)}, u32[]{:S(2)}, u32[]{:S(2)}) collective-permute-start(s16[8,16,640]{2,1,0:T(8,128)(2,1)S(1)} %get-tuple-element.22), channel_id=1, source_target_pairs={{0,32},{32,0},{64,96},{96,64},{128,160},{160,128},{192,224},{224,1... | collective-permute-start | bytes 491528 | tf_op jit(solution)/shard_map/ppermute | solution.py:366
  47.3 1.0 %collective-permute-done.3.other_ref = s16[8,16,640]{2,1,0:T(8,128)(2,1)S(1)} collective-permute-done((s16[8,16,640]{2,1,0:T(8,128)(2,1)S(1)}, s16[8,16,640]{2,1,0:T(8,128)(2,1)S(1)}, u32[]{:S(2)}, u32[]{:S(2)}) %collective-permute-start.3) | collective-permute-done | bytes 163872 | tf_op jit(solution)/shard_map/ppermute | solution.py:366
  48.3 0.5 shard_map.58
  48.9 15.2 %all_to_all.11.parts_ref = s16[8,16,640]{2,1,0:T(8,128)(2,1)S(1)} all-to-all(s16[8,16,640]{2,1,0:T(8,128)(2,1)S(1)} %shard_map.58), channel_id=1, replica_groups={{0,64,128,192,256,320,384,448},{32,96,160,224,288,352,416,480},{1,65,12..., dimensions={0} | all-to-all | bytes 327680 | tf_op jit(solution)/shard_map/all_to_all | solution.py:375
  64.1 0.9 %shard_map.59 = bf16[8,4,256]{2,1,0:T(4,128)(2,1)} custom-call(s16[8,16,640]{2,1,0:T(8,128)(2,1)S(1)} %all_to_all.11.parts_ref), custom_call_target="tpu_custom_call" | custom-call | tf_op jit(solution)/shard_map/pallas_call | solution.py:376
Async XLA Ops:
  21.9 12.9 %collective-permute-start.2 = (bf16[8,32,512]{2,1,0:T(8,128)(2,1)S(1)}, bf16[8,32,512]{2,1,0:T(8,128)(2,1)S(1)}, u32[]{:S(2)}, u32[]{:S(2)}) collective-permute-start(bf16[8,32,512]{2,1,0:T(8,128)(2,1)S(1)} %all_to_all.10.refs_0_), channel_id=1, source_target_pairs={{0,24},{1,25},{2,26},{3,27},{4,28},{5,29},{6,30},{7,31},{8,0},{9,1... | collective-permute-start | bytes 786440 | tf_op jit(solution)/shard_map/ppermute | solution.py:304
  26.3 8.7 %collective-permute-start.1 = (bf16[8,32,512]{2,1,0:T(8,128)(2,1)S(1)}, bf16[8,32,512]{2,1,0:T(8,128)(2,1)S(1)}, u32[]{:S(2)}, u32[]{:S(2)}) collective-permute-start(bf16[8,32,512]{2,1,0:T(8,128)(2,1)S(1)} %all_to_all.10.refs_0_), channel_id=1, source_target_pairs={{0,16},{1,17},{2,18},{3,19},{4,20},{5,21},{6,22},{7,23},{8,24},{9,... | collective-permute-start | bytes 786440 | tf_op jit(solution)/shard_map/ppermute | solution.py:304
  28.7 13.2 %collective-permute-start = (bf16[8,32,512]{2,1,0:T(8,128)(2,1)S(1)}, bf16[8,32,512]{2,1,0:T(8,128)(2,1)S(1)}, u32[]{:S(2)}, u32[]{:S(2)}) collective-permute-start(bf16[8,32,512]{2,1,0:T(8,128)(2,1)S(1)} %all_to_all.10.refs_0_), channel_id=1, source_target_pairs={{0,8},{1,9},{2,10},{3,11},{4,12},{5,13},{6,14},{7,15},{8,16},{9,17... | collective-permute-start | bytes 786440 | tf_op jit(solution)/shard_map/ppermute | solution.py:304
  43.3 5.0 %collective-permute-start.3 = (s16[8,16,640]{2,1,0:T(8,128)(2,1)S(1)}, s16[8,16,640]{2,1,0:T(8,128)(2,1)S(1)}, u32[]{:S(2)}, u32[]{:S(2)}) collective-permute-start(s16[8,16,640]{2,1,0:T(8,128)(2,1)S(1)} %get-tuple-element.22), channel_id=1, source_target_pairs={{0,32},{32,0},{64,96},{96,64},{128,160},{160,128},{192,224},{224,1... | collective-permute-start | bytes 491528 | tf_op jit(solution)/shard_map/ppermute | solution.py:366

commit v9 on v7

--- a/solution.py
+++ b/solution.py
@@ -14,6 +14,7 @@
 CHUNK = 256
 LANES = 128
 Z = 8
+STRIDE = 2
 INVALID_KEY = 256.0
 TOP = 32767.0
 POINTS = (2.0**18, 2.0**26, 2.0**23)
@@ -90,12 +91,8 @@
     node_hbm,
     q_ref,
     w_ref,
-    max_ref,
-    total_ref,
-    query_ref,
+    half_ref,
     count_ref,
-    prompt_values_ref,
-    node_values_ref,
     lengths_ref,
     anc_ref,
     prompt_ref,
@@ -108,8 +105,11 @@
             (anc_hbm, anc_ref),
             (node_hbm.at[0], node_ref),
             (prompt_hbm.at[0], prompt_ref),
-            (node_hbm.at[1], node_values_ref),
-            (prompt_hbm.at[1], prompt_values_ref),
+            (prompt_hbm.at[1], half_ref.at[pl.ds(0, prompt_ref.shape[0])]),
+        ]
+        + [
+            (node_hbm.at[1, n], half_ref.at[pl.ds(prompt_ref.shape[0] + n * node_ref.shape[1], node_ref.shape[1])])
+            for n in range(node_ref.shape[0])
         ],
         sems,
     )
@@ -119,13 +119,14 @@
     prompt_cols = prompt_ref.shape[0]
     shared_cols = count_ref.shape[1]
     for k in range(KV_HEADS):
-        query_ref[k] = group_query(q_ref, k)
+        half_ref[prompt_cols + node_cols :, k * HEAD_DIM : (k + 1) * HEAD_DIM] = group_query(q_ref, k)
     copies[0].wait()
     copies[1].wait()
     anc = anc_ref[...]
 
     lane = lax.broadcasted_iota(jnp.int32, (1, shared_cols), 1)
-    owner = lane // tokens
+    block = lane // tokens
+    owner = block // Z * Z + block % (Z // STRIDE) * STRIDE + block // (Z // STRIDE) % STRIDE
     count = node_counts(anc, owner * node_slots + node_slots - 1, range(level_count - 1))
     count_ref[...] = jnp.where(owner == lax.axis_index("leaf"), 0.0, count)
 
@@ -148,39 +149,39 @@
 
     for k in range(KV_HEADS):
         cols = slice(k * HEAD_DIM, (k + 1) * HEAD_DIM)
-        query = query_ref[k]
+        query = half_ref[prompt_cols + node_cols :, cols]
         top = None
         for start in range(0, prompt_cols, CHUNK):
             s = dot_nt(query, prompt_ref[start : start + CHUNK, cols])
-            w_ref[k, :, start : start + CHUNK] = s
+            w_ref[k, start // CHUNK] = s
             part = fold(s, jnp.maximum)
             top = part if top is None else jnp.maximum(top, part)
         s = dot_nt(query, node_ref[:, :, cols].reshape(node_cols, HEAD_DIM))
         s = jnp.where(mult > 0.0, s, -jnp.inf)
-        w_ref[k, :, prompt_cols:] = s
+        w_ref[k, prompt_cols // CHUNK] = s
         top = jnp.max(jnp.maximum(top, fold(s, jnp.maximum)), axis=1, keepdims=True)
         total = jnp.zeros((s.shape[0], LANES), jnp.float32)
         for start in range(0, prompt_cols, CHUNK):
-            w = jnp.exp(w_ref[k, :, start : start + CHUNK] - top)
-            w_ref[k, :, start : start + CHUNK] = w
+            w = jnp.exp(w_ref[k, start // CHUNK] - top)
+            w_ref[k, start // CHUNK] = w
             total = total + fold(w, jnp.add)
-        w = jnp.exp(w_ref[k, :, prompt_cols:] - top) * mult
-        w_ref[k, :, prompt_cols:] = w
+        w = jnp.exp(w_ref[k, prompt_cols // CHUNK] - top) * mult
+        w_ref[k, prompt_cols // CHUNK] = w
         total = total + fold(w, jnp.add)
-        total_ref[k] = jnp.broadcast_to(jnp.sum(total, axis=1, keepdims=True), total.shape)
-        max_ref[k] = jnp.broadcast_to(top, total.shape)
-    copies[4].wait()
-    copies[5].wait()
-
-
-def late_kernel(query_ref, shared_ref, w_ref, max_ref, total_ref, count_ref, prompt_ref, node_ref, own_ref, out_ref):
+        w_ref[k, prompt_cols // CHUNK + 1, :, LANES:] = jnp.broadcast_to(jnp.sum(total, axis=1, keepdims=True), total.shape)
+        w_ref[k, prompt_cols // CHUNK + 1, :, :LANES] = jnp.broadcast_to(top, total.shape)
+    for copy in copies[4:]:
+        copy.wait()
+
+
+def late_kernel(shared_ref, w_ref, half_ref, count_ref, own_ref, out_ref):
     owners = shared_ref.shape[0]
     tokens = shared_ref.shape[1] // 2
-    prompt_cols = prompt_ref.shape[0]
-    node_cols = node_ref.shape[0] * node_ref.shape[1]
     shared_cols = owners * tokens
-    rows = query_ref.shape[1] // GROUP
+    rows = w_ref.shape[2] // GROUP
     half = rows // 2
+    chunks = w_ref.shape[1] - 1
+    early_cols = chunks * CHUNK
     count = count_ref[...]
     reps = GROUP * rows // count.shape[0]
     pick = jnp.where(lax.broadcasted_iota(jnp.int32, (8, HEAD_DIM), 1) == 0, 1.0, 0.0).astype(jnp.bfloat16)
@@ -191,21 +192,18 @@
         values = shared_ref[:, tokens : 2 * tokens, cols].reshape(shared_cols, HEAD_DIM)
         marks = dot_nt(pick, keys)[0:1]
         mult = tall(jnp.where(marks < INVALID_KEY / 2, count, 0.0), reps)
-        s = dot_nt(query_ref[k], keys)
+        s = dot_nt(half_ref[early_cols:, cols], keys)
         s = jnp.where(mult > 0.0, s, -jnp.inf)
-        early_max = max_ref[k]
+        early_max = w_ref[k, chunks, :, :LANES]
         block_max = jnp.maximum(jnp.max(fold(s, jnp.maximum), axis=1, keepdims=True), early_max)
         scale = jnp.exp(early_max - block_max)
         w = jnp.exp(s - block_max[:, 0:1]) * mult
-        total = jnp.sum(fold(w, jnp.add), axis=1, keepdims=True) + total_ref[k] * scale
+        total = jnp.sum(fold(w, jnp.add), axis=1, keepdims=True) + w_ref[k, chunks, :, LANES:] * scale
         acc = jnp.dot(w.astype(jnp.bfloat16), values, preferred_element_type=jnp.float32)
         wide = jnp.concatenate([scale, scale], axis=1)
-        for start in range(0, prompt_cols, CHUNK):
-            w = (w_ref[k, :, start : start + CHUNK] * wide).astype(jnp.bfloat16)
-            acc = acc + jnp.dot(w, prompt_ref[start : start + CHUNK, cols], preferred_element_type=jnp.float32)
-        w = (w_ref[k, :, prompt_cols:] * wide).astype(jnp.bfloat16)
-        node_values = node_ref[:, :, cols].reshape(node_cols, HEAD_DIM)
-        acc = acc + jnp.dot(w, node_values, preferred_element_type=jnp.float32)
+        for c in range(chunks):
+            w = (w_ref[k, c] * wide).astype(jnp.bfloat16)
+            acc = acc + jnp.dot(w, half_ref[c * CHUNK : (c + 1) * CHUNK, cols], preferred_element_type=jnp.float32)
 
         core = lax.rem(lax.axis_index("seq"), 2)
         total = jnp.broadcast_to(total, block_max.shape)
@@ -293,17 +291,17 @@
 
 
 def gather_shared(own, owners, early):
-    along_z = [list(range(x, x + Z)) for x in range(0, owners, Z)]
-    along_x = [list(range(z, owners, Z)) for z in range(Z)]
-    plane = lax.all_to_all(own, "leaf", 0, 0, tiled=True, axis_index_groups=along_z)
-    plane = pl.pallas_call(
+    first = [[x + z + k for k in range(0, Z, STRIDE)] for x in range(0, owners, Z) for z in range(STRIDE)]
+    second = [[x + z + k for x in range(0, owners, Z) for k in range(STRIDE)] for z in range(0, Z, STRIDE)]
+    part = lax.all_to_all(own, "leaf", 0, 0, tiled=True, axis_index_groups=first)
+    parts = pl.pallas_call(
         copies_kernel,
-        out_shape=jax.ShapeDtypeStruct((owners // Z,) + plane.shape, plane.dtype),
+        out_shape=jax.ShapeDtypeStruct((len(second[0]),) + part.shape, part.dtype),
         in_specs=[VMEM, VMEM],
         out_specs=VMEM,
         compiler_params=params(8),
-    )(plane, early)
-    shared = lax.all_to_all(plane, "leaf", 0, 0, tiled=True, axis_index_groups=along_x)
+    )(part, early)
+    shared = lax.all_to_all(parts, "leaf", 0, 0, tiled=True, axis_index_groups=second)
     return shared.reshape((owners,) + own.shape[1:])
 
 
@@ -317,7 +315,7 @@
 
     own = pl.pallas_call(
         post_kernel,
-        out_shape=jax.ShapeDtypeStruct((Z, 2 * tokens, width), jnp.bfloat16),
+        out_shape=pltpu.VMEM((Z // STRIDE, 2 * tokens, width), jnp.bfloat16),
         in_specs=[HBM, HBM],
         out_specs=VMEM,
         scratch_shapes=[
@@ -328,27 +326,23 @@
         compiler_params=params(8),
     )(*in_hbm(node_lengths, node_kv))
     query_rows = queries.transpose(1, 0, 2).reshape(rows, feat_width)
-    cols = prompt_cols + node_slots * tokens
-    row_shape = jax.ShapeDtypeStruct((KV_HEADS, GROUP * rows, LANES), jnp.float32)
-    weights, early_max, early_total, query, count, prompt_values, node_values = pl.pallas_call(
+    early_cols = prompt_cols + node_slots * tokens
+    assert prompt_cols % CHUNK == 0 and node_slots * tokens == CHUNK and GROUP * rows == CHUNK
+    early, halves, count = pl.pallas_call(
         functools.partial(early_kernel, steps),
         out_shape=(
-            jax.ShapeDtypeStruct((KV_HEADS, GROUP * rows, cols), jnp.float32),
-            row_shape,
-            row_shape,
-            jax.ShapeDtypeStruct((KV_HEADS, GROUP * rows, HEAD_DIM), jnp.bfloat16),
+            jax.ShapeDtypeStruct((KV_HEADS, early_cols // CHUNK + 1, CHUNK, CHUNK), jnp.float32),
+            jax.ShapeDtypeStruct((early_cols + GROUP * rows, width), jnp.bfloat16),
             jax.ShapeDtypeStruct((leaf_count, owners * tokens), jnp.float32),
-            jax.ShapeDtypeStruct((prompt_cols, width), jnp.bfloat16),
-            jax.ShapeDtypeStruct((node_slots, tokens, width), jnp.bfloat16),
         ),
         in_specs=[HBM, HBM, HBM, HBM, VMEM],
-        out_specs=(VMEM,) * 7,
+        out_specs=(VMEM,) * 3,
         scratch_shapes=[
             pltpu.SMEM((node_slots,), jnp.int32),
             pltpu.VMEM(ancestors.shape, jnp.int32),
             pltpu.VMEM((prompt_cols, width), jnp.bfloat16),
             pltpu.VMEM((node_slots, tokens, width), jnp.bfloat16),
-            pltpu.SemaphoreType.DMA((6,)),
+            pltpu.SemaphoreType.DMA((5 + node_slots,)),
         ],
         compiler_params=params(16),
         cost_estimate=pl.CostEstimate(flops=500_000_000, bytes_accessed=6_000_000, transcendentals=800_000),
@@ -360,10 +354,10 @@
     kept, sent = pl.pallas_call(
         late_kernel,
         out_shape=(jax.ShapeDtypeStruct(wire.shape, jnp.float32), wire),
-        in_specs=[VMEM] * 8,
+        in_specs=[VMEM] * 4,
         out_specs=(VMEM, VMEM),
         compiler_params=params(16),
-    )(query, shared, weights, early_max, early_total, count, prompt_values, node_values)
+    )(shared, early, halves, count)
 
     got = lax.ppermute(sent, "seq", [(i, i ^ 1) for i in range(seqs)])
     parts = pl.pallas_call(

time: 64.4 us -> 64.9 us (level)
  blocking collectives: 31.3 us -> 33.4 us
  waiting for transfers between devices: 3.87 us -> 3.04 us
    all_to_all x1, blocking collectives: 16 us -> 18.2 us  [gather_shared(): lax.all_to_all(parts, 'leaf', 0, 0, tiled=True, axis_index_groups=second)]
    all_to_all x1, waiting for transfers between devices: 2.87 us -> 2.03 us  [gather_shared(): lax.all_to_all(own, 'leaf', 0, 0, tiled=True, axis_index_groups=first)]
    ppermute x1, starting transfers between devices: 5.87 us -> 5.2 us  [shards(): got = lax.ppermute(sent, 'seq', [(i, i ^ 1) for i in range(seqs)])]
    unnamed x20 -> x4, local copies, waits for them, and re-layouts: 3.93 us -> 3.82 us
where the time goes in v9:
time: 64.9 us; the launch traced here: 64.5 us
  blocking collectives  33.4 us (51%)
  starting transfers between devices  16.1 us (25%)
  Pallas kernels  7.02 us (11%)
  local copies, waits for them, and re-layouts  4.92 us (8%)
  waiting for transfers between devices  3.04 us (5%)
    all_to_all x1, blocking collectives, gather_shared(): lax.all_to_all(parts, 'leaf', 0, 0, tiled=True, axis_index_groups=second)  18.2 us
    all_to_all x1, blocking collectives, shards(): lax.all_to_all(parts, 'seq', 0, 0, tiled=True, axis_index_groups=chips)  15.2 us
    all_to_all x1, starting transfers between devices, gather_shared(): lax.all_to_all(own, 'leaf', 0, 0, tiled=True, axis_index_groups=first)  10.9 us
    ppermute x1, starting transfers between devices, shards(): got = lax.ppermute(sent, 'seq', [(i, i ^ 1) for i in range(seqs)])  5.2 us
    unnamed x4, local copies, waits for them, and re-layouts  3.82 us
    pallas_call x1, Pallas kernels, shards(): pl.pallas_call(functools.partial(early_kernel, steps), out_shape=(jax.Sha...  2.63 us
    all_to_all x1, waiting for transfers between devices, gather_shared(): lax.all_to_all(own, 'leaf', 0, 0, tiled=True, axis_index_groups=first)  2.03 us
    pallas_call x1, Pallas kernels, shards(): pl.pallas_call(post_kernel, out_shape=pltpu.VMEM((Z // STRIDE, 2 * tokens...  1.48 us
  transfers between devices with their start and end apart: 2, of which 2 were waited for; matrix products, arithmetic and copies ran while one was open for 2% of the time, Pallas kernels for 4%

profile of v9, /device:TPU:1, one launch (start us, length us, event | category | flops | bytes accessed | tf_op | source)
XLA Modules:
  0.0 64.5 jit_solution(13527662882043497198)
XLA Ops:
  0.0 1.5 %shard_map.55 = bf16[4,32,512]{2,1,0:T(8,128)(2,1)} custom-call(s32[16]{0:T(128)} %lengths_hbm.3, bf16[2,16,16,512]{3,2,1,0:T(8,128)(2,1)} %node_hbm.3), custom_call_target="tpu_custom_call" | custom-call | tf_op jit(solution)/shard_map/pallas_call | solution.py:316
  1.5 10.9 %all-to-all-start = ((bf16[4,32,512]{2,1,0:T(8,128)(2,1)}), bf16[4,32,512]{2,1,0:T(8,128)(2,1)S(1)}, u32[]{:S(2)}, u32[]{:S(2)}) async-start(bf16[4,32,512]{2,1,0:T(8,128)(2,1)} %shard_map.55), calls=%async_computation | async-start | bytes 262144 | tf_op jit(solution)/shard_map/all_to_all | solution.py:296
  12.3 1.1 %copy.8 = bf16[4,8,4096]{2,1,0:T(8,128)(2,1)S(1)} copy(bf16[4,8,4096]{2,0,1:T(4,128)(2,1)} %bitcast.7) | data formatting | bytes 524288 | tf_op jit(solution)/shard_map/transpose | solution.py:328
  13.4 2.6 %shard_map.56 = (f32[2,7,256,256]{3,2,1,0:T(8,128)S(1)}, bf16[1792,512]{1,0:T(8,128)(2,1)S(1)}, f32[8,512]{1,0:T(8,128)S(1)}) custom-call(s32[16]{0:T(128)} %lengths_hbm.3, s32[8,10]{1,0:T(8,128)} %anc_hbm.1, bf16[2,1280,512]{2,1,0:T(8,128)(2,1)} %prompt_hbm.1, bf16[2,16,16,512]{3,2,1,0:T(8,128)(2,1)} %node_hbm.3, bf16[32,4096]{1,0:T(8,128)(2,1)S(1)} %bitcast.6), custom_call_target="tpu_custom_call" | custom-call | flops 500000000 | bytes 6000000 | tf_op jit(solution)/shard_map/pallas_call | solution.py:331
  16.1 0.0 copy-start
  16.1 1.8 %copy-done = f32[2,7,256,256]{3,2,1,0:T(8,128)} copy-done((f32[2,7,256,256]{3,2,1,0:T(8,128)}, f32[2,7,256,256]{3,2,1,0:T(8,128)S(1)}, u32[]{:S(2)}) %copy-start) | copy-done | bytes 3670040
  17.9 2.0 %all-to-all-done.plane_ref = bf16[4,32,512]{2,1,0:T(8,128)(2,1)S(1)} async-done(((bf16[4,32,512]{2,1,0:T(8,128)(2,1)}), bf16[4,32,512]{2,1,0:T(8,128)(2,1)S(1)}, u32[]{:S(2)}, u32[]{:S(2)}) %all-to-all-start) | async-done | bytes 131104 | tf_op jit(solution)/shard_map/all_to_all | solution.py:296
  19.9 0.1 shard_map.57
  20.0 18.2 %all_to_all.15 = bf16[8,4,32,512]{3,2,1,0:T(8,128)(2,1)S(1)} all-to-all(bf16[8,4,32,512]{3,2,1,0:T(8,128)(2,1)S(1)} %shard_map.57), channel_id=1, replica_groups={{0,1,8,9,16,17,24,25},{2,3,10,11,18,19,26,27},{4,5,12,13,20,21,28,29},{..., dimensions={0} | all-to-all | bytes 2097152 | tf_op jit(solution)/shard_map/all_to_all | solution.py:304
  38.1 0.0 copy-start.1
  38.1 2.0 %copy-done.1 = f32[2,7,256,256]{3,2,1,0:T(8,128)S(1)} copy-done((f32[2,7,256,256]{3,2,1,0:T(8,128)S(1)}, f32[2,7,256,256]{3,2,1,0:T(8,128)}, u32[]{:S(2)}) %copy-start.1) | copy-done | bytes 3670040
  40.2 1.4 %shard_map.58 = (f32[8,16,640]{2,1,0:T(8,128)S(1)}, s16[8,16,640]{2,1,0:T(8,128)(2,1)S(1)}) custom-call(bf16[32,32,512]{2,1,0:T(8,128)(2,1)S(1)} %bitcast.5, f32[2,7,256,256]{3,2,1,0:T(8,128)S(1)} %copy-done.1, bf16[1792,512]{1,0:T(8,128)(2,1)S(1)} %get-tuple-element.12.half_ref, f32[8,512]{1,0:T(8,128)S(1)} %get-tuple-element.10.early_ref.count_ref), custom_call_target="tpu_custom_call" | custom-call | tf_op jit(solution)/shard_map/pallas_call | solution.py:354
  41.6 5.2 %collective-permute-start = (s16[8,16,640]{2,1,0:T(8,128)(2,1)S(1)}, s16[8,16,640]{2,1,0:T(8,128)(2,1)S(1)}, u32[]{:S(2)}, u32[]{:S(2)}) collective-permute-start(s16[8,16,640]{2,1,0:T(8,128)(2,1)S(1)} %get-tuple-element.14), channel_id=1, source_target_pairs={{0,32},{32,0},{64,96},{96,64},{128,160},{160,128},{192,224},{224,1... | collective-permute-start | bytes 491528 | tf_op jit(solution)/shard_map/ppermute | solution.py:362
  46.8 1.0 %collective-permute-done.other_ref = s16[8,16,640]{2,1,0:T(8,128)(2,1)S(1)} collective-permute-done((s16[8,16,640]{2,1,0:T(8,128)(2,1)S(1)}, s16[8,16,640]{2,1,0:T(8,128)(2,1)S(1)}, u32[]{:S(2)}, u32[]{:S(2)}) %collective-permute-start) | collective-permute-done | bytes 163872 | tf_op jit(solution)/shard_map/ppermute | solution.py:362
  47.8 0.5 shard_map.59
  48.3 15.2 %all_to_all.16.parts_ref = s16[8,16,640]{2,1,0:T(8,128)(2,1)S(1)} all-to-all(s16[8,16,640]{2,1,0:T(8,128)(2,1)S(1)} %shard_map.59), channel_id=1, replica_groups={{0,64,128,192,256,320,384,448},{32,96,160,224,288,352,416,480},{1,65,12..., dimensions={0} | all-to-all | bytes 327680 | tf_op jit(solution)/shard_map/all_to_all | solution.py:371
  63.6 0.9 %shard_map.60 = bf16[8,4,256]{2,1,0:T(4,128)(2,1)} custom-call(s16[8,16,640]{2,1,0:T(8,128)(2,1)S(1)} %all_to_all.16.parts_ref), custom_call_target="tpu_custom_call" | custom-call | tf_op jit(solution)/shard_map/pallas_call | solution.py:372
Async XLA Ops:
  1.5 18.4 %all-to-all-start = ((bf16[4,32,512]{2,1,0:T(8,128)(2,1)}), bf16[4,32,512]{2,1,0:T(8,128)(2,1)S(1)}, u32[]{:S(2)}, u32[]{:S(2)}) async-start(bf16[4,32,512]{2,1,0:T(8,128)(2,1)} %shard_map.55), calls=%async_computation | async-start | bytes 262144 | tf_op jit(solution)/shard_map/all_to_all | solution.py:296
  16.1 1.8 %copy-start = (f32[2,7,256,256]{3,2,1,0:T(8,128)}, f32[2,7,256,256]{3,2,1,0:T(8,128)S(1)}, u32[]{:S(2)}) copy-start(f32[2,7,256,256]{3,2,1,0:T(8,128)S(1)} %get-tuple-element.11.w_ref) | copy-start | bytes 11010052
  38.1 2.0 %copy-start.1 = (f32[2,7,256,256]{3,2,1,0:T(8,128)S(1)}, f32[2,7,256,256]{3,2,1,0:T(8,128)}, u32[]{:S(2)}) copy-start(f32[2,7,256,256]{3,2,1,0:T(8,128)} %copy-done) | copy-start | bytes 11010052
  41.6 6.2 %collective-permute-start = (s16[8,16,640]{2,1,0:T(8,128)(2,1)S(1)}, s16[8,16,640]{2,1,0:T(8,128)(2,1)S(1)}, u32[]{:S(2)}, u32[]{:S(2)}) collective-permute-start(s16[8,16,640]{2,1,0:T(8,128)(2,1)S(1)} %get-tuple-element.14), channel_id=1, source_target_pairs={{0,32},{32,0},{64,96},{96,64},{128,160},{160,128},{192,224},{224,1... | collective-permute-start | bytes 491528 | tf_op jit(solution)/shard_map/ppermute | solution.py:362

commit v10 on v9

--- a/solution.py
+++ b/solution.py
@@ -91,6 +91,7 @@
     node_hbm,
     q_ref,
     w_ref,
+    row_ref,
     half_ref,
     count_ref,
     lengths_ref,
@@ -168,19 +169,19 @@
         w = jnp.exp(w_ref[k, prompt_cols // CHUNK] - top) * mult
         w_ref[k, prompt_cols // CHUNK] = w
         total = total + fold(w, jnp.add)
-        w_ref[k, prompt_cols // CHUNK + 1, :, LANES:] = jnp.broadcast_to(jnp.sum(total, axis=1, keepdims=True), total.shape)
-        w_ref[k, prompt_cols // CHUNK + 1, :, :LANES] = jnp.broadcast_to(top, total.shape)
+        row_ref[k, :, LANES:] = jnp.broadcast_to(jnp.sum(total, axis=1, keepdims=True), total.shape)
+        row_ref[k, :, :LANES] = jnp.broadcast_to(top, total.shape)
     for copy in copies[4:]:
         copy.wait()
 
 
-def late_kernel(shared_ref, w_ref, half_ref, count_ref, own_ref, out_ref):
+def late_kernel(shared_ref, w_ref, row_ref, half_ref, count_ref, own_ref, out_ref):
     owners = shared_ref.shape[0]
     tokens = shared_ref.shape[1] // 2
     shared_cols = owners * tokens
     rows = w_ref.shape[2] // GROUP
     half = rows // 2
-    chunks = w_ref.shape[1] - 1
+    chunks = w_ref.shape[1]
     early_cols = chunks * CHUNK
     count = count_ref[...]
     reps = GROUP * rows // count.shape[0]
@@ -194,11 +195,11 @@
         mult = tall(jnp.where(marks < INVALID_KEY / 2, count, 0.0), reps)
         s = dot_nt(half_ref[early_cols:, cols], keys)
         s = jnp.where(mult > 0.0, s, -jnp.inf)
-        early_max = w_ref[k, chunks, :, :LANES]
+        early_max = row_ref[k, :, :LANES]
         block_max = jnp.maximum(jnp.max(fold(s, jnp.maximum), axis=1, keepdims=True), early_max)
         scale = jnp.exp(early_max - block_max)
         w = jnp.exp(s - block_max[:, 0:1]) * mult
-        total = jnp.sum(fold(w, jnp.add), axis=1, keepdims=True) + w_ref[k, chunks, :, LANES:] * scale
+        total = jnp.sum(fold(w, jnp.add), axis=1, keepdims=True) + row_ref[k, :, LANES:] * scale
         acc = jnp.dot(w.astype(jnp.bfloat16), values, preferred_element_type=jnp.float32)
         wide = jnp.concatenate([scale, scale], axis=1)
         for c in range(chunks):
@@ -315,7 +316,7 @@
 
     own = pl.pallas_call(
         post_kernel,
-        out_shape=pltpu.VMEM((Z // STRIDE, 2 * tokens, width), jnp.bfloat16),
+        out_shape=jax.ShapeDtypeStruct((Z // STRIDE, 2 * tokens, width), jnp.bfloat16),
         in_specs=[HBM, HBM],
         out_specs=VMEM,
         scratch_shapes=[
@@ -328,15 +329,16 @@
     query_rows = queries.transpose(1, 0, 2).reshape(rows, feat_width)
     early_cols = prompt_cols + node_slots * tokens
     assert prompt_cols % CHUNK == 0 and node_slots * tokens == CHUNK and GROUP * rows == CHUNK
-    early, halves, count = pl.pallas_call(
+    early, early_rows, halves, count = pl.pallas_call(
         functools.partial(early_kernel, steps),
         out_shape=(
-            jax.ShapeDtypeStruct((KV_HEADS, early_cols // CHUNK + 1, CHUNK, CHUNK), jnp.float32),
+            jax.ShapeDtypeStruct((KV_HEADS, early_cols // CHUNK, CHUNK, CHUNK), jnp.float32),
+            jax.ShapeDtypeStruct((KV_HEADS, GROUP * rows, 2 * LANES), jnp.float32),
             jax.ShapeDtypeStruct((early_cols + GROUP * rows, width), jnp.bfloat16),
             jax.ShapeDtypeStruct((leaf_count, owners * tokens), jnp.float32),
         ),
         in_specs=[HBM, HBM, HBM, HBM, VMEM],
-        out_specs=(VMEM,) * 3,
+        out_specs=(VMEM,) * 4,
         scratch_shapes=[
             pltpu.SMEM((node_slots,), jnp.int32),
             pltpu.VMEM(ancestors.shape, jnp.int32),
@@ -354,10 +356,10 @@
     kept, sent = pl.pallas_call(
         late_kernel,
         out_shape=(jax.ShapeDtypeStruct(wire.shape, jnp.float32), wire),
-        in_specs=[VMEM] * 4,
+        in_specs=[VMEM] * 5,
         out_specs=(VMEM, VMEM),
         compiler_params=params(16),
-    )(shared, early, halves, count)
+    )(shared, early, early_rows, halves, count)
 
     got = lax.ppermute(sent, "seq", [(i, i ^ 1) for i in range(seqs)])
     parts = pl.pallas_call(

time: 64.9 us -> 63 us (0.971)
  local copies, waits for them, and re-layouts: 4.92 us -> 3.14 us
    unnamed x4 -> x8, local copies, waits for them, and re-layouts: 3.82 us -> 2.04 us
where the time goes in v10:
time: 63 us; the launch traced here: 62.6 us
  blocking collectives  33.5 us (53%)
  starting transfers between devices  16.1 us (26%)
  Pallas kernels  7.03 us (11%)
  local copies, waits for them, and re-layouts  3.14 us (5%)
  waiting for transfers between devices  2.79 us (4%)
    all_to_all x1, blocking collectives, gather_shared(): lax.all_to_all(parts, 'leaf', 0, 0, tiled=True, axis_index_groups=second)  18.3 us
    all_to_all x1, blocking collectives, shards(): lax.all_to_all(parts, 'seq', 0, 0, tiled=True, axis_index_groups=chips)  15.2 us
    all_to_all x1, starting transfers between devices, gather_shared(): lax.all_to_all(own, 'leaf', 0, 0, tiled=True, axis_index_groups=first)  10.9 us
    ppermute x1, starting transfers between devices, shards(): got = lax.ppermute(sent, 'seq', [(i, i ^ 1) for i in range(seqs)])  5.2 us
    pallas_call x1, Pallas kernels, shards(): pl.pallas_call(functools.partial(early_kernel, steps), out_shape=(jax.Sha...  2.62 us
    unnamed x8, local copies, waits for them, and re-layouts  2.04 us
    all_to_all x1, waiting for transfers between devices, gather_shared(): lax.all_to_all(own, 'leaf', 0, 0, tiled=True, axis_index_groups=first)  1.79 us
    pallas_call x1, Pallas kernels, shards(): pl.pallas_call(post_kernel, out_shape=jax.ShapeDtypeStruct((Z // STRIDE,...  1.49 us
  transfers between devices with their start and end apart: 2, of which 2 were waited for; matrix products, arithmetic and copies ran while one was open for 2% of the time, Pallas kernels for 4%

profile of v10, /device:TPU:1, one launch (start us, length us, event | category | flops | bytes accessed | tf_op | source)
XLA Modules:
  0.0 62.6 jit_solution(13969481327064248112)
XLA Ops:
  0.0 1.5 %shard_map.55 = bf16[4,32,512]{2,1,0:T(8,128)(2,1)} custom-call(s32[16]{0:T(128)} %lengths_hbm.3, bf16[2,16,16,512]{3,2,1,0:T(8,128)(2,1)} %node_hbm.3), custom_call_target="tpu_custom_call" | custom-call | tf_op jit(solution)/shard_map/pallas_call | solution.py:317
  1.5 10.9 %all-to-all-start = ((bf16[4,32,512]{2,1,0:T(8,128)(2,1)}), bf16[4,32,512]{2,1,0:T(8,128)(2,1)S(1)}, u32[]{:S(2)}, u32[]{:S(2)}) async-start(bf16[4,32,512]{2,1,0:T(8,128)(2,1)} %shard_map.55), calls=%async_computation | async-start | bytes 262144 | tf_op jit(solution)/shard_map/all_to_all | solution.py:297
  12.4 1.1 %copy.8 = bf16[4,8,4096]{2,1,0:T(8,128)(2,1)S(1)} copy(bf16[4,8,4096]{2,0,1:T(4,128)(2,1)} %bitcast.7) | data formatting | bytes 524288 | tf_op jit(solution)/shard_map/transpose | solution.py:329
  13.5 2.6 %shard_map.56 = (f32[2,6,256,256]{3,2,1,0:T(8,128)S(1)}, f32[2,256,256]{2,1,0:T(8,128)S(1)}, bf16[1792,512]{1,0:T(8,128)(2,1)S(1)}, f32[8,512]{1,0:T(8,128)S(1)}) custom-call(s32[16]{0:T(128)} %lengths_hbm.3, s32[8,10]{1,0:T(8,128)} %anc_hbm.1, bf16[2,1280,512]{2,1,0:T(8,128)(2,1)} %prompt_hbm.1, bf16[2,16,16,512]{3,2,1,0:T(8,128)(2,1)} %node_hbm.3, ...), custom_call_target="tpu_custom_call" | custom-call | flops 500000000 | bytes 6000000 | tf_op jit(solution)/shard_map/pallas_call | solution.py:332
  16.1 0.0 copy-start
  16.1 1.2 %copy-done = bf16[1792,512]{1,0:T(8,128)(2,1)} copy-done((bf16[1792,512]{1,0:T(8,128)(2,1)}, bf16[1792,512]{1,0:T(8,128)(2,1)S(1)}, u32[]{:S(2)}) %copy-start) | copy-done | bytes 1835032
  17.3 0.0 copy-start.2
  17.3 0.8 %copy-done.2 = f32[2,256,256]{2,1,0:T(8,128)} copy-done((f32[2,256,256]{2,1,0:T(8,128)}, f32[2,256,256]{2,1,0:T(8,128)S(1)}, u32[]{:S(2)}) %copy-start.2) | copy-done | bytes 524312
  18.1 1.8 %all-to-all-done.plane_ref = bf16[4,32,512]{2,1,0:T(8,128)(2,1)S(1)} async-done(((bf16[4,32,512]{2,1,0:T(8,128)(2,1)}), bf16[4,32,512]{2,1,0:T(8,128)(2,1)S(1)}, u32[]{:S(2)}, u32[]{:S(2)}) %all-to-all-start) | async-done | bytes 131104 | tf_op jit(solution)/shard_map/all_to_all | solution.py:297
  19.9 0.0 copy-start.1
  19.9 0.0 copy-start.3
  19.9 0.1 shard_map.57
  20.0 18.3 %all_to_all.15 = bf16[8,4,32,512]{3,2,1,0:T(8,128)(2,1)S(1)} all-to-all(bf16[8,4,32,512]{3,2,1,0:T(8,128)(2,1)S(1)} %shard_map.57), channel_id=1, replica_groups={{0,1,8,9,16,17,24,25},{2,3,10,11,18,19,26,27},{4,5,12,13,20,21,28,29},{..., dimensions={0} | all-to-all | bytes 2097152 | tf_op jit(solution)/shard_map/all_to_all | solution.py:305
  38.3 0.0 copy-done.1
  38.3 0.0 copy-done.3
  38.3 1.4 %shard_map.58 = (f32[8,16,640]{2,1,0:T(8,128)S(1)}, s16[8,16,640]{2,1,0:T(8,128)(2,1)S(1)}) custom-call(bf16[32,32,512]{2,1,0:T(8,128)(2,1)S(1)} %bitcast.5, f32[2,6,256,256]{3,2,1,0:T(8,128)S(1)} %get-tuple-element.12.w_ref, f32[2,256,256]{2,1,0:T(8,128)S(1)} %copy-done.3, bf16[1792,512]{1,0:T(8,128)(2,1)S(1)} %copy-done.1, ...), custom_call_target="tpu_custom_call" | custom-call | tf_op jit(solution)/shard_map/pallas_call | solution.py:356
  39.7 5.2 %collective-permute-start = (s16[8,16,640]{2,1,0:T(8,128)(2,1)S(1)}, s16[8,16,640]{2,1,0:T(8,128)(2,1)S(1)}, u32[]{:S(2)}, u32[]{:S(2)}) collective-permute-start(s16[8,16,640]{2,1,0:T(8,128)(2,1)S(1)} %get-tuple-element.16), channel_id=1, source_target_pairs={{0,32},{32,0},{64,96},{96,64},{128,160},{160,128},{192,224},{224,1... | collective-permute-start | bytes 491528 | tf_op jit(solution)/shard_map/ppermute | solution.py:364
  44.9 1.0 %collective-permute-done.other_ref = s16[8,16,640]{2,1,0:T(8,128)(2,1)S(1)} collective-permute-done((s16[8,16,640]{2,1,0:T(8,128)(2,1)S(1)}, s16[8,16,640]{2,1,0:T(8,128)(2,1)S(1)}, u32[]{:S(2)}, u32[]{:S(2)}) %collective-permute-start) | collective-permute-done | bytes 163872 | tf_op jit(solution)/shard_map/ppermute | solution.py:364
  45.9 0.5 shard_map.59
  46.5 15.2 %all_to_all.16.parts_ref = s16[8,16,640]{2,1,0:T(8,128)(2,1)S(1)} all-to-all(s16[8,16,640]{2,1,0:T(8,128)(2,1)S(1)} %shard_map.59), channel_id=1, replica_groups={{0,64,128,192,256,320,384,448},{32,96,160,224,288,352,416,480},{1,65,12..., dimensions={0} | all-to-all | bytes 327680 | tf_op jit(solution)/shard_map/all_to_all | solution.py:373
  61.7 0.9 %shard_map.60 = bf16[8,4,256]{2,1,0:T(4,128)(2,1)} custom-call(s16[8,16,640]{2,1,0:T(8,128)(2,1)S(1)} %all_to_all.16.parts_ref), custom_call_target="tpu_custom_call" | custom-call | tf_op jit(solution)/shard_map/pallas_call | solution.py:374
Async XLA Ops:
  1.5 18.4 %all-to-all-start = ((bf16[4,32,512]{2,1,0:T(8,128)(2,1)}), bf16[4,32,512]{2,1,0:T(8,128)(2,1)S(1)}, u32[]{:S(2)}, u32[]{:S(2)}) async-start(bf16[4,32,512]{2,1,0:T(8,128)(2,1)} %shard_map.55), calls=%async_computation | async-start | bytes 262144 | tf_op jit(solution)/shard_map/all_to_all | solution.py:297
  16.1 1.2 %copy-start = (bf16[1792,512]{1,0:T(8,128)(2,1)}, bf16[1792,512]{1,0:T(8,128)(2,1)S(1)}, u32[]{:S(2)}) copy-start(bf16[1792,512]{1,0:T(8,128)(2,1)S(1)} %get-tuple-element.14.half_ref) | copy-start | bytes 5505028
  17.3 0.8 %copy-start.2 = (f32[2,256,256]{2,1,0:T(8,128)}, f32[2,256,256]{2,1,0:T(8,128)S(1)}, u32[]{:S(2)}) copy-start(f32[2,256,256]{2,1,0:T(8,128)S(1)} %get-tuple-element.13.row_ref) | copy-start | bytes 1572868
  19.9 18.4 %copy-start.1 = (bf16[1792,512]{1,0:T(8,128)(2,1)S(1)}, bf16[1792,512]{1,0:T(8,128)(2,1)}, u32[]{:S(2)}) copy-start(bf16[1792,512]{1,0:T(8,128)(2,1)} %copy-done) | copy-start | bytes 5505028
  19.9 18.4 %copy-start.3 = (f32[2,256,256]{2,1,0:T(8,128)S(1)}, f32[2,256,256]{2,1,0:T(8,128)}, u32[]{:S(2)}) copy-start(f32[2,256,256]{2,1,0:T(8,128)} %copy-done.2) | copy-start | bytes 1572868
  39.7 6.2 %collective-permute-start = (s16[8,16,640]{2,1,0:T(8,128)(2,1)S(1)}, s16[8,16,640]{2,1,0:T(8,128)(2,1)S(1)}, u32[]{:S(2)}, u32[]{:S(2)}) collective-permute-start(s16[8,16,640]{2,1,0:T(8,128)(2,1)S(1)} %get-tuple-element.16), channel_id=1, source_target_pairs={{0,32},{32,0},{64,96},{96,64},{128,160},{160,128},{192,224},{224,1... | collective-permute-start | bytes 491528 | tf_op jit(solution)/shard_map/ppermute | solution.py:364

commit v11 on v10

--- a/solution.py
+++ b/solution.py
@@ -15,6 +15,7 @@
 LANES = 128
 Z = 8
 STRIDE = 2
+FIRST_Z, FIRST_X, FIRST_CHIP = 2, 2, 6
 INVALID_KEY = 256.0
 TOP = 32767.0
 POINTS = (2.0**18, 2.0**26, 2.0**23)
@@ -126,8 +127,7 @@
     anc = anc_ref[...]
 
     lane = lax.broadcasted_iota(jnp.int32, (1, shared_cols), 1)
-    block = lane // tokens
-    owner = block // Z * Z + block % (Z // STRIDE) * STRIDE + block // (Z // STRIDE) % STRIDE
+    owner = owner_of(lane // tokens, shared_cols // tokens)
     count = node_counts(anc, owner * node_slots + node_slots - 1, range(level_count - 1))
     count_ref[...] = jnp.where(owner == lax.axis_index("leaf"), 0.0, count)
 
@@ -215,7 +215,7 @@
                 odd = x[(2 * pair + 1) * rows : (2 * pair + 2) * rows]
                 kept.append(jnp.where(core == 0, even, odd))
                 sent.append(jnp.where(core == 0, odd, even))
-            slot = k * (GROUP // 2) + pair
+            slot = (k * (GROUP // 2) + pair - FIRST_CHIP) % (HEADS // 2)
             lane = lax.broadcasted_iota(jnp.int32, (half, LANES), 1)
             stats = [jnp.where(lane % (LANES // 2) == 0, kept[1][i : i + half], kept[2][i : i + half]) for i in (0, half)]
             own_ref[slot, :, 2 * HEAD_DIM :] = jnp.where(lane < LANES // 2, stats[0], stats[1])
@@ -291,9 +291,29 @@
             out_ref[:, part * half // leaf_count + i, :] = merged[i * leaf_count : (i + 1) * leaf_count]
 
 
+def turned(items, start):
+    items = list(items)
+    return items[start:] + items[:start]
+
+
+def gather_orders(owners):
+    return turned(range(0, Z, STRIDE), FIRST_Z), turned(range(0, owners, Z), FIRST_X)
+
+
+def owner_of(block, owners):
+    along_z, along_x = gather_orders(owners)
+    owner = block // (Z // STRIDE) % STRIDE
+    for i, z in enumerate(along_z):
+        owner = owner + jnp.where(block % (Z // STRIDE) == i, z, 0)
+    for i, x in enumerate(along_x):
+        owner = owner + jnp.where(block // Z == i, x, 0)
+    return owner
+
+
 def gather_shared(own, owners, early):
-    first = [[x + z + k for k in range(0, Z, STRIDE)] for x in range(0, owners, Z) for z in range(STRIDE)]
-    second = [[x + z + k for x in range(0, owners, Z) for k in range(STRIDE)] for z in range(0, Z, STRIDE)]
+    along_z, along_x = gather_orders(owners)
+    first = [[x + z + k for k in along_z] for x in range(0, owners, Z) for z in range(STRIDE)]
+    second = [[x + z + k for x in along_x for k in range(STRIDE)] for z in range(0, Z, STRIDE)]
     part = lax.all_to_all(own, "leaf", 0, 0, tiled=True, axis_index_groups=first)
     parts = pl.pallas_call(
         copies_kernel,
@@ -369,7 +389,7 @@
         out_specs=VMEM,
         compiler_params=params(8),
     )(kept, got)
-    chips = [list(range(c, seqs, 2)) for c in range(2)]
+    chips = [turned(range(c, seqs, 2), FIRST_CHIP) for c in range(2)]
     parts = lax.all_to_all(parts, "seq", 0, 0, tiled=True, axis_index_groups=chips)
     return pl.pallas_call(
         merge_kernel,

time: 63 us -> 58.7 us (0.932); the launches traced: 62.6 us -> 57.6 us
  blocking collectives: 33.5 us -> 28.9 us
  waiting for transfers between devices: 2.79 us -> 1.01 us
  starting transfers between devices: 16.1 us -> 17.4 us
    all_to_all x1, blocking collectives: 15.2 us -> 11.5 us  [shards(): lax.all_to_all(parts, 'seq', 0, 0, tiled=True, axis_index_groups=chips)]
    all_to_all x1, starting transfers between devices: 10.9 us -> 12.9 us  [gather_shared(): lax.all_to_all(own, 'leaf', 0, 0, tiled=True, axis_index_groups=first)]
    all_to_all x1, waiting for transfers between devices: 1.79 us -> 0.01 us  [gather_shared(): lax.all_to_all(own, 'leaf', 0, 0, tiled=True, axis_index_groups=first)]
    all_to_all x1, blocking collectives: 18.3 us -> 17.5 us  [gather_shared(): lax.all_to_all(parts, 'leaf', 0, 0, tiled=True, axis_index_groups=second)]
    ppermute x1, starting transfers between devices: 5.2 us -> 4.48 us  [shards(): got = lax.ppermute(sent, 'seq', [(i, i ^ 1) for i in range(seqs)])]
  transfers between devices with their start and end apart: 2 -> 2, of which waited for: 2 -> 1; matrix products, arithmetic and copies ran while one was open for 2% -> 2% of each run, Pallas kernels for 4% -> 5%
where the time goes in v11:
time: 58.7 us; the launch traced here: 57.6 us
  blocking collectives  28.9 us (49%)
  starting transfers between devices  17.4 us (30%)
  Pallas kernels  7.03 us (12%)
  local copies, waits for them, and re-layouts  3.14 us (5%)
  waiting for transfers between devices  1.01 us (2%)
    all_to_all x1, blocking collectives, gather_shared(): lax.all_to_all(parts, 'leaf', 0, 0, tiled=True, axis_index_groups=second)  17.5 us
    all_to_all x1, starting transfers between devices, gather_shared(): lax.all_to_all(own, 'leaf', 0, 0, tiled=True, axis_index_groups=first)  12.9 us
    all_to_all x1, blocking collectives, shards(): lax.all_to_all(parts, 'seq', 0, 0, tiled=True, axis_index_groups=chips)  11.5 us
    ppermute x1, starting transfers between devices, shards(): got = lax.ppermute(sent, 'seq', [(i, i ^ 1) for i in range(seqs)])  4.48 us
    pallas_call x1, Pallas kernels, shards(): pl.pallas_call(functools.partial(early_kernel, steps), out_shape=(jax.Sha...  2.62 us
    unnamed x8, local copies, waits for them, and re-layouts  2.04 us
    pallas_call x1, Pallas kernels, shards(): pl.pallas_call(post_kernel, out_shape=jax.ShapeDtypeStruct((Z // STRIDE,...  1.49 us
    pallas_call x1, Pallas kernels, shards(): pl.pallas_call(late_kernel, out_shape=(jax.ShapeDtypeStruct(wire.shape, j...  1.43 us
  transfers between devices with their start and end apart: 2, of which 1 were waited for; matrix products, arithmetic and copies ran while one was open for 2% of the time, Pallas kernels for 5%

profile of v11, /device:TPU:1, one launch (start us, length us, event | category | flops | bytes accessed | tf_op | source)
XLA Modules:
  0.0 57.6 jit_solution(7130842737178860832)
XLA Ops:
  0.0 1.5 %shard_map.55 = bf16[4,32,512]{2,1,0:T(8,128)(2,1)} custom-call(s32[16]{0:T(128)} %lengths_hbm.3, bf16[2,16,16,512]{3,2,1,0:T(8,128)(2,1)} %node_hbm.3), custom_call_target="tpu_custom_call" | custom-call | tf_op jit(solution)/shard_map/pallas_call | solution.py:337
  1.5 12.9 %all-to-all-start = ((bf16[4,32,512]{2,1,0:T(8,128)(2,1)}), bf16[4,32,512]{2,1,0:T(8,128)(2,1)S(1)}, u32[]{:S(2)}, u32[]{:S(2)}) async-start(bf16[4,32,512]{2,1,0:T(8,128)(2,1)} %shard_map.55), calls=%async_computation | async-start | bytes 262144 | tf_op jit(solution)/shard_map/all_to_all | solution.py:317
  14.4 1.1 %copy.8 = bf16[4,8,4096]{2,1,0:T(8,128)(2,1)S(1)} copy(bf16[4,8,4096]{2,0,1:T(4,128)(2,1)} %bitcast.7) | data formatting | bytes 524288 | tf_op jit(solution)/shard_map/transpose | solution.py:349
  15.5 2.6 %shard_map.56 = (f32[2,6,256,256]{3,2,1,0:T(8,128)S(1)}, f32[2,256,256]{2,1,0:T(8,128)S(1)}, bf16[1792,512]{1,0:T(8,128)(2,1)S(1)}, f32[8,512]{1,0:T(8,128)S(1)}) custom-call(s32[16]{0:T(128)} %lengths_hbm.3, s32[8,10]{1,0:T(8,128)} %anc_hbm.1, bf16[2,1280,512]{2,1,0:T(8,128)(2,1)} %prompt_hbm.1, bf16[2,16,16,512]{3,2,1,0:T(8,128)(2,1)} %node_hbm.3, ...), custom_call_target="tpu_custom_call" | custom-call | flops 500000000 | bytes 6000000 | tf_op jit(solution)/shard_map/pallas_call | solution.py:352
  18.2 0.0 copy-start
  18.2 1.2 %copy-done = bf16[1792,512]{1,0:T(8,128)(2,1)} copy-done((bf16[1792,512]{1,0:T(8,128)(2,1)}, bf16[1792,512]{1,0:T(8,128)(2,1)S(1)}, u32[]{:S(2)}) %copy-start) | copy-done | bytes 1835032
  19.4 0.0 copy-start.2
  19.4 0.8 %copy-done.2 = f32[2,256,256]{2,1,0:T(8,128)} copy-done((f32[2,256,256]{2,1,0:T(8,128)}, f32[2,256,256]{2,1,0:T(8,128)S(1)}, u32[]{:S(2)}) %copy-start.2) | copy-done | bytes 524312
  20.2 0.0 all-to-all-done.plane_ref
  20.2 0.0 copy-start.1
  20.2 0.0 copy-start.3
  20.2 0.1 shard_map.57
  20.3 17.5 %all_to_all.15 = bf16[8,4,32,512]{3,2,1,0:T(8,128)(2,1)S(1)} all-to-all(bf16[8,4,32,512]{3,2,1,0:T(8,128)(2,1)S(1)} %shard_map.57), channel_id=1, replica_groups={{16,17,24,25,0,1,8,9},{18,19,26,27,2,3,10,11},{20,21,28,29,4,5,12,13},{..., dimensions={0} | all-to-all | bytes 2097152 | tf_op jit(solution)/shard_map/all_to_all | solution.py:325
  37.8 0.0 copy-done.1
  37.8 0.0 copy-done.3
  37.8 1.4 %shard_map.58 = (f32[8,16,640]{2,1,0:T(8,128)S(1)}, s16[8,16,640]{2,1,0:T(8,128)(2,1)S(1)}) custom-call(bf16[32,32,512]{2,1,0:T(8,128)(2,1)S(1)} %bitcast.5, f32[2,6,256,256]{3,2,1,0:T(8,128)S(1)} %get-tuple-element.12.w_ref, f32[2,256,256]{2,1,0:T(8,128)S(1)} %copy-done.3, bf16[1792,512]{1,0:T(8,128)(2,1)S(1)} %copy-done.1, ...), custom_call_target="tpu_custom_call" | custom-call | tf_op jit(solution)/shard_map/pallas_call | solution.py:376
  39.2 4.5 %collective-permute-start = (s16[8,16,640]{2,1,0:T(8,128)(2,1)S(1)}, s16[8,16,640]{2,1,0:T(8,128)(2,1)S(1)}, u32[]{:S(2)}, u32[]{:S(2)}) collective-permute-start(s16[8,16,640]{2,1,0:T(8,128)(2,1)S(1)} %get-tuple-element.16), channel_id=1, source_target_pairs={{0,32},{32,0},{64,96},{96,64},{128,160},{160,128},{192,224},{224,1... | collective-permute-start | bytes 491528 | tf_op jit(solution)/shard_map/ppermute | solution.py:384
  43.7 1.0 %collective-permute-done.other_ref = s16[8,16,640]{2,1,0:T(8,128)(2,1)S(1)} collective-permute-done((s16[8,16,640]{2,1,0:T(8,128)(2,1)S(1)}, s16[8,16,640]{2,1,0:T(8,128)(2,1)S(1)}, u32[]{:S(2)}, u32[]{:S(2)}) %collective-permute-start) | collective-permute-done | bytes 163872 | tf_op jit(solution)/shard_map/ppermute | solution.py:384
  44.7 0.5 shard_map.59
  45.2 11.5 %all_to_all.16.parts_ref = s16[8,16,640]{2,1,0:T(8,128)(2,1)S(1)} all-to-all(s16[8,16,640]{2,1,0:T(8,128)(2,1)S(1)} %shard_map.59), channel_id=1, replica_groups={{384,448,0,64,128,192,256,320},{416,480,32,96,160,224,288,352},{385,449..., dimensions={0} | all-to-all | bytes 327680 | tf_op jit(solution)/shard_map/all_to_all | solution.py:393
  56.7 0.9 %shard_map.60 = bf16[8,4,256]{2,1,0:T(4,128)(2,1)} custom-call(s16[8,16,640]{2,1,0:T(8,128)(2,1)S(1)} %all_to_all.16.parts_ref), custom_call_target="tpu_custom_call" | custom-call | tf_op jit(solution)/shard_map/pallas_call | solution.py:394
Async XLA Ops:
  1.5 18.7 %all-to-all-start = ((bf16[4,32,512]{2,1,0:T(8,128)(2,1)}), bf16[4,32,512]{2,1,0:T(8,128)(2,1)S(1)}, u32[]{:S(2)}, u32[]{:S(2)}) async-start(bf16[4,32,512]{2,1,0:T(8,128)(2,1)} %shard_map.55), calls=%async_computation | async-start | bytes 262144 | tf_op jit(solution)/shard_map/all_to_all | solution.py:317
  18.2 1.2 %copy-start = (bf16[1792,512]{1,0:T(8,128)(2,1)}, bf16[1792,512]{1,0:T(8,128)(2,1)S(1)}, u32[]{:S(2)}) copy-start(bf16[1792,512]{1,0:T(8,128)(2,1)S(1)} %get-tuple-element.14.half_ref) | copy-start | bytes 5505028
  19.4 0.8 %copy-start.2 = (f32[2,256,256]{2,1,0:T(8,128)}, f32[2,256,256]{2,1,0:T(8,128)S(1)}, u32[]{:S(2)}) copy-start(f32[2,256,256]{2,1,0:T(8,128)S(1)} %get-tuple-element.13.row_ref) | copy-start | bytes 1572868
  20.2 17.5 %copy-start.1 = (bf16[1792,512]{1,0:T(8,128)(2,1)S(1)}, bf16[1792,512]{1,0:T(8,128)(2,1)}, u32[]{:S(2)}) copy-start(bf16[1792,512]{1,0:T(8,128)(2,1)} %copy-done) | copy-start | bytes 5505028
  20.2 17.5 %copy-start.3 = (f32[2,256,256]{2,1,0:T(8,128)S(1)}, f32[2,256,256]{2,1,0:T(8,128)}, u32[]{:S(2)}) copy-start(f32[2,256,256]{2,1,0:T(8,128)} %copy-done.2) | copy-start | bytes 1572868
  39.2 5.5 %collective-permute-start = (s16[8,16,640]{2,1,0:T(8,128)(2,1)S(1)}, s16[8,16,640]{2,1,0:T(8,128)(2,1)S(1)}, u32[]{:S(2)}, u32[]{:S(2)}) collective-permute-start(s16[8,16,640]{2,1,0:T(8,128)(2,1)S(1)} %get-tuple-element.16), channel_id=1, source_target_pairs={{0,32},{32,0},{64,96},{96,64},{128,160},{160,128},{192,224},{224,1... | collective-permute-start | bytes 491528 | tf_op jit(solution)/shard_map/ppermute | solution.py:384

commit v12 on v11

--- a/solution.py
+++ b/solution.py
@@ -16,6 +16,7 @@
 Z = 8
 STRIDE = 2
 FIRST_Z, FIRST_X, FIRST_CHIP = 2, 2, 6
+WAITING_Z = 4
 INVALID_KEY = 256.0
 TOP = 32767.0
 POINTS = (2.0**18, 2.0**26, 2.0**23)
@@ -50,8 +51,8 @@
 
 def group_query(q_ref, k):
     heads = range(k * GROUP, (k + 1) * GROUP)
-    query = jnp.concatenate([q_ref[:, h * HEAD_DIM : (h + 1) * HEAD_DIM] for h in heads], axis=0)
-    return query * jnp.bfloat16(1.0 / 16.0)
+    pieces = [q_ref[:, step, h * HEAD_DIM : (h + 1) * HEAD_DIM] for h in heads for step in range(q_ref.shape[1])]
+    return (jnp.concatenate(pieces, axis=0) * (1.0 / 16.0)).astype(jnp.bfloat16)
 
 
 def dot_nt(a, b):
@@ -65,7 +66,13 @@
     return copies
 
 
-def post_kernel(lengths_hbm, node_hbm, out_ref, node_ref, lengths_ref, sems):
+def waits():
+    return lax.rem(lax.axis_index("leaf"), Z) < WAITING_Z
+
+
+def first_kernel(inputs, outputs, scratch):
+    lengths_hbm, node_hbm = inputs[0], inputs[3]
+    out_ref, (node_ref, lengths_ref, sems) = outputs[0], scratch[:3]
     node_slots = lengths_hbm.shape[0]
     tokens = node_ref.shape[1]
     for copy in fetch([(node_hbm.at[:, node_slots - 1], node_ref), (lengths_hbm, lengths_ref)], sems):
@@ -77,20 +84,27 @@
         out_ref[copy, 0:tokens] = keys
         out_ref[copy, tokens : 2 * tokens] = values
 
-
-def copies_kernel(plane_ref, early_ref, out_ref):
-    del early_ref
+    @pl.when(waits())
+    def _():
+        early_work(*inputs, *outputs[1:], *scratch[3:])
+
+
+def second_kernel(inputs, outputs, scratch):
+    part_ref, out_ref = inputs[0], outputs[0]
     for copy in range(out_ref.shape[0]):
-        out_ref[copy] = plane_ref[...]
-
-
-def early_kernel(
-    steps,
+        out_ref[copy] = part_ref[...]
+
+    @pl.when(jnp.logical_not(waits()))
+    def _():
+        early_work(*inputs[1:], *outputs[1:], *scratch)
+
+
+def early_work(
     lengths_hbm,
     anc_hbm,
     prompt_hbm,
     node_hbm,
-    q_ref,
+    q_hbm,
     w_ref,
     row_ref,
     half_ref,
@@ -99,12 +113,15 @@
     anc_ref,
     prompt_ref,
     node_ref,
+    q_raw_ref,
+    q_ref,
     sems,
 ):
     copies = fetch(
         [
             (lengths_hbm, lengths_ref),
             (anc_hbm, anc_ref),
+            (q_hbm, q_raw_ref),
             (node_hbm.at[0], node_ref),
             (prompt_hbm.at[0], prompt_ref),
             (prompt_hbm.at[1], half_ref.at[pl.ds(0, prompt_ref.shape[0])]),
@@ -115,11 +132,14 @@
         ],
         sems,
     )
-    leaf_count, level_count = anc_ref.shape
+    level_count = anc_ref.shape[1]
+    steps = q_ref.shape[1]
     node_slots, tokens, width = node_ref.shape
     node_cols = node_slots * tokens
     prompt_cols = prompt_ref.shape[0]
     shared_cols = count_ref.shape[1]
+    copies[2].wait()
+    q_ref[...] = q_raw_ref[...].astype(jnp.float32)
     for k in range(KV_HEADS):
         half_ref[prompt_cols + node_cols :, k * HEAD_DIM : (k + 1) * HEAD_DIM] = group_query(q_ref, k)
     copies[0].wait()
@@ -145,8 +165,8 @@
         causal = jnp.where(position <= length - steps + step, 1.0, 0.0)
         mult.append(jnp.where(position < length, upper + own * causal, 0.0))
     mult = tall(jnp.concatenate(mult, axis=0), GROUP)
-    copies[2].wait()
     copies[3].wait()
+    copies[4].wait()
 
     for k in range(KV_HEADS):
         cols = slice(k * HEAD_DIM, (k + 1) * HEAD_DIM)
@@ -171,11 +191,23 @@
         total = total + fold(w, jnp.add)
         row_ref[k, :, LANES:] = jnp.broadcast_to(jnp.sum(total, axis=1, keepdims=True), total.shape)
         row_ref[k, :, :LANES] = jnp.broadcast_to(top, total.shape)
-    for copy in copies[4:]:
+    for copy in copies[5:]:
         copy.wait()
 
 
-def late_kernel(shared_ref, w_ref, row_ref, half_ref, count_ref, own_ref, out_ref):
+def late_kernel(shared_ref, *refs):
+    sets, outputs = (refs[:4], refs[4:8]), refs[8:]
+
+    @pl.when(waits())
+    def _():
+        late_work(shared_ref, *sets[0], *outputs)
+
+    @pl.when(jnp.logical_not(waits()))
+    def _():
+        late_work(shared_ref, *sets[1], *outputs)
+
+
+def late_work(shared_ref, w_ref, row_ref, half_ref, count_ref, own_ref, out_ref):
     owners = shared_ref.shape[0]
     tokens = shared_ref.shape[1] // 2
     shared_cols = owners * tokens
@@ -310,20 +342,11 @@
     return owner
 
 
-def gather_shared(own, owners, early):
+def gather_groups(owners):
     along_z, along_x = gather_orders(owners)
     first = [[x + z + k for k in along_z] for x in range(0, owners, Z) for z in range(STRIDE)]
     second = [[x + z + k for x in along_x for k in range(STRIDE)] for z in range(0, Z, STRIDE)]
-    part = lax.all_to_all(own, "leaf", 0, 0, tiled=True, axis_index_groups=first)
-    parts = pl.pallas_call(
-        copies_kernel,
-        out_shape=jax.ShapeDtypeStruct((len(second[0]),) + part.shape, part.dtype),
-        in_specs=[VMEM, VMEM],
-        out_specs=VMEM,
-        compiler_params=params(8),
-    )(part, early)
-    shared = lax.all_to_all(parts, "leaf", 0, 0, tiled=True, axis_index_groups=second)
-    return shared.reshape((owners,) + own.shape[1:])
+    return first, second
 
 
 def shards(queries, prompt_kv, node_kv, node_lengths, ancestors):
@@ -334,52 +357,72 @@
     rows = steps * leaf_count
     owners = lax.axis_size("leaf")
 
-    own = pl.pallas_call(
-        post_kernel,
-        out_shape=jax.ShapeDtypeStruct((Z // STRIDE, 2 * tokens, width), jnp.bfloat16),
-        in_specs=[HBM, HBM],
-        out_specs=VMEM,
-        scratch_shapes=[
+    first, second = gather_groups(owners)
+    early_cols = prompt_cols + node_slots * tokens
+    assert prompt_cols % CHUNK == 0 and node_slots * tokens == CHUNK and GROUP * rows == CHUNK
+    arrays = in_hbm(node_lengths, ancestors, prompt_kv, node_kv, queries)
+    early_shapes = (
+        jax.ShapeDtypeStruct((KV_HEADS, early_cols // CHUNK, CHUNK, CHUNK), jnp.float32),
+        jax.ShapeDtypeStruct((KV_HEADS, GROUP * rows, 2 * LANES), jnp.float32),
+        jax.ShapeDtypeStruct((early_cols + GROUP * rows, width), jnp.bfloat16),
+        jax.ShapeDtypeStruct((leaf_count, owners * tokens), jnp.float32),
+    )
+    early_scratch = [
+        pltpu.SMEM((node_slots,), jnp.int32),
+        pltpu.VMEM(ancestors.shape, jnp.int32),
+        pltpu.VMEM((prompt_cols, width), jnp.bfloat16),
+        pltpu.VMEM((node_slots, tokens, width), jnp.bfloat16),
+        pltpu.VMEM(queries.shape, jnp.bfloat16),
+        pltpu.VMEM(queries.shape, jnp.float32),
+        pltpu.SemaphoreType.DMA((6 + node_slots,)),
+    ]
+
+    def stage_kernel(body, out_shape, scratch, *operands):
+        ins, outs = len(operands), 1 + len(early_shapes)
+
+        def kernel(*refs):
+            body(refs[:ins], refs[ins : ins + outs], refs[ins + outs :])
+
+        return pl.pallas_call(
+            kernel,
+            out_shape=(out_shape, *early_shapes),
+            in_specs=[VMEM] * (ins - len(arrays)) + [HBM] * len(arrays),
+            out_specs=(VMEM,) * outs,
+            scratch_shapes=scratch,
+            compiler_params=params(24),
+        )(*operands)
+
+    own, *before = stage_kernel(
+        first_kernel,
+        jax.ShapeDtypeStruct((len(first[0]), 2 * tokens, width), jnp.bfloat16),
+        [
             pltpu.VMEM((2, tokens, width), jnp.bfloat16),
             pltpu.SMEM((node_slots,), jnp.int32),
             pltpu.SemaphoreType.DMA((2,)),
+            *early_scratch,
         ],
-        compiler_params=params(8),
-    )(*in_hbm(node_lengths, node_kv))
-    query_rows = queries.transpose(1, 0, 2).reshape(rows, feat_width)
-    early_cols = prompt_cols + node_slots * tokens
-    assert prompt_cols % CHUNK == 0 and node_slots * tokens == CHUNK and GROUP * rows == CHUNK
-    early, early_rows, halves, count = pl.pallas_call(
-        functools.partial(early_kernel, steps),
-        out_shape=(
-            jax.ShapeDtypeStruct((KV_HEADS, early_cols // CHUNK, CHUNK, CHUNK), jnp.float32),
-            jax.ShapeDtypeStruct((KV_HEADS, GROUP * rows, 2 * LANES), jnp.float32),
-            jax.ShapeDtypeStruct((early_cols + GROUP * rows, width), jnp.bfloat16),
-            jax.ShapeDtypeStruct((leaf_count, owners * tokens), jnp.float32),
-        ),
-        in_specs=[HBM, HBM, HBM, HBM, VMEM],
-        out_specs=(VMEM,) * 4,
-        scratch_shapes=[
-            pltpu.SMEM((node_slots,), jnp.int32),
-            pltpu.VMEM(ancestors.shape, jnp.int32),
-            pltpu.VMEM((prompt_cols, width), jnp.bfloat16),
-            pltpu.VMEM((node_slots, tokens, width), jnp.bfloat16),
-            pltpu.SemaphoreType.DMA((5 + node_slots,)),
-        ],
-        compiler_params=params(16),
-        cost_estimate=pl.CostEstimate(flops=500_000_000, bytes_accessed=6_000_000, transcendentals=800_000),
-    )(*in_hbm(node_lengths, ancestors, prompt_kv, node_kv), query_rows)
-
-    shared = gather_shared(own, owners, count)
+        *arrays,
+    )
+    part = lax.all_to_all(own, "leaf", 0, 0, tiled=True, axis_index_groups=first)
+    part_copies, *after = stage_kernel(
+        second_kernel,
+        jax.ShapeDtypeStruct((len(second[0]),) + part.shape, part.dtype),
+        early_scratch,
+        part,
+        *arrays,
+    )
+    shared = lax.all_to_all(part_copies, "leaf", 0, 0, tiled=True, axis_index_groups=second)
+    shared = shared.reshape(owners, 2 * tokens, width)
+
     seqs = lax.axis_size("seq")
     wire = jax.ShapeDtypeStruct((HEADS // 2, rows // 2, 2 * HEAD_DIM + LANES), jnp.int16)
     kept, sent = pl.pallas_call(
         late_kernel,
         out_shape=(jax.ShapeDtypeStruct(wire.shape, jnp.float32), wire),
-        in_specs=[VMEM] * 5,
+        in_specs=[VMEM] * 9,
         out_specs=(VMEM, VMEM),
         compiler_params=params(16),
-    )(shared, early, early_rows, halves, count)
+    )(shared, *before, *after)
 
     got = lax.ppermute(sent, "seq", [(i, i ^ 1) for i in range(seqs)])
     parts = pl.pallas_call(

time: 58.7 us -> 55.5 us (0.945)
  blocking collectives: 28.9 us -> 41.5 us
  starting transfers between devices: 17.4 us -> 5.32 us
  local copies, waits for them, and re-layouts: 3.14 us -> 0 us
    all_to_all x1 -> x0, starting transfers between devices: 12.9 us -> none  [gather_shared(): lax.all_to_all(own, 'leaf', 0, 0, tiled=True, axis_index_groups=first)]
    all_to_all x1 -> x2, blocking collectives: 17.5 us -> 30.1 us  [the longest x1 17.1 us: shards(): lax.all_to_all(part_copies, 'leaf', 0, 0, tiled=True, axis_index_groups=s...]
    unnamed x8 -> x0, local copies, waits for them, and re-layouts: 2.04 us -> none
    transpose x1 -> x0, local copies, waits for them, and re-layouts: 1.1 us -> none  [shards(): query_rows = queries.transpose(1, 0, 2).reshape(rows, feat_width)]
    ppermute x1, starting transfers between devices: 4.48 us -> 5.32 us  [shards(): got = lax.ppermute(sent, 'seq', [(i, i ^ 1) for i in range(seqs)])]
    pallas_call x3 -> x2, Pallas kernels: 4.18 us -> 3.8 us  [stage_kernel(): pl.pallas_call(kernel, out_shape=(out_shape, *early_shapes), in_specs=[VM...]
  transfers between devices with their start and end apart: 2 -> 1, of which waited for: 1 -> 1; matrix products, arithmetic and copies ran while one was open for 2% -> 0% of each run, Pallas kernels for 5% -> 0%
where the time goes in v12:
time: 55.5 us; the launch traced here: 54.5 us
  blocking collectives  41.5 us (75%)
  Pallas kernels  6.64 us (12%)
  starting transfers between devices  5.32 us (10%)
  waiting for transfers between devices  1.01 us (2%)
    all_to_all x1, blocking collectives, shards(): lax.all_to_all(part_copies, 'leaf', 0, 0, tiled=True, axis_index_groups=s...  17.1 us
    all_to_all x1, blocking collectives, shards(): lax.all_to_all(own, 'leaf', 0, 0, tiled=True, axis_index_groups=first)  13 us
    all_to_all x1, blocking collectives, shards(): lax.all_to_all(parts, 'seq', 0, 0, tiled=True, axis_index_groups=chips)  11.4 us
    ppermute x1, starting transfers between devices, shards(): got = lax.ppermute(sent, 'seq', [(i, i ^ 1) for i in range(seqs)])  5.32 us
    pallas_call x2, Pallas kernels, stage_kernel(): pl.pallas_call(kernel, out_shape=(out_shape, *early_shapes), in_specs=[VM...  3.8 us
    pallas_call x1, Pallas kernels, shards(): pl.pallas_call(late_kernel, out_shape=(jax.ShapeDtypeStruct(wire.shape, j...  1.43 us
  transfers between devices with their start and end apart: 1, of which 1 were waited for; matrix products, arithmetic and copies ran while one was open for 0% of the time, Pallas kernels for 0%

profile of v12, /device:TPU:1, one launch (start us, length us, event | category | flops | bytes accessed | tf_op | source)
XLA Modules:
  0.0 54.5 jit_solution(10490663108233502070)
XLA Ops:
  0.0 3.5 %shard_map.55 = (bf16[4,32,512]{2,1,0:T(8,128)(2,1)S(1)}, f32[2,6,256,256]{3,2,1,0:T(8,128)S(1)}, f32[2,256,256]{2,1,0:T(8,128)S(1)}, bf16[1792,512]{1,0:T(8,128)(2,1)S(1)}, f32[8,512]{1,0:T(8,128)S(1)}) custom-call(s32[16]{0:T(128)} %refs_1_.3, s32[8,10]{1,0:T(8,128)} %refs_2_.3, bf16[2,1280,512]{2,1,0:T(8,128)(2,1)} %refs_3_.3, ...), custom_call_target="tpu_custom_call" | custom-call | tf_op jit(solution)/shard_map/pallas_call | solution.py:386
  3.5 13.0 %all_to_all.15.refs_0_ = bf16[4,32,512]{2,1,0:T(8,128)(2,1)S(1)} all-to-all(bf16[4,32,512]{2,1,0:T(8,128)(2,1)S(1)} %get-tuple-element.17), channel_id=1, replica_groups={{4,6,0,2},{5,7,1,3},{12,14,8,10},{13,15,9,11},{20,22,16,18},{21,23,17,1..., dimensions={0} | all-to-all | bytes 262144 | tf_op jit(solution)/shard_map/all_to_all | solution.py:406
  16.6 0.3 shard_map.56
  16.9 17.1 %all_to_all.16 = bf16[8,4,32,512]{3,2,1,0:T(8,128)(2,1)S(1)} all-to-all(bf16[8,4,32,512]{3,2,1,0:T(8,128)(2,1)S(1)} %get-tuple-element.18), channel_id=1, replica_groups={{16,17,24,25,0,1,8,9},{18,19,26,27,2,3,10,11},{20,21,28,29,4,5,12,13},{..., dimensions={0} | all-to-all | bytes 2097152 | tf_op jit(solution)/shard_map/all_to_all | solution.py:414
  33.9 1.4 %shard_map.57 = (f32[8,16,640]{2,1,0:T(8,128)S(1)}, s16[8,16,640]{2,1,0:T(8,128)(2,1)S(1)}) custom-call(bf16[32,32,512]{2,1,0:T(8,128)(2,1)S(1)} %bitcast.1, f32[2,6,256,256]{3,2,1,0:T(8,128)S(1)} %get-tuple-element.19.refs_0_, f32[2,256,256]{2,1,0:T(8,128)S(1)} %get-tuple-element.20.refs_1_, bf16[1792,512]{1,0:T(8,128)(2,1)S(1)} %get-tuple-element.21.refs_2_, ...), custom_call_target="tpu_custom_call" | custom-call | tf_op jit(solution)/shard_map/pallas_call | solution.py:419
  35.4 5.3 %collective-permute-start = (s16[8,16,640]{2,1,0:T(8,128)(2,1)S(1)}, s16[8,16,640]{2,1,0:T(8,128)(2,1)S(1)}, u32[]{:S(2)}, u32[]{:S(2)}) collective-permute-start(s16[8,16,640]{2,1,0:T(8,128)(2,1)S(1)} %get-tuple-element.28), channel_id=1, source_target_pairs={{0,32},{32,0},{64,96},{96,64},{128,160},{160,128},{192,224},{224,1... | collective-permute-start | bytes 491528 | tf_op jit(solution)/shard_map/ppermute | solution.py:427
  40.7 1.0 %collective-permute-done.other_ref = s16[8,16,640]{2,1,0:T(8,128)(2,1)S(1)} collective-permute-done((s16[8,16,640]{2,1,0:T(8,128)(2,1)S(1)}, s16[8,16,640]{2,1,0:T(8,128)(2,1)S(1)}, u32[]{:S(2)}, u32[]{:S(2)}) %collective-permute-start) | collective-permute-done | bytes 163872 | tf_op jit(solution)/shard_map/ppermute | solution.py:427
  41.7 0.5 shard_map.58
  42.2 11.4 %all_to_all.17.parts_ref = s16[8,16,640]{2,1,0:T(8,128)(2,1)S(1)} all-to-all(s16[8,16,640]{2,1,0:T(8,128)(2,1)S(1)} %shard_map.58), channel_id=1, replica_groups={{384,448,0,64,128,192,256,320},{416,480,32,96,160,224,288,352},{385,449..., dimensions={0} | all-to-all | bytes 327680 | tf_op jit(solution)/shard_map/all_to_all | solution.py:436
  53.6 0.9 %shard_map.59 = bf16[8,4,256]{2,1,0:T(4,128)(2,1)} custom-call(s16[8,16,640]{2,1,0:T(8,128)(2,1)S(1)} %all_to_all.17.parts_ref), custom_call_target="tpu_custom_call" | custom-call | tf_op jit(solution)/shard_map/pallas_call | solution.py:437
Async XLA Ops:
  35.4 6.3 %collective-permute-start = (s16[8,16,640]{2,1,0:T(8,128)(2,1)S(1)}, s16[8,16,640]{2,1,0:T(8,128)(2,1)S(1)}, u32[]{:S(2)}, u32[]{:S(2)}) collective-permute-start(s16[8,16,640]{2,1,0:T(8,128)(2,1)S(1)} %get-tuple-element.28), channel_id=1, source_target_pairs={{0,32},{32,0},{64,96},{96,64},{128,160},{160,128},{192,224},{224,1... | collective-permute-start | bytes 491528 | tf_op jit(solution)/shard_map/ppermute | solution.py:427

commit v13 on v12

--- a/solution.py
+++ b/solution.py
@@ -19,6 +19,7 @@
 WAITING_Z = 4
 INVALID_KEY = 256.0
 TOP = 32767.0
+STATS = 32
 POINTS = (2.0**18, 2.0**26, 2.0**23)
 
 VMEM = pl.BlockSpec(memory_space=pltpu.VMEM)
@@ -212,7 +213,8 @@
     tokens = shared_ref.shape[1] // 2
     shared_cols = owners * tokens
     rows = w_ref.shape[2] // GROUP
-    half = rows // 2
+    steps = rows // count_ref.shape[0]
+    leaf_count = rows // steps
     chunks = w_ref.shape[1]
     early_cols = chunks * CHUNK
     count = count_ref[...]
@@ -248,21 +250,27 @@
                 kept.append(jnp.where(core == 0, even, odd))
                 sent.append(jnp.where(core == 0, odd, even))
             slot = (k * (GROUP // 2) + pair - FIRST_CHIP) % (HEADS // 2)
-            lane = lax.broadcasted_iota(jnp.int32, (half, LANES), 1)
-            stats = [jnp.where(lane % (LANES // 2) == 0, kept[1][i : i + half], kept[2][i : i + half]) for i in (0, half)]
-            own_ref[slot, :, 2 * HEAD_DIM :] = jnp.where(lane < LANES // 2, stats[0], stats[1])
-            own_ref[slot, :, 0:HEAD_DIM] = kept[0][:half]
-            own_ref[slot, :, HEAD_DIM : 2 * HEAD_DIM] = kept[0][half:]
+            lane = lax.broadcasted_iota(jnp.int32, (rows, LANES), 1)
             data, fixed = to_wire(*sent)
-            out_ref[slot, :, 0:HEAD_DIM] = data[:half]
-            out_ref[slot, :, HEAD_DIM : 2 * HEAD_DIM] = data[half:]
-            out_ref[slot, :, 2 * HEAD_DIM :] = jnp.where(lane < LANES // 2, fixed[:half], fixed[half:]).astype(jnp.int16)
+            put(own_ref, slot, steps, kept[0], jnp.where(lane % STATS == 0, kept[1], kept[2]))
+            put(out_ref, slot, steps, data, fixed)
+
+
+def put(ref, slot, steps, data, stats):
+    leaf_count = data.shape[0] // steps
+    group = lax.broadcasted_iota(jnp.int32, (leaf_count, LANES), 1) // STATS
+    joint = stats[:leaf_count]
+    for step in range(steps):
+        rows = slice(step * leaf_count, (step + 1) * leaf_count)
+        ref[slot, :, step * HEAD_DIM : (step + 1) * HEAD_DIM] = data[rows]
+        joint = jnp.where(group == step, stats[rows], joint)
+    ref[slot, :, steps * HEAD_DIM :] = joint.astype(ref.dtype)
 
 
 def to_wire(acc, block_max, total):
     reach = jnp.maximum(jnp.max(fold(jnp.abs(acc), jnp.maximum), axis=1, keepdims=True), 1e-30)
     data = jnp.round(acc * (TOP / reach)).astype(jnp.int32).astype(jnp.int16)
-    lane = lax.broadcasted_iota(jnp.int32, block_max.shape, 1) % (LANES // 2)
+    lane = lax.broadcasted_iota(jnp.int32, block_max.shape, 1) % STATS
     log_total = jnp.log(total) * POINTS[1]
     log_reach = jnp.log(reach) * POINTS[2]
     value = jnp.where(lane < 2, block_max * POINTS[0], jnp.where(lane < 4, log_total, log_reach))
@@ -270,57 +278,61 @@
     return data, jnp.where(lane % 2 == 0, value >> 16, (value & 0xFFFF) - 0x8000)
 
 
-def from_wire(stats, first, i):
-    high = stats[:, first + 2 * i : first + 2 * i + 1]
-    low = stats[:, first + 2 * i + 1 : first + 2 * i + 2] + 0x8000
-    return ((high << 16) + low).astype(jnp.float32) * (1.0 / POINTS[i])
+def from_wire(stats):
+    lane = lax.broadcasted_iota(jnp.int32, stats.shape, 1) % STATS
+    unit = jnp.where(lane < 2, 1.0 / POINTS[0], jnp.where(lane < 4, 1.0 / POINTS[1], 1.0 / POINTS[2]))
+    return ((stats << 16) + (pltpu.roll(stats, LANES - 1, 1) + 0x8000)).astype(jnp.float32) * unit
+
+
+def factors(values, top):
+    lane = lax.broadcasted_iota(jnp.int32, values.shape, 1) % STATS
+    shift = values - top
+    return jnp.exp(values + jnp.where(lane == 2, pltpu.roll(shift, 2, 1), pltpu.roll(shift, 4, 1)))
 
 
 def pair_kernel(own_ref, other_ref, out_ref):
-    slots, half, lanes = own_ref.shape
-    rows = slots * half
-    own_stats = own_ref[:, :, 2 * HEAD_DIM :].reshape(rows, LANES)
-    other_stats = other_ref[:, :, 2 * HEAD_DIM :].reshape(rows, LANES).astype(jnp.int32)
-    fixed = []
-    for part in range(2):
-        first = part * LANES // 2
-        span = slice(part * HEAD_DIM, (part + 1) * HEAD_DIM)
-        own_max, own_total = own_stats[:, first : first + 1], own_stats[:, first + 1 : first + 2]
-        other_max = from_wire(other_stats, first, 0)
-        top = jnp.maximum(own_max, other_max)
-        own_scale = jnp.exp(own_max - top)
-        shift = other_max - top
-        total = own_total * own_scale + jnp.exp(shift + from_wire(other_stats, first, 1))
-        other = other_ref[:, :, span].reshape(rows, HEAD_DIM).astype(jnp.int32).astype(jnp.float32)
-        acc = own_ref[:, :, span].reshape(rows, HEAD_DIM) * own_scale
-        acc = acc + other * (jnp.exp(shift + from_wire(other_stats, first, 2)) * (1.0 / TOP))
-        shape = (rows, LANES)
-        data, stats = to_wire(acc, jnp.broadcast_to(top, shape), jnp.broadcast_to(total, shape))
-        out_ref[:, :, span] = data.reshape(slots, half, HEAD_DIM)
-        fixed.append(stats)
-    lane = lax.broadcasted_iota(jnp.int32, (rows, LANES), 1)
-    stats = jnp.where(lane < LANES // 2, fixed[0], fixed[1]).astype(jnp.int16)
-    out_ref[:, :, 2 * HEAD_DIM :] = stats.reshape(slots, half, LANES)
+    slots, leaf_count, lanes = own_ref.shape
+    steps = lanes // HEAD_DIM
+    rows = slots * leaf_count
+    shape = (rows, LANES)
+    own = own_ref[:, :, steps * HEAD_DIM :].reshape(shape)
+    other = from_wire(other_ref[:, :, steps * HEAD_DIM :].astype(jnp.int32).reshape(shape))
+    top = jnp.maximum(own, other)
+    own_scale = jnp.exp(own - top)
+    other_scale = factors(other, top)
+    total = own * pltpu.roll(own_scale, 2, 1) + other_scale
+    group = lax.broadcasted_iota(jnp.int32, shape, 1) // STATS
+    joint = jnp.zeros(shape, jnp.int32)
+    for step in range(steps):
+        first = step * STATS
+        span = slice(step * HEAD_DIM, (step + 1) * HEAD_DIM)
+        data = other_ref[:, :, span].astype(jnp.int32).reshape(rows, HEAD_DIM).astype(jnp.float32)
+        acc = own_ref[:, :, span].reshape(rows, HEAD_DIM) * own_scale[:, first : first + 1]
+        acc = acc + data * (other_scale[:, first + 4 : first + 5] * (1.0 / TOP))
+        data, stats = to_wire(
+            acc,
+            jnp.broadcast_to(top[:, first : first + 1], shape),
+            jnp.broadcast_to(total[:, first + 2 : first + 3], shape),
+        )
+        out_ref[:, :, span] = data.reshape(slots, leaf_count, HEAD_DIM)
+        joint = jnp.where(group == step, stats, joint)
+    out_ref[:, :, steps * HEAD_DIM :] = joint.astype(jnp.int16).reshape(slots, leaf_count, LANES)
 
 
 def merge_kernel(parts_ref, out_ref):
-    blocks, half, _ = parts_ref.shape
-    leaf_count = out_ref.shape[0]
-    stats = [parts_ref[b, :, 2 * HEAD_DIM :].astype(jnp.int32) for b in range(blocks)]
-    for part in range(2):
-        first = part * LANES // 2
-        tops = [from_wire(stats[b], first, 0) for b in range(blocks)]
-        row_max = functools.reduce(jnp.maximum, tops)
-        denominator = jnp.zeros((half, 1), jnp.float32)
-        numerator = jnp.zeros((half, HEAD_DIM), jnp.float32)
+    blocks = parts_ref.shape[0]
+    steps = out_ref.shape[1]
+    values = [from_wire(parts_ref[b, :, steps * HEAD_DIM :].astype(jnp.int32)) for b in range(blocks)]
+    row_max = functools.reduce(jnp.maximum, values)
+    scales = [factors(value, row_max) for value in values]
+    denominator = functools.reduce(jnp.add, scales) * TOP
+    for step in range(steps):
+        first = step * STATS
+        numerator = jnp.zeros((out_ref.shape[0], HEAD_DIM), jnp.float32)
         for b in range(blocks):
-            shift = tops[b] - row_max
-            denominator = denominator + jnp.exp(shift + from_wire(stats[b], first, 1))
-            data = parts_ref[b, :, part * HEAD_DIM : (part + 1) * HEAD_DIM].astype(jnp.int32).astype(jnp.float32)
-            numerator = numerator + jnp.exp(shift + from_wire(stats[b], first, 2)) * data
-        merged = (numerator / (denominator * TOP)).astype(jnp.bfloat16)
-        for i in range(half // leaf_count):
-            out_ref[:, part * half // leaf_count + i, :] = merged[i * leaf_count : (i + 1) * leaf_count]
+            data = parts_ref[b, :, step * HEAD_DIM : (step + 1) * HEAD_DIM].astype(jnp.int32).astype(jnp.float32)
+            numerator = numerator + scales[b][:, first + 4 : first + 5] * data
+        out_ref[:, step, :] = (numerator / denominator[:, first + 2 : first + 3]).astype(jnp.bfloat16)
 
 
 def turned(items, start):
@@ -415,7 +427,8 @@
     shared = shared.reshape(owners, 2 * tokens, width)
 
     seqs = lax.axis_size("seq")
-    wire = jax.ShapeDtypeStruct((HEADS // 2, rows // 2, 2 * HEAD_DIM + LANES), jnp.int16)
+    assert steps * STATS == LANES
+    wire = jax.ShapeDtypeStruct((HEADS // 2, leaf_count, steps * HEAD_DIM + LANES), jnp.int16)
     kept, sent = pl.pallas_call(
         late_kernel,
         out_shape=(jax.ShapeDtypeStruct(wire.shape, jnp.float32), wire),

time: 55.5 us -> 55.1 us (level)
  no operation moved by 1% of the time
where the time goes in v13:
time: 55.1 us; the launch traced here: 54.3 us
  blocking collectives  41.3 us (75%)
  Pallas kernels  6.66 us (12%)
  starting transfers between devices  5.32 us (10%)
  waiting for transfers between devices  0.99 us (2%)
    all_to_all x1, blocking collectives, shards(): lax.all_to_all(part_copies, 'leaf', 0, 0, tiled=True, axis_index_groups=s...  17.1 us
    all_to_all x1, blocking collectives, shards(): lax.all_to_all(own, 'leaf', 0, 0, tiled=True, axis_index_groups=first)  13 us
    all_to_all x1, blocking collectives, shards(): lax.all_to_all(parts, 'seq', 0, 0, tiled=True, axis_index_groups=chips)  11.1 us
    ppermute x1, starting transfers between devices, shards(): got = lax.ppermute(sent, 'seq', [(i, i ^ 1) for i in range(seqs)])  5.32 us
    pallas_call x2, Pallas kernels, stage_kernel(): pl.pallas_call(kernel, out_shape=(out_shape, *early_shapes), in_specs=[VM...  3.8 us
    pallas_call x1, Pallas kernels, shards(): pl.pallas_call(late_kernel, out_shape=(jax.ShapeDtypeStruct(wire.shape, j...  1.43 us
  transfers between devices with their start and end apart: 1, of which 1 were waited for; matrix products, arithmetic and copies ran while one was open for 0% of the time, Pallas kernels for 0%

profile of v13, /device:TPU:1, one launch (start us, length us, event | category | flops | bytes accessed | tf_op | source)
XLA Modules:
  0.0 54.3 jit_solution(6102903492659773142)
XLA Ops:
  0.0 3.5 %shard_map.55 = (bf16[4,32,512]{2,1,0:T(8,128)(2,1)S(1)}, f32[2,6,256,256]{3,2,1,0:T(8,128)S(1)}, f32[2,256,256]{2,1,0:T(8,128)S(1)}, bf16[1792,512]{1,0:T(8,128)(2,1)S(1)}, f32[8,512]{1,0:T(8,128)S(1)}) custom-call(s32[16]{0:T(128)} %refs_1_.3, s32[8,10]{1,0:T(8,128)} %refs_2_.3, bf16[2,1280,512]{2,1,0:T(8,128)(2,1)} %refs_3_.3, ...), custom_call_target="tpu_custom_call" | custom-call | tf_op jit(solution)/shard_map/pallas_call | solution.py:398
  3.5 13.0 %all_to_all.15.refs_0_ = bf16[4,32,512]{2,1,0:T(8,128)(2,1)S(1)} all-to-all(bf16[4,32,512]{2,1,0:T(8,128)(2,1)S(1)} %get-tuple-element.17), channel_id=1, replica_groups={{4,6,0,2},{5,7,1,3},{12,14,8,10},{13,15,9,11},{20,22,16,18},{21,23,17,1..., dimensions={0} | all-to-all | bytes 262144 | tf_op jit(solution)/shard_map/all_to_all | solution.py:418
  16.6 0.3 shard_map.56
  16.9 17.1 %all_to_all.16 = bf16[8,4,32,512]{3,2,1,0:T(8,128)(2,1)S(1)} all-to-all(bf16[8,4,32,512]{3,2,1,0:T(8,128)(2,1)S(1)} %get-tuple-element.18), channel_id=1, replica_groups={{16,17,24,25,0,1,8,9},{18,19,26,27,2,3,10,11},{20,21,28,29,4,5,12,13},{..., dimensions={0} | all-to-all | bytes 2097152 | tf_op jit(solution)/shard_map/all_to_all | solution.py:426
  33.9 1.4 %shard_map.57 = (f32[8,8,1152]{2,1,0:T(8,128)S(1)}, s16[8,8,1152]{2,1,0:T(8,128)(2,1)S(1)}) custom-call(bf16[32,32,512]{2,1,0:T(8,128)(2,1)S(1)} %bitcast.1, f32[2,6,256,256]{3,2,1,0:T(8,128)S(1)} %get-tuple-element.19.refs_0_, f32[2,256,256]{2,1,0:T(8,128)S(1)} %get-tuple-element.20.refs_1_, bf16[1792,512]{1,0:T(8,128)(2,1)S(1)} %get-tuple-element.21.refs_2_, ...), custom_call_target="tpu_custom_call" | custom-call | tf_op jit(solution)/shard_map/pallas_call | solution.py:432
  35.4 5.3 %collective-permute-start = (s16[8,8,1152]{2,1,0:T(8,128)(2,1)S(1)}, s16[8,8,1152]{2,1,0:T(8,128)(2,1)S(1)}, u32[]{:S(2)}, u32[]{:S(2)}) collective-permute-start(s16[8,8,1152]{2,1,0:T(8,128)(2,1)S(1)} %get-tuple-element.28), channel_id=1, source_target_pairs={{0,32},{32,0},{64,96},{96,64},{128,160},{160,128},{192,224},{224,1... | collective-permute-start | bytes 442376 | tf_op jit(solution)/shard_map/ppermute | solution.py:440
  40.7 1.0 %collective-permute-done.other_ref = s16[8,8,1152]{2,1,0:T(8,128)(2,1)S(1)} collective-permute-done((s16[8,8,1152]{2,1,0:T(8,128)(2,1)S(1)}, s16[8,8,1152]{2,1,0:T(8,128)(2,1)S(1)}, u32[]{:S(2)}, u32[]{:S(2)}) %collective-permute-start) | collective-permute-done | bytes 147488 | tf_op jit(solution)/shard_map/ppermute | solution.py:440
  41.7 0.5 shard_map.58
  42.2 11.1 %all_to_all.17.parts_ref = s16[8,8,1152]{2,1,0:T(8,128)(2,1)S(1)} all-to-all(s16[8,8,1152]{2,1,0:T(8,128)(2,1)S(1)} %shard_map.58), channel_id=1, replica_groups={{384,448,0,64,128,192,256,320},{416,480,32,96,160,224,288,352},{385,449..., dimensions={0} | all-to-all | bytes 294912 | tf_op jit(solution)/shard_map/all_to_all | solution.py:449
  53.4 0.9 %shard_map.59 = bf16[8,4,256]{2,1,0:T(4,128)(2,1)} custom-call(s16[8,8,1152]{2,1,0:T(8,128)(2,1)S(1)} %all_to_all.17.parts_ref), custom_call_target="tpu_custom_call" | custom-call | tf_op jit(solution)/shard_map/pallas_call | solution.py:450
Async XLA Ops:
  35.4 6.3 %collective-permute-start = (s16[8,8,1152]{2,1,0:T(8,128)(2,1)S(1)}, s16[8,8,1152]{2,1,0:T(8,128)(2,1)S(1)}, u32[]{:S(2)}, u32[]{:S(2)}) collective-permute-start(s16[8,8,1152]{2,1,0:T(8,128)(2,1)S(1)} %get-tuple-element.28), channel_id=1, source_target_pairs={{0,32},{32,0},{64,96},{96,64},{128,160},{160,128},{192,224},{224,1... | collective-permute-start | bytes 442376 | tf_op jit(solution)/shard_map/ppermute | solution.py:440

commit v14 on v13

--- a/solution.py
+++ b/solution.py
@@ -15,7 +15,8 @@
 LANES = 128
 Z = 8
 STRIDE = 2
-FIRST_Z, FIRST_X, FIRST_CHIP = 2, 2, 6
+FIRST_Z, FIRST_X, FIRST_MEMBER = 2, 2, 1
+CHIPS = [4, 3, 2, 1, 0, 7, 6, 5]
 WAITING_Z = 4
 INVALID_KEY = 256.0
 TOP = 32767.0
@@ -249,7 +250,7 @@
                 odd = x[(2 * pair + 1) * rows : (2 * pair + 2) * rows]
                 kept.append(jnp.where(core == 0, even, odd))
                 sent.append(jnp.where(core == 0, odd, even))
-            slot = (k * (GROUP // 2) + pair - FIRST_CHIP) % (HEADS // 2)
+            slot = CHIPS.index(k * (GROUP // 2) + pair)
             lane = lax.broadcasted_iota(jnp.int32, (rows, LANES), 1)
             data, fixed = to_wire(*sent)
             put(own_ref, slot, steps, kept[0], jnp.where(lane % STATS == 0, kept[1], kept[2]))
@@ -346,18 +347,21 @@
 
 def owner_of(block, owners):
     along_z, along_x = gather_orders(owners)
-    owner = block // (Z // STRIDE) % STRIDE
+    owner = 0
     for i, z in enumerate(along_z):
         owner = owner + jnp.where(block % (Z // STRIDE) == i, z, 0)
-    for i, x in enumerate(along_x):
-        owner = owner + jnp.where(block // Z == i, x, 0)
+    members = turned([x + k for x in along_x for k in range(STRIDE)], FIRST_MEMBER)
+    for i, m in enumerate(members):
+        owner = owner + jnp.where(block // (Z // STRIDE) == i, m, 0)
     return owner
 
 
 def gather_groups(owners):
     along_z, along_x = gather_orders(owners)
     first = [[x + z + k for k in along_z] for x in range(0, owners, Z) for z in range(STRIDE)]
-    second = [[x + z + k for x in along_x for k in range(STRIDE)] for z in range(0, Z, STRIDE)]
+    members = [x + k for x in along_x for k in range(STRIDE)]
+    members = turned(members, FIRST_MEMBER)
+    second = [[m + z for m in members] for z in range(0, Z, STRIDE)]
     return first, second
 
 
@@ -445,7 +449,7 @@
         out_specs=VMEM,
         compiler_params=params(8),
     )(kept, got)
-    chips = [turned(range(c, seqs, 2), FIRST_CHIP) for c in range(2)]
+    chips = [[2 * y + c for y in CHIPS] for c in range(2)]
     parts = lax.all_to_all(parts, "seq", 0, 0, tiled=True, axis_index_groups=chips)
     return pl.pallas_call(
         merge_kernel,

time: 55.1 us -> 54.9 us (level)
  starting transfers between devices: 5.32 us -> 6.06 us
    all_to_all x1, blocking collectives: 17.1 us -> 16 us  [shards(): lax.all_to_all(part_copies, 'leaf', 0, 0, tiled=True, axis_index_groups=s...]
    ppermute x1, starting transfers between devices: 5.32 us -> 6.06 us  [shards(): got = lax.ppermute(sent, 'seq', [(i, i ^ 1) for i in range(seqs)])]
    all_to_all x1, blocking collectives: 11.1 us -> 11.7 us  [shards(): lax.all_to_all(parts, 'seq', 0, 0, tiled=True, axis_index_groups=chips)]
where the time goes in v14:
time: 54.9 us; the launch traced here: 54.6 us
  blocking collectives  40.8 us (74%)
  Pallas kernels  6.66 us (12%)
  starting transfers between devices  6.06 us (11%)
  waiting for transfers between devices  0.99 us (2%)
    all_to_all x1, blocking collectives, shards(): lax.all_to_all(part_copies, 'leaf', 0, 0, tiled=True, axis_index_groups=s...  16 us
    all_to_all x1, blocking collectives, shards(): lax.all_to_all(own, 'leaf', 0, 0, tiled=True, axis_index_groups=first)  13 us
    all_to_all x1, blocking collectives, shards(): lax.all_to_all(parts, 'seq', 0, 0, tiled=True, axis_index_groups=chips)  11.7 us
    ppermute x1, starting transfers between devices, shards(): got = lax.ppermute(sent, 'seq', [(i, i ^ 1) for i in range(seqs)])  6.06 us
    pallas_call x2, Pallas kernels, stage_kernel(): pl.pallas_call(kernel, out_shape=(out_shape, *early_shapes), in_specs=[VM...  3.8 us
    pallas_call x1, Pallas kernels, shards(): pl.pallas_call(late_kernel, out_shape=(jax.ShapeDtypeStruct(wire.shape, j...  1.43 us
  transfers between devices with their start and end apart: 1, of which 1 were waited for; matrix products, arithmetic and copies ran while one was open for 0% of the time, Pallas kernels for 0%

profile of v14, /device:TPU:1, one launch (start us, length us, event | category | flops | bytes accessed | tf_op | source)
XLA Modules:
  0.0 54.6 jit_solution(4665714269226276876)
XLA Ops:
  0.0 3.5 %shard_map.55 = (bf16[4,32,512]{2,1,0:T(8,128)(2,1)S(1)}, f32[2,6,256,256]{3,2,1,0:T(8,128)S(1)}, f32[2,256,256]{2,1,0:T(8,128)S(1)}, bf16[1792,512]{1,0:T(8,128)(2,1)S(1)}, f32[8,512]{1,0:T(8,128)S(1)}) custom-call(s32[16]{0:T(128)} %refs_1_.3, s32[8,10]{1,0:T(8,128)} %refs_2_.3, bf16[2,1280,512]{2,1,0:T(8,128)(2,1)} %refs_3_.3, ...), custom_call_target="tpu_custom_call" | custom-call | tf_op jit(solution)/shard_map/pallas_call | solution.py:402
  3.5 13.0 %all_to_all.15.refs_0_ = bf16[4,32,512]{2,1,0:T(8,128)(2,1)S(1)} all-to-all(bf16[4,32,512]{2,1,0:T(8,128)(2,1)S(1)} %get-tuple-element.17), channel_id=1, replica_groups={{4,6,0,2},{5,7,1,3},{12,14,8,10},{13,15,9,11},{20,22,16,18},{21,23,17,1..., dimensions={0} | all-to-all | bytes 262144 | tf_op jit(solution)/shard_map/all_to_all | solution.py:422
  16.6 0.3 shard_map.56
  16.9 16.0 %all_to_all.16 = bf16[8,4,32,512]{3,2,1,0:T(8,128)(2,1)S(1)} all-to-all(bf16[8,4,32,512]{3,2,1,0:T(8,128)(2,1)S(1)} %get-tuple-element.18), channel_id=1, replica_groups={{17,24,25,0,1,8,9,16},{19,26,27,2,3,10,11,18},{21,28,29,4,5,12,13,20},{..., dimensions={0} | all-to-all | bytes 2097152 | tf_op jit(solution)/shard_map/all_to_all | solution.py:430
  32.9 1.4 %shard_map.57 = (f32[8,8,1152]{2,1,0:T(8,128)S(1)}, s16[8,8,1152]{2,1,0:T(8,128)(2,1)S(1)}) custom-call(bf16[32,32,512]{2,1,0:T(8,128)(2,1)S(1)} %bitcast.1, f32[2,6,256,256]{3,2,1,0:T(8,128)S(1)} %get-tuple-element.19.refs_0_, f32[2,256,256]{2,1,0:T(8,128)S(1)} %get-tuple-element.20.refs_1_, bf16[1792,512]{1,0:T(8,128)(2,1)S(1)} %get-tuple-element.21.refs_2_, ...), custom_call_target="tpu_custom_call" | custom-call | tf_op jit(solution)/shard_map/pallas_call | solution.py:436
  34.3 6.1 %collective-permute-start = (s16[8,8,1152]{2,1,0:T(8,128)(2,1)S(1)}, s16[8,8,1152]{2,1,0:T(8,128)(2,1)S(1)}, u32[]{:S(2)}, u32[]{:S(2)}) collective-permute-start(s16[8,8,1152]{2,1,0:T(8,128)(2,1)S(1)} %get-tuple-element.28), channel_id=1, source_target_pairs={{0,32},{32,0},{64,96},{96,64},{128,160},{160,128},{192,224},{224,1... | collective-permute-start | bytes 442376 | tf_op jit(solution)/shard_map/ppermute | solution.py:444
  40.4 1.0 %collective-permute-done.other_ref = s16[8,8,1152]{2,1,0:T(8,128)(2,1)S(1)} collective-permute-done((s16[8,8,1152]{2,1,0:T(8,128)(2,1)S(1)}, s16[8,8,1152]{2,1,0:T(8,128)(2,1)S(1)}, u32[]{:S(2)}, u32[]{:S(2)}) %collective-permute-start) | collective-permute-done | bytes 147488 | tf_op jit(solution)/shard_map/ppermute | solution.py:444
  41.4 0.5 shard_map.58
  41.9 11.7 %all_to_all.17.parts_ref = s16[8,8,1152]{2,1,0:T(8,128)(2,1)S(1)} all-to-all(s16[8,8,1152]{2,1,0:T(8,128)(2,1)S(1)} %shard_map.58), channel_id=1, replica_groups={{256,192,128,64,0,448,384,320},{288,224,160,96,32,480,416,352},{257,193..., dimensions={0} | all-to-all | bytes 294912 | tf_op jit(solution)/shard_map/all_to_all | solution.py:453
  53.6 0.9 %shard_map.59 = bf16[8,4,256]{2,1,0:T(4,128)(2,1)} custom-call(s16[8,8,1152]{2,1,0:T(8,128)(2,1)S(1)} %all_to_all.17.parts_ref), custom_call_target="tpu_custom_call" | custom-call | tf_op jit(solution)/shard_map/pallas_call | solution.py:454
Async XLA Ops:
  34.3 7.1 %collective-permute-start = (s16[8,8,1152]{2,1,0:T(8,128)(2,1)S(1)}, s16[8,8,1152]{2,1,0:T(8,128)(2,1)S(1)}, u32[]{:S(2)}, u32[]{:S(2)}) collective-permute-start(s16[8,8,1152]{2,1,0:T(8,128)(2,1)S(1)} %get-tuple-element.28), channel_id=1, source_target_pairs={{0,32},{32,0},{64,96},{96,64},{128,160},{160,128},{192,224},{224,1... | collective-permute-start | bytes 442376 | tf_op jit(solution)/shard_map/ppermute | solution.py:444

commit v15 on v14

--- a/solution.py
+++ b/solution.py
@@ -220,15 +220,16 @@
     early_cols = chunks * CHUNK
     count = count_ref[...]
     reps = GROUP * rows // count.shape[0]
-    pick = jnp.where(lax.broadcasted_iota(jnp.int32, (8, HEAD_DIM), 1) == 0, 1.0, 0.0).astype(jnp.bfloat16)
+    pick = jnp.where(lax.broadcasted_iota(jnp.int32, (16, HEAD_DIM), 1) == 0, 1.0, 0.0).astype(jnp.bfloat16)
 
     for k in range(KV_HEADS):
         cols = slice(k * HEAD_DIM, (k + 1) * HEAD_DIM)
         keys = shared_ref[:, 0:tokens, cols].reshape(shared_cols, HEAD_DIM)
         values = shared_ref[:, tokens : 2 * tokens, cols].reshape(shared_cols, HEAD_DIM)
-        marks = dot_nt(pick, keys)[0:1]
+        query = half_ref[early_cols:, cols]
+        both = dot_nt(jnp.concatenate([query, pick], axis=0), keys)
+        s, marks = both[: query.shape[0]], both[query.shape[0] : query.shape[0] + 1]
         mult = tall(jnp.where(marks < INVALID_KEY / 2, count, 0.0), reps)
-        s = dot_nt(half_ref[early_cols:, cols], keys)
         s = jnp.where(mult > 0.0, s, -jnp.inf)
         early_max = row_ref[k, :, :LANES]
         block_max = jnp.maximum(jnp.max(fold(s, jnp.maximum), axis=1, keepdims=True), early_max)

time: 54.9 us -> 54.8 us (level)
  no operation moved by 1% of the time
where the time goes in v15:
time: 54.8 us; the launch traced here: 54.5 us
  blocking collectives  40.8 us (74%)
  Pallas kernels  6.59 us (12%)
  starting transfers between devices  6.07 us (11%)
  waiting for transfers between devices  0.99 us (2%)
    all_to_all x1, blocking collectives, shards(): lax.all_to_all(part_copies, 'leaf', 0, 0, tiled=True, axis_index_groups=s...  16 us
    all_to_all x1, blocking collectives, shards(): lax.all_to_all(own, 'leaf', 0, 0, tiled=True, axis_index_groups=first)  13 us
    all_to_all x1, blocking collectives, shards(): lax.all_to_all(parts, 'seq', 0, 0, tiled=True, axis_index_groups=chips)  11.7 us
    ppermute x1, starting transfers between devices, shards(): got = lax.ppermute(sent, 'seq', [(i, i ^ 1) for i in range(seqs)])  6.07 us
    pallas_call x2, Pallas kernels, stage_kernel(): pl.pallas_call(kernel, out_shape=(out_shape, *early_shapes), in_specs=[VM...  3.8 us
    pallas_call x1, Pallas kernels, shards(): pl.pallas_call(late_kernel, out_shape=(jax.ShapeDtypeStruct(wire.shape, j...  1.36 us
  transfers between devices with their start and end apart: 1, of which 1 were waited for; matrix products, arithmetic and copies ran while one was open for 0% of the time, Pallas kernels for 0%

profile of v15, /device:TPU:1, one launch (start us, length us, event | category | flops | bytes accessed | tf_op | source)
XLA Modules:
  0.0 54.5 jit_solution(2115177801544942375)
XLA Ops:
  0.0 3.5 %shard_map.55 = (bf16[4,32,512]{2,1,0:T(8,128)(2,1)S(1)}, f32[2,6,256,256]{3,2,1,0:T(8,128)S(1)}, f32[2,256,256]{2,1,0:T(8,128)S(1)}, bf16[1792,512]{1,0:T(8,128)(2,1)S(1)}, f32[8,512]{1,0:T(8,128)S(1)}) custom-call(s32[16]{0:T(128)} %refs_1_.3, s32[8,10]{1,0:T(8,128)} %refs_2_.3, bf16[2,1280,512]{2,1,0:T(8,128)(2,1)} %refs_3_.3, ...), custom_call_target="tpu_custom_call" | custom-call | tf_op jit(solution)/shard_map/pallas_call | solution.py:403
  3.5 13.0 %all_to_all.15.refs_0_ = bf16[4,32,512]{2,1,0:T(8,128)(2,1)S(1)} all-to-all(bf16[4,32,512]{2,1,0:T(8,128)(2,1)S(1)} %get-tuple-element.17), channel_id=1, replica_groups={{4,6,0,2},{5,7,1,3},{12,14,8,10},{13,15,9,11},{20,22,16,18},{21,23,17,1..., dimensions={0} | all-to-all | bytes 262144 | tf_op jit(solution)/shard_map/all_to_all | solution.py:423
  16.6 0.3 shard_map.56
  16.9 16.0 %all_to_all.16 = bf16[8,4,32,512]{3,2,1,0:T(8,128)(2,1)S(1)} all-to-all(bf16[8,4,32,512]{3,2,1,0:T(8,128)(2,1)S(1)} %get-tuple-element.18), channel_id=1, replica_groups={{17,24,25,0,1,8,9,16},{19,26,27,2,3,10,11,18},{21,28,29,4,5,12,13,20},{..., dimensions={0} | all-to-all | bytes 2097152 | tf_op jit(solution)/shard_map/all_to_all | solution.py:431
  32.9 1.4 %shard_map.57 = (f32[8,8,1152]{2,1,0:T(8,128)S(1)}, s16[8,8,1152]{2,1,0:T(8,128)(2,1)S(1)}) custom-call(bf16[32,32,512]{2,1,0:T(8,128)(2,1)S(1)} %bitcast.1, f32[2,6,256,256]{3,2,1,0:T(8,128)S(1)} %get-tuple-element.19.refs_0_, f32[2,256,256]{2,1,0:T(8,128)S(1)} %get-tuple-element.20.refs_1_, bf16[1792,512]{1,0:T(8,128)(2,1)S(1)} %get-tuple-element.21.refs_2_, ...), custom_call_target="tpu_custom_call" | custom-call | tf_op jit(solution)/shard_map/pallas_call | solution.py:437
  34.3 6.1 %collective-permute-start = (s16[8,8,1152]{2,1,0:T(8,128)(2,1)S(1)}, s16[8,8,1152]{2,1,0:T(8,128)(2,1)S(1)}, u32[]{:S(2)}, u32[]{:S(2)}) collective-permute-start(s16[8,8,1152]{2,1,0:T(8,128)(2,1)S(1)} %get-tuple-element.28), channel_id=1, source_target_pairs={{0,32},{32,0},{64,96},{96,64},{128,160},{160,128},{192,224},{224,1... | collective-permute-start | bytes 442376 | tf_op jit(solution)/shard_map/ppermute | solution.py:445
  40.3 1.0 %collective-permute-done.other_ref = s16[8,8,1152]{2,1,0:T(8,128)(2,1)S(1)} collective-permute-done((s16[8,8,1152]{2,1,0:T(8,128)(2,1)S(1)}, s16[8,8,1152]{2,1,0:T(8,128)(2,1)S(1)}, u32[]{:S(2)}, u32[]{:S(2)}) %collective-permute-start) | collective-permute-done | bytes 147488 | tf_op jit(solution)/shard_map/ppermute | solution.py:445
  41.3 0.5 shard_map.58
  41.8 11.7 %all_to_all.17.parts_ref = s16[8,8,1152]{2,1,0:T(8,128)(2,1)S(1)} all-to-all(s16[8,8,1152]{2,1,0:T(8,128)(2,1)S(1)} %shard_map.58), channel_id=1, replica_groups={{256,192,128,64,0,448,384,320},{288,224,160,96,32,480,416,352},{257,193..., dimensions={0} | all-to-all | bytes 294912 | tf_op jit(solution)/shard_map/all_to_all | solution.py:454
  53.6 0.9 %shard_map.59 = bf16[8,4,256]{2,1,0:T(4,128)(2,1)} custom-call(s16[8,8,1152]{2,1,0:T(8,128)(2,1)S(1)} %all_to_all.17.parts_ref), custom_call_target="tpu_custom_call" | custom-call | tf_op jit(solution)/shard_map/pallas_call | solution.py:455
Async XLA Ops:
  34.3 7.1 %collective-permute-start = (s16[8,8,1152]{2,1,0:T(8,128)(2,1)S(1)}, s16[8,8,1152]{2,1,0:T(8,128)(2,1)S(1)}, u32[]{:S(2)}, u32[]{:S(2)}) collective-permute-start(s16[8,8,1152]{2,1,0:T(8,128)(2,1)S(1)} %get-tuple-element.28), channel_id=1, source_target_pairs={{0,32},{32,0},{64,96},{96,64},{128,160},{160,128},{192,224},{224,1... | collective-permute-start | bytes 442376 | tf_op jit(solution)/shard_map/ppermute | solution.py:445
